TPU v7x, 128 devices: a whole 4x4x4 slice. The times are simulated.
128 devices in a mesh: lat: 32 (over y, z, core), dep: 4 (over x).
Axes of the slice: x: 4, y: 4, z: 4, core: 2. Of those that a mesh axis runs over, the one named last changes fastest.
Arguments:
- stored_energy_density: float32 [128, 32, 4096], P('dep', None, 'lat'), may hold values from 0.2 to 3
- zones: int32 [32, 4096], P(None, 'lat'), may hold values from 0 to 15
- fluence: float32 [16], replicated, may hold values from 5 to 40
- seed_adjoint: float32 [128, 32, 4096], P('dep', None, 'lat'), may hold values from -6 to 6
Outputs:
- adjoint_start: float32 [128, 32, 4096], P('dep', None, 'lat')
- fluence_grad: float32 [16], replicated
All inputs are finite; a program needn't handle non-finite values.
Results may differ from a plain program's by a relative error of at most 0.00021.
Values sent between devices are 32-bit elements; how exact they have to be, the bound alone decides.
No kernel may reach another device: no remote copies, remote signals or barrier semaphores. Data moves between devices by JAX's collectives and lax.ppermute only.
A program may use at most 128 MiB of HBM per device.

v0:
```python
import jax
import jax.numpy as jnp
from jax import lax
from jax.sharding import PartitionSpec as P

STEPS = 4
NZONE = 16


melt_level = 1.0
latent_heat = 1.0
smooth_width = 0.1
resting_diffusivity_level = 0.6
peak_diffusivity_level = 0.8
absorb_solid = 0.004
absorb_liquid = 0.03
wafer_drain_rate = 0.5
time_step = 0.1


def with_halo(block, sides, width):
    for axis, dim in sides:
        count = lax.axis_size(axis)
        forward = [(i, i + 1) for i in range(count - 1)]
        backward = [(target, source) for source, target in forward]
        low = lax.ppermute(
            lax.slice_in_dim(block, block.shape[dim] - width, None, axis=dim), axis, forward
        )
        high = lax.ppermute(lax.slice_in_dim(block, 0, width, axis=dim), axis, backward)
        block = jnp.concatenate([low, block, high], axis=dim)
    return block


def entering(part, axis, combine, identity, reverse):
    count = lax.axis_size(axis)
    place = lax.axis_index(axis)
    ahead = count - 1 - place if reverse else place
    gathered = lax.all_gather(part, axis)
    state = jnp.zeros_like(part) + jnp.asarray(identity, part.dtype)

    def one(step, state):
        source = count - 1 - step if reverse else step
        return combine(state, lax.dynamic_index_in_dim(gathered, source, 0, False))

    return lax.fori_loop(0, ahead, one, state)


def silicon_constants(stored_energy_density):
    lower = (stored_energy_density - melt_level) / smooth_width
    upper = (stored_energy_density - melt_level - latent_heat) / smooth_width
    phase_change_ramp = smooth_width * (jax.nn.softplus(lower) - jax.nn.softplus(upper))
    rise = jax.nn.sigmoid(lower) - jax.nn.sigmoid(upper)
    kelvin_distribution = stored_energy_density - phase_change_ramp
    energy_to_kelvin_map = 1.0 / (1.0 + kelvin_distribution * kelvin_distribution)
    diffusive_transport_coefficient = (
        resting_diffusivity_level + peak_diffusivity_level * energy_to_kelvin_map
    )
    optical_capture_share = (
        absorb_solid + (absorb_liquid - absorb_solid) * phase_change_ramp / latent_heat
    )
    transition_steepness = 1.0 - rise
    conduction_steepness = (
        -2.0
        * peak_diffusivity_level
        * kelvin_distribution
        * energy_to_kelvin_map
        * energy_to_kelvin_map
    )
    absorption_gradient_factor = (absorb_liquid - absorb_solid) * rise / latent_heat
    return (
        kelvin_distribution,
        diffusive_transport_coefficient,
        optical_capture_share,
        transition_steepness,
        conduction_steepness,
        absorption_gradient_factor,
    )


def inner(field):
    return field[1:-1, 1:-1, 1:-1]


def add_pair(earlier, later):
    return earlier + later


def shorter(field, first, axis_orientation):
    return lax.slice_in_dim(
        field, first, first + field.shape[axis_orientation] - 1, axis=axis_orientation
    )


def line_of(field, axis_orientation):
    picks = [slice(1, -1), slice(1, -1), slice(1, -1)]
    picks[axis_orientation] = slice(None)
    return field[tuple(picks)]


def face_masks(depth, rows, width):
    dep_pos = lax.axis_index("dep")
    dep_count = lax.axis_size("dep")
    lat_pos = lax.axis_index("lat")
    lat_count = lax.axis_size("lat")
    zface = jnp.arange(depth + 1)
    yface = jnp.arange(rows + 1)
    layer = jnp.arange(depth)
    zmask = ((zface > 0) | (dep_pos > 0)) & ((zface < depth) | (dep_pos < dep_count - 1))
    ymask = (yface > 0) & (yface < rows)
    bottom_voxel_layer = (layer == depth - 1) & (dep_pos == dep_count - 1)
    xface = jnp.arange(width + 1)
    xmask = ((xface > 0) | (lat_pos > 0)) & ((xface < width) | (lat_pos < lat_count - 1))
    masks = (
        zmask.astype(jnp.float32)[:, None, None],
        ymask.astype(jnp.float32)[None, :, None],
        xmask.astype(jnp.float32)[None, None, :],
    )
    return (masks, bottom_voxel_layer.astype(jnp.float32)[:, None, None])


def state_halo(field):
    padded = with_halo(field, (("lat", 2), ("dep", 0)), 1)
    return jnp.pad(padded, ((0, 0), (1, 1), (0, 0)))


def paired_halo(stacked):
    padded = with_halo(stacked, (("lat", 3), ("dep", 1)), 1)
    return jnp.pad(padded, ((0, 0), (0, 0), (1, 1), (0, 0)))


def shade_top(optical_capture_share):
    column = jnp.sum(optical_capture_share, axis=0)
    return entering(column, "dep", add_pair, jnp.zeros_like(column), False)


def shade_below(deposit):
    column = jnp.sum(deposit, axis=0)
    return entering(column, "dep", add_pair, jnp.zeros_like(column), True)


def heat_flow(ptemp, pcond, masks):
    deposited_power_density = 0.0
    for axis_orientation in range(3):
        line_t = line_of(ptemp, axis_orientation)
        line_k = line_of(pcond, axis_orientation)
        flux = (
            masks[axis_orientation]
            * 0.5
            * (shorter(line_k, 0, axis_orientation) + shorter(line_k, 1, axis_orientation))
            * (shorter(line_t, 1, axis_orientation) - shorter(line_t, 0, axis_orientation))
        )
        deposited_power_density = deposited_power_density + (
            shorter(flux, 1, axis_orientation) - shorter(flux, 0, axis_orientation)
        )
    return deposited_power_density


def heat_pullback(padj, ptemp, pcond, masks):
    grad_t = 0.0
    grad_k = 0.0
    for axis_orientation in range(3):
        line_a = line_of(padj, axis_orientation)
        line_t = line_of(ptemp, axis_orientation)
        line_k = line_of(pcond, axis_orientation)
        jump = shorter(line_a, 0, axis_orientation) - shorter(line_a, 1, axis_orientation)
        push = (
            masks[axis_orientation]
            * jump
            * 0.5
            * (shorter(line_k, 0, axis_orientation) + shorter(line_k, 1, axis_orientation))
        )
        share = (
            masks[axis_orientation]
            * 0.5
            * jump
            * (shorter(line_t, 1, axis_orientation) - shorter(line_t, 0, axis_orientation))
        )
        grad_t = grad_t + (shorter(push, 0, axis_orientation) - shorter(push, 1, axis_orientation))
        grad_k = grad_k + (
            shorter(share, 0, axis_orientation) + shorter(share, 1, axis_orientation)
        )
    return (grad_t, grad_k)


def advance_local(stored_energy_density, padded, shade, intensity, masks, bottom_voxel_layer):
    ptemp, pcond, pabs, _, _, _ = silicon_constants(padded)
    deposited_power_density = heat_flow(ptemp, pcond, masks)
    deposited_power_density = (
        deposited_power_density - wafer_drain_rate * bottom_voxel_layer * inner(ptemp)
    )
    optical_capture_share = inner(pabs)
    light = jnp.exp(
        -(shade[None] + jnp.cumsum(optical_capture_share, axis=0) - optical_capture_share)
    )
    source = intensity[None] * light * (1.0 - jnp.exp(-optical_capture_share))
    return stored_energy_density + time_step * (deposited_power_density + source)


def retreat(adjoint, padj, padded, shade, intensity, zone_table, masks, bottom_voxel_layer):
    ptemp, pcond, pabs, pslope, pcslope, paslope = silicon_constants(padded)
    grad_t, grad_k = heat_pullback(padj, ptemp, pcond, masks)
    scaled = inner(padj)
    grad_t = grad_t - wafer_drain_rate * bottom_voxel_layer * scaled
    optical_capture_share = inner(pabs)
    light = jnp.exp(
        -(shade[None] + jnp.cumsum(optical_capture_share, axis=0) - optical_capture_share)
    )
    passed = jnp.exp(-optical_capture_share)
    unit = light * (1.0 - passed)
    weighted = scaled * intensity[None]
    deposit = weighted * unit
    below = shade_below(deposit)
    suffix = jnp.sum(deposit, axis=0)[None] - jnp.cumsum(deposit, axis=0) + below[None]
    grad_a = weighted * light * passed - suffix
    transition_steepness = inner(pslope)
    updated = (
        adjoint
        + grad_t * transition_steepness
        + grad_k * inner(pcslope) * transition_steepness
        + grad_a * inner(paslope)
    )
    zone_part = jnp.sum(zone_table * jnp.sum(scaled * unit, axis=0)[None], axis=(1, 2))
    return (updated, zone_part)


def per_device(stored_energy_density, zones, fluence, seed_adjoint):
    depth, rows, width = stored_energy_density.shape
    masks, bottom_voxel_layer = face_masks(depth, rows, width)
    zone_table = (zones[None] == jnp.arange(NZONE)[:, None, None]).astype(jnp.float32)
    intensity = jnp.sum(zone_table * fluence[:, None, None], axis=0)
    states = []
    current = stored_energy_density
    for step in range(STEPS):
        states.append(current)
        if step + 1 < STEPS:
            padded = state_halo(current)
            shade = shade_top(inner(silicon_constants(padded)[2]))
            current = advance_local(current, padded, shade, intensity, masks, bottom_voxel_layer)
    adjoint = seed_adjoint
    total = jnp.zeros((NZONE,), jnp.float32)
    for step in reversed(range(STEPS)):
        scaled = time_step * adjoint
        both = paired_halo(jnp.stack([scaled, states[step]]))
        padj = both[0]
        padded = both[1]
        shade = shade_top(silicon_constants(states[step])[2])
        adjoint, zone_part = retreat(
            adjoint, padj, padded, shade, intensity, zone_table, masks, bottom_voxel_layer
        )
        total = total + lax.psum(zone_part, ("lat", "dep"))
    return (adjoint, total)


def solution(mesh):
    in_specs = (P("dep", None, "lat"), P(None, "lat"), P(), P("dep", None, "lat"))
    out_specs = (P("dep", None, "lat"), P())
    return jax.shard_map(
        per_device, mesh=mesh, in_specs=in_specs, out_specs=out_specs, check_vma=False
    )
```

profile of v0, /device:TPU:0, one launch (start us, length us, event | category | flops | bytes accessed | tf_op | source)
XLA Modules:
  0.0 450.3 jit_solution(6899726968335430981)
XLA Ops:
  5.0 4.5 collective-permute-done.1
  9.6 3.4 collective-permute-start.2
  14.6 4.2 collective-permute-done.3
  18.8 3.6 multiply_add_fusion.6
  23.7 11.9 %all-gather = f32[128,128]{1,0:T(8,128)S(1)} all-gather(f32[32,128]{1,0:T(8,128)S(1)} %fusion.175), channel_id=2, replica_groups=mesh['lat'=32,'dep'=4] {'dep'}, dimensions={0}, use_global_device_ids=true | all-gather | bytes 81920 | tf_op jit(solution)/shard_map/all_gather | solution.py:38
  40.7 4.8 %collective-permute-start.4 = (f32[32,32,1]{2,1,0:T(8,128)S(1)}, f32[32,32,1]{2,1,0:T(8,128)S(1)}, u32[]{:S(2)}, u32[]{:S(2)}) collective-permute-start(f32[32,32,1]{2,1,0:T(8,128)S(1)} %get-tuple-element.592), channel_id=1, source_target_pairs={{0,4},{4,8},{8,12},{12,16},{16,20},{20,24},{24,28},{28,32},{32,36}... | collective-permute-start | bytes 12296 | tf_op jit(solution)/shard_map/ppermute | solution.py:26
  47.7 5.3 %collective-permute-done.5 = f32[32,32,1]{2,1,0:T(8,128)S(1)} collective-permute-done((f32[32,32,1]{2,1,0:T(8,128)S(1)}, f32[32,32,1]{2,1,0:T(8,128)S(1)}, u32[]{:S(2)}, u32[]{:S(2)}) %collective-permute-start.5) | collective-permute-done | bytes 4128 | tf_op jit(solution)/shard_map/ppermute | solution.py:29
  56.8 4.2 collective-permute-done.7
  67.8 11.9 %all-gather.1 = f32[128,128]{1,0:T(8,128)S(1)} all-gather(f32[32,128]{1,0:T(8,128)S(1)} %fusion.177), channel_id=3, replica_groups=mesh['lat'=32,'dep'=4] {'dep'}, dimensions={0}, use_global_device_ids=true | all-gather | bytes 81920 | tf_op jit(solution)/shard_map/all_gather | solution.py:38
  79.7 4.0 fusion.109
  84.0 4.8 %collective-permute-start.8 = (f32[32,32,1]{2,1,0:T(8,128)S(1)}, f32[32,32,1]{2,1,0:T(8,128)S(1)}, u32[]{:S(2)}, u32[]{:S(2)}) collective-permute-start(f32[32,32,1]{2,1,0:T(8,128)S(1)} %get-tuple-element.590), channel_id=1, source_target_pairs={{0,4},{4,8},{8,12},{12,16},{16,20},{20,24},{24,28},{28,32},{32,36}... | collective-permute-start | bytes 12296 | tf_op jit(solution)/shard_map/ppermute | solution.py:26
  90.6 5.6 %collective-permute-done.9 = f32[32,32,1]{2,1,0:T(8,128)S(1)} collective-permute-done((f32[32,32,1]{2,1,0:T(8,128)S(1)}, f32[32,32,1]{2,1,0:T(8,128)S(1)}, u32[]{:S(2)}, u32[]{:S(2)}) %collective-permute-start.9) | collective-permute-done | bytes 4128 | tf_op jit(solution)/shard_map/ppermute | solution.py:29
  100.4 3.7 collective-permute-done.11
  104.0 3.5 multiply_add_fusion.4
  112.6 11.9 %all-gather.2 = f32[128,128]{1,0:T(8,128)S(1)} all-gather(f32[32,128]{1,0:T(8,128)S(1)} %fusion.179), channel_id=4, replica_groups=mesh['lat'=32,'dep'=4] {'dep'}, dimensions={0}, use_global_device_ids=true | all-gather | bytes 81920 | tf_op jit(solution)/shard_map/all_gather | solution.py:38
  124.6 4.4 fusion.105
  131.6 5.4 %collective-permute-start.12 = (f32[2,32,32,1]{2,1,3,0:T(8,128)S(1)}, f32[2,32,32,1]{2,1,3,0:T(8,128)S(1)}, u32[]{:S(2)}, u32[]{:S(2)}) collective-permute-start(f32[2,32,32,1]{2,1,3,0:T(8,128)S(1)} %copy.22), channel_id=1, source_target_pairs={{0,4},{4,8},{8,12},{12,16},{16,20},{20,24},{24,28},{28,32},{32,36}... | collective-permute-start | bytes 24584 | tf_op jit(solution)/shard_map/ppermute | solution.py:26
  137.0 11.9 %all-gather.3 = f32[128,128]{1,0:T(8,128)S(1)} all-gather(f32[32,128]{1,0:T(8,128)S(1)} %get-tuple-element.514), channel_id=5, replica_groups=mesh['lat'=32,'dep'=4] {'dep'}, dimensions={0}, use_global_device_ids=true | all-gather | bytes 81920 | tf_op jit(solution)/shard_map/all_gather | solution.py:38
  155.7 4.3 collective-permute-done.15
  160.0 3.0 select_maximum_fusion.15
  163.1 4.0 divide_subtract_fusion.3
  169.5 11.9 %all-gather.4 = f32[128,128]{1,0:T(8,128)S(1)} all-gather(f32[32,128]{1,0:T(8,128)S(1)} %get-tuple-element.401), channel_id=6, replica_groups=mesh['lat'=32,'dep'=4] {'dep'}, dimensions={0}, use_global_device_ids=true | all-gather | bytes 81920 | tf_op jit(solution)/shard_map/all_gather | solution.py:38
  187.5 3.2 multiply_bitcast_fusion.2
  193.8 3.0 collective-permute-start.16
  196.9 11.9 %all-gather.5 = f32[128,128]{1,0:T(8,128)S(1)} all-gather(f32[32,128]{1,0:T(8,128)S(1)} %get-tuple-element.508), channel_id=7, replica_groups=mesh['lat'=32,'dep'=4] {'dep'}, dimensions={0}, use_global_device_ids=true | all-gather | bytes 81920 | tf_op jit(solution)/shard_map/all_gather | solution.py:38
  215.6 3.8 collective-permute-done.19
  219.4 3.0 select_maximum_fusion.10
  222.6 3.6 divide_subtract_fusion.2
  230.5 2.6 fusion.14
  235.8 11.9 %all-gather.6 = f32[128,128]{1,0:T(8,128)S(1)} all-gather(f32[32,128]{1,0:T(8,128)S(1)} %get-tuple-element.399), channel_id=8, replica_groups=mesh['lat'=32,'dep'=4] {'dep'}, dimensions={0}, use_global_device_ids=true | all-gather | bytes 81920 | tf_op jit(solution)/shard_map/all_gather | solution.py:38
  247.8 2.8 fusion.53
  250.8 4.1 multiply_bitcast_fusion.1
  258.0 3.0 collective-permute-start.20
  261.1 11.9 %all-gather.7 = f32[128,128]{1,0:T(8,128)S(1)} all-gather(f32[32,128]{1,0:T(8,128)S(1)} %get-tuple-element.502), channel_id=9, replica_groups=mesh['lat'=32,'dep'=4] {'dep'}, dimensions={0}, use_global_device_ids=true | all-gather | bytes 81920 | tf_op jit(solution)/shard_map/all_gather | solution.py:38
  279.1 4.0 collective-permute-done.23
  285.3 3.6 divide_subtract_fusion.1
  293.2 2.6 fusion.12
  297.7 11.9 %all-gather.8 = f32[128,128]{1,0:T(8,128)S(1)} all-gather(f32[32,128]{1,0:T(8,128)S(1)} %get-tuple-element.403), channel_id=10, replica_groups=mesh['lat'=32,'dep'=4] {'dep'}, dimensions={0}, use_global_device_ids=true | all-gather | bytes 81920 | tf_op jit(solution)/shard_map/all_gather | solution.py:38
  312.4 4.2 multiply_bitcast_fusion
  319.7 3.0 collective-permute-start.24
  322.7 11.9 %all-gather.9 = f32[128,128]{1,0:T(8,128)S(1)} all-gather(f32[32,128]{1,0:T(8,128)S(1)} %get-tuple-element.589), channel_id=11, replica_groups=mesh['lat'=32,'dep'=4] {'dep'}, dimensions={0}, use_global_device_ids=true | all-gather | bytes 81920 | tf_op jit(solution)/shard_map/all_gather | solution.py:38
  340.2 3.9 collective-permute-done.27
  346.2 3.6 divide_subtract_fusion
  352.1 2.6 fusion.10
  359.1 72.0 %psum.34 = f32[16]{0:T(128)} all-reduce(f32[16]{0:T(128)S(1)} %add_add_fusion), channel_id=1, replica_groups=mesh['lat'=32,'dep'=4] {'lat','dep'}, use_global_device_ids=true, to_apply=%region_47.48 | all-reduce | flops 16 | bytes 128 | tf_op jit(solution)/shard_map/psum | solution.py:250
  431.1 11.9 %all-gather.10 = f32[128,128]{1,0:T(8,128)S(1)} all-gather(f32[32,128]{1,0:T(8,128)S(1)} %get-tuple-element.405), channel_id=12, replica_groups=mesh['lat'=32,'dep'=4] {'dep'}, dimensions={0}, use_global_device_ids=true | all-gather | bytes 81920 | tf_op jit(solution)/shard_map/all_gather | solution.py:38
  443.1 2.5 fusion.51
  445.8 4.1 fusion.101
  (303 shorter events, 109.6 us)
Async XLA Ops:
  0.6 8.8 %copy-start.3 = (f32[32,32,128]{2,1,0:T(8,128)S(1)}, f32[32,32,128]{2,1,0:T(8,128)}, u32[]{:S(2)}) copy-start(f32[32,32,128]{2,1,0:T(8,128)} %param.26) | copy-start | bytes 1572868
  2.1 2.8 collective-permute-start
  3.5 6.0 %collective-permute-start.1 = (f32[32,32,1]{2,1,0:T(8,128)S(1)}, f32[32,32,1]{2,1,0:T(8,128)S(1)}, u32[]{:S(2)}, u32[]{:S(2)}) collective-permute-start(f32[32,32,1]{2,1,0:T(8,128)S(1)} %get-tuple-element.595), channel_id=1, source_target_pairs={{4,0},{8,4},{12,8},{16,12},{20,16},{24,20},{28,24},{32,28},{36,32}... | collective-permute-start | bytes 12296 | tf_op jit(solution)/shard_map/ppermute | solution.py:29
  4.8 179.1 %copy-start.56 = (f32[33]{0:T(128)}, f32[33]{0:T(128)S(1)}, u32[]{:S(2)}) copy-start(f32[33]{0:T(128)S(1)} %broadcast_select_fusion.1) | copy-start | bytes 400
  4.8 180.2 %copy-start.44 = (f32[129]{0:T(256)}, f32[129]{0:T(256)S(1)}, u32[]{:S(2)}) copy-start(f32[129]{0:T(256)S(1)} %broadcast_select_fusion) | copy-start | bytes 1552
  4.9 74.8 %copy-start.60 = (f32[32]{0:T(128)}, f32[32]{0:T(128)S(1)}, u32[]{:S(2)}) copy-start(f32[32]{0:T(128)S(1)} %and_select_fusion) | copy-start | bytes 388
  5.0 9.6 %copy-start.37 = (f32[32,32,1]{2,1,0:T(8,128)}, f32[32,32,1]{2,1,0:T(8,128)S(1)}, u32[]{:S(2)}) copy-start(f32[32,32,1]{2,1,0:T(8,128)S(1)} %collective-permute-done) | copy-start | bytes 12292
  9.5 5.1 %copy-start.38 = (f32[32,32,1]{2,1,0:T(8,128)}, f32[32,32,1]{2,1,0:T(8,128)S(1)}, u32[]{:S(2)}) copy-start(f32[32,32,1]{2,1,0:T(8,128)S(1)} %collective-permute-done.1) | copy-start | bytes 12292
  9.6 5.0 %collective-permute-start.2 = (f32[1,32,130]{2,1,0:T(8,128)S(1)}, f32[1,32,130]{2,1,0:T(8,128)S(1)}, u32[]{:S(2)}, u32[]{:S(2)}) collective-permute-start(f32[1,32,130]{2,1,0:T(8,128)S(1)} %get-tuple-element.555), channel_id=1, source_target_pairs={{0,1},{1,2},{2,3},{4,5},{5,6},{6,7},{8,9},{9,10},{10,11},{12,13},{... | collective-permute-start | bytes 49928 | tf_op jit(solution)/shard_map/ppermute | solution.py:26
  13.0 5.8 %collective-permute-start.3 = (f32[1,32,130]{2,1,0:T(8,128)S(1)}, f32[1,32,130]{2,1,0:T(8,128)S(1)}, u32[]{:S(2)}, u32[]{:S(2)}) collective-permute-start(f32[1,32,130]{2,1,0:T(8,128)S(1)} %get-tuple-element.556), channel_id=1, source_target_pairs={{1,0},{2,1},{3,2},{5,4},{6,5},{7,6},{9,8},{10,9},{11,10},{13,12},{... | collective-permute-start | bytes 49928 | tf_op jit(solution)/shard_map/ppermute | solution.py:29
  14.3 167.4 %copy-start.52 = (f32[33]{0:T(128)}, f32[33]{0:T(128)S(1)}, u32[]{:S(2)}) copy-start(f32[33]{0:T(128)S(1)} %broadcast_select_fusion.2) | copy-start | bytes 400
  40.5 6.3 %copy-start.40 = (f32[32,32,128]{2,1,0:T(8,128)S(1)}, f32[32,32,128]{2,1,0:T(8,128)}, u32[]{:S(2)}) copy-start(f32[32,32,128]{2,1,0:T(8,128)} %param.29) | copy-start | bytes 1572868
  40.7 7.0 %collective-permute-start.4 = (f32[32,32,1]{2,1,0:T(8,128)S(1)}, f32[32,32,1]{2,1,0:T(8,128)S(1)}, u32[]{:S(2)}, u32[]{:S(2)}) collective-permute-start(f32[32,32,1]{2,1,0:T(8,128)S(1)} %get-tuple-element.592), channel_id=1, source_target_pairs={{0,4},{4,8},{8,12},{12,16},{16,20},{20,24},{24,28},{28,32},{32,36}... | collective-permute-start | bytes 12296 | tf_op jit(solution)/shard_map/ppermute | solution.py:26
  45.5 7.4 %collective-permute-start.5 = (f32[32,32,1]{2,1,0:T(8,128)S(1)}, f32[32,32,1]{2,1,0:T(8,128)S(1)}, u32[]{:S(2)}, u32[]{:S(2)}) collective-permute-start(f32[32,32,1]{2,1,0:T(8,128)S(1)} %get-tuple-element.593), channel_id=1, source_target_pairs={{4,0},{8,4},{12,8},{16,12},{20,16},{24,20},{28,24},{32,28},{36,32}... | collective-permute-start | bytes 12296 | tf_op jit(solution)/shard_map/ppermute | solution.py:29
  53.0 3.7 collective-permute-start.6
  55.2 5.8 %collective-permute-start.7 = (f32[1,32,130]{2,1,0:T(8,128)S(1)}, f32[1,32,130]{2,1,0:T(8,128)S(1)}, u32[]{:S(2)}, u32[]{:S(2)}) collective-permute-start(f32[1,32,130]{2,1,0:T(8,128)S(1)} %get-tuple-element.554), channel_id=1, source_target_pairs={{1,0},{2,1},{3,2},{5,4},{6,5},{7,6},{9,8},{10,9},{11,10},{13,12},{... | collective-permute-start | bytes 49928 | tf_op jit(solution)/shard_map/ppermute | solution.py:29
  56.7 128.3 %copy-start.48 = (f32[129]{0:T(256)}, f32[129]{0:T(256)S(1)}, u32[]{:S(2)}) copy-start(f32[129]{0:T(256)S(1)} %fusion.209) | copy-start | bytes 1552
  83.7 40.8 %copy-start = (f32[32,32,128]{2,1,0:T(8,128)}, f32[32,32,128]{2,1,0:T(8,128)S(1)}, u32[]{:S(2)}) copy-start(f32[32,32,128]{2,1,0:T(8,128)S(1)} %get-tuple-element.509) | copy-start | bytes 1572868
  84.0 6.6 %collective-permute-start.8 = (f32[32,32,1]{2,1,0:T(8,128)S(1)}, f32[32,32,1]{2,1,0:T(8,128)S(1)}, u32[]{:S(2)}, u32[]{:S(2)}) collective-permute-start(f32[32,32,1]{2,1,0:T(8,128)S(1)} %get-tuple-element.590), channel_id=1, source_target_pairs={{0,4},{4,8},{8,12},{12,16},{16,20},{20,24},{24,28},{28,32},{32,36}... | collective-permute-start | bytes 12296 | tf_op jit(solution)/shard_map/ppermute | solution.py:26
  88.8 7.4 %collective-permute-start.9 = (f32[32,32,1]{2,1,0:T(8,128)S(1)}, f32[32,32,1]{2,1,0:T(8,128)S(1)}, u32[]{:S(2)}, u32[]{:S(2)}) collective-permute-start(f32[32,32,1]{2,1,0:T(8,128)S(1)} %get-tuple-element.591), channel_id=1, source_target_pairs={{4,0},{8,4},{12,8},{16,12},{20,16},{24,20},{28,24},{32,28},{36,32}... | collective-permute-start | bytes 12296 | tf_op jit(solution)/shard_map/ppermute | solution.py:29
  96.3 4.0 collective-permute-start.10
  98.2 5.8 %collective-permute-start.11 = (f32[1,32,130]{2,1,0:T(8,128)S(1)}, f32[1,32,130]{2,1,0:T(8,128)S(1)}, u32[]{:S(2)}, u32[]{:S(2)}) collective-permute-start(f32[1,32,130]{2,1,0:T(8,128)S(1)} %get-tuple-element.552), channel_id=1, source_target_pairs={{1,0},{2,1},{3,2},{5,4},{6,5},{7,6},{9,8},{10,9},{11,10},{13,12},{... | collective-permute-start | bytes 49928 | tf_op jit(solution)/shard_map/ppermute | solution.py:29
  107.5 4.9 %copy-start.20 = (f32[34,34,130]{2,1,0:T(8,128)}, f32[34,34,130]{2,1,0:T(8,128)S(1)}, u32[]{:S(2)}) copy-start(f32[34,34,130]{2,1,0:T(8,128)S(1)} %get-tuple-element.520) | copy-start | bytes 1803364
  110.6 14.0 %copy-start.61 = (f32[32]{0:T(128)S(1)}, f32[32]{0:T(128)}, u32[]{:S(2)}) copy-start(f32[32]{0:T(128)} %copy-done.60) | copy-start | bytes 388
  124.6 4.4 copy-start.11
  130.3 19.1 %collective-permute-start.13 = (f32[2,32,32,1]{2,1,3,0:T(8,128)S(1)}, f32[2,32,32,1]{2,1,3,0:T(8,128)S(1)}, u32[]{:S(2)}, u32[]{:S(2)}) collective-permute-start(f32[2,32,32,1]{2,1,3,0:T(8,128)S(1)} %copy.23), channel_id=1, source_target_pairs={{4,0},{8,4},{12,8},{16,12},{20,16},{24,20},{28,24},{32,28},{36,32}... | collective-permute-start | bytes 24584 | tf_op jit(solution)/shard_map/ppermute | solution.py:29
  131.6 17.3 %collective-permute-start.12 = (f32[2,32,32,1]{2,1,3,0:T(8,128)S(1)}, f32[2,32,32,1]{2,1,3,0:T(8,128)S(1)}, u32[]{:S(2)}, u32[]{:S(2)}) collective-permute-start(f32[2,32,32,1]{2,1,3,0:T(8,128)S(1)} %copy.22), channel_id=1, source_target_pairs={{0,4},{4,8},{8,12},{12,16},{16,20},{20,24},{24,28},{28,32},{32,36}... | collective-permute-start | bytes 24584 | tf_op jit(solution)/shard_map/ppermute | solution.py:26
  151.2 4.4 collective-permute-start.14
  153.4 6.5 %collective-permute-start.15 = (f32[2,1,32,130]{3,2,1,0:T(8,128)S(1)}, f32[2,1,32,130]{3,2,1,0:T(8,128)S(1)}, u32[]{:S(2)}, u32[]{:S(2)}) collective-permute-start(f32[2,1,32,130]{3,2,1,0:T(8,128)S(1)} %get-tuple-element.534), channel_id=1, source_target_pairs={{1,0},{2,1},{3,2},{5,4},{6,5},{7,6},{9,8},{10,9},{11,10},{13,12},{... | collective-permute-start | bytes 99848 | tf_op jit(solution)/shard_map/ppermute | solution.py:29
  192.4 17.3 %copy-start.2 = (f32[32,32,128]{2,1,0:T(8,128)S(1)}, f32[32,32,128]{2,1,0:T(8,128)}, u32[]{:S(2)}) copy-start(f32[32,32,128]{2,1,0:T(8,128)} %copy-done) | copy-start | bytes 1572868
  192.4 16.8 %collective-permute-start.17 = (f32[2,32,32,1]{2,1,3,0:T(8,128)S(1)}, f32[2,32,32,1]{2,1,3,0:T(8,128)S(1)}, u32[]{:S(2)}, u32[]{:S(2)}) collective-permute-start(f32[2,32,32,1]{2,1,3,0:T(8,128)S(1)} %copy.27), channel_id=1, source_target_pairs={{4,0},{8,4},{12,8},{16,12},{20,16},{24,20},{28,24},{32,28},{36,32}... | collective-permute-start | bytes 24584 | tf_op jit(solution)/shard_map/ppermute | solution.py:29
  193.8 14.9 %collective-permute-start.16 = (f32[2,32,32,1]{2,1,3,0:T(8,128)S(1)}, f32[2,32,32,1]{2,1,3,0:T(8,128)S(1)}, u32[]{:S(2)}, u32[]{:S(2)}) collective-permute-start(f32[2,32,32,1]{2,1,3,0:T(8,128)S(1)} %copy.26), channel_id=1, source_target_pairs={{0,4},{4,8},{8,12},{12,16},{16,20},{20,24},{24,28},{28,32},{32,36}... | collective-permute-start | bytes 24584 | tf_op jit(solution)/shard_map/ppermute | solution.py:26
  211.1 4.5 collective-permute-start.18
  212.9 6.5 %collective-permute-start.19 = (f32[2,1,32,130]{3,2,1,0:T(8,128)S(1)}, f32[2,1,32,130]{3,2,1,0:T(8,128)S(1)}, u32[]{:S(2)}, u32[]{:S(2)}) collective-permute-start(f32[2,1,32,130]{3,2,1,0:T(8,128)S(1)} %get-tuple-element.532), channel_id=1, source_target_pairs={{1,0},{2,1},{3,2},{5,4},{6,5},{7,6},{9,8},{10,9},{11,10},{13,12},{... | collective-permute-start | bytes 99848 | tf_op jit(solution)/shard_map/ppermute | solution.py:29
  226.1 8.3 %copy-start.9 = (f32[34,34,130]{2,1,0:T(8,128)}, f32[34,34,130]{2,1,0:T(8,128)S(1)}, u32[]{:S(2)}) copy-start(f32[34,34,130]{2,1,0:T(8,128)S(1)} %get-tuple-element.544) | copy-start | bytes 1803364
  256.6 17.3 %copy-start.16 = (f32[1,32,32,128]{3,2,1,0:T(8,128)S(1)}, f32[1,32,32,128]{3,2,1,0:T(8,128)}, u32[]{:S(2)}) copy-start(f32[1,32,32,128]{3,2,1,0:T(8,128)} %copy-done.15) | copy-start | bytes 1572868
  256.6 16.8 %collective-permute-start.21 = (f32[2,32,32,1]{2,1,3,0:T(8,128)S(1)}, f32[2,32,32,1]{2,1,3,0:T(8,128)S(1)}, u32[]{:S(2)}, u32[]{:S(2)}) collective-permute-start(f32[2,32,32,1]{2,1,3,0:T(8,128)S(1)} %copy.31), channel_id=1, source_target_pairs={{4,0},{8,4},{12,8},{16,12},{20,16},{24,20},{28,24},{32,28},{36,32}... | collective-permute-start | bytes 24584 | tf_op jit(solution)/shard_map/ppermute | solution.py:29
  258.0 14.9 %collective-permute-start.20 = (f32[2,32,32,1]{2,1,3,0:T(8,128)S(1)}, f32[2,32,32,1]{2,1,3,0:T(8,128)S(1)}, u32[]{:S(2)}, u32[]{:S(2)}) collective-permute-start(f32[2,32,32,1]{2,1,3,0:T(8,128)S(1)} %copy.30), channel_id=1, source_target_pairs={{0,4},{4,8},{8,12},{12,16},{16,20},{20,24},{24,28},{28,32},{32,36}... | collective-permute-start | bytes 24584 | tf_op jit(solution)/shard_map/ppermute | solution.py:26
  274.6 4.5 %collective-permute-start.22 = (f32[2,1,32,130]{3,2,1,0:T(8,128)}, f32[2,1,32,130]{3,2,1,0:T(8,128)S(1)}, u32[]{:S(2)}, u32[]{:S(2)}) collective-permute-start(f32[2,1,32,130]{3,2,1,0:T(8,128)} %get-tuple-element.529), channel_id=1, source_target_pairs={{0,1},{1,2},{2,3},{4,5},{5,6},{6,7},{8,9},{9,10},{10,11},{12,13},{... | collective-permute-start | bytes 99848 | tf_op jit(solution)/shard_map/ppermute | solution.py:26
  276.9 6.2 %collective-permute-start.23 = (f32[2,1,32,130]{3,2,1,0:T(8,128)S(1)}, f32[2,1,32,130]{3,2,1,0:T(8,128)S(1)}, u32[]{:S(2)}, u32[]{:S(2)}) collective-permute-start(f32[2,1,32,130]{3,2,1,0:T(8,128)S(1)} %get-tuple-element.530), channel_id=1, source_target_pairs={{1,0},{2,1},{3,2},{5,4},{6,5},{7,6},{9,8},{10,9},{11,10},{13,12},{... | collective-permute-start | bytes 99848 | tf_op jit(solution)/shard_map/ppermute | solution.py:29
  288.8 8.3 %copy-start.10 = (f32[34,34,130]{2,1,0:T(8,128)}, f32[34,34,130]{2,1,0:T(8,128)S(1)}, u32[]{:S(2)}) copy-start(f32[34,34,130]{2,1,0:T(8,128)S(1)} %get-tuple-element.540) | copy-start | bytes 1803364
  312.4 4.2 copy-start.4
  318.3 17.3 %copy-start.13 = (f32[1,32,32,128]{3,2,1,0:T(8,128)S(1)}, f32[1,32,32,128]{3,2,1,0:T(8,128)}, u32[]{:S(2)}) copy-start(f32[1,32,32,128]{3,2,1,0:T(8,128)} %copy-done.12) | copy-start | bytes 1572868
  318.3 16.8 %collective-permute-start.25 = (f32[2,32,32,1]{2,1,3,0:T(8,128)S(1)}, f32[2,32,32,1]{2,1,3,0:T(8,128)S(1)}, u32[]{:S(2)}, u32[]{:S(2)}) collective-permute-start(f32[2,32,32,1]{2,1,3,0:T(8,128)S(1)} %copy.35), channel_id=1, source_target_pairs={{4,0},{8,4},{12,8},{16,12},{20,16},{24,20},{28,24},{32,28},{36,32}... | collective-permute-start | bytes 24584 | tf_op jit(solution)/shard_map/ppermute | solution.py:29
  319.7 14.9 %collective-permute-start.24 = (f32[2,32,32,1]{2,1,3,0:T(8,128)S(1)}, f32[2,32,32,1]{2,1,3,0:T(8,128)S(1)}, u32[]{:S(2)}, u32[]{:S(2)}) collective-permute-start(f32[2,32,32,1]{2,1,3,0:T(8,128)S(1)} %copy.34), channel_id=1, source_target_pairs={{0,4},{4,8},{8,12},{12,16},{16,20},{20,24},{24,28},{28,32},{32,36}... | collective-permute-start | bytes 24584 | tf_op jit(solution)/shard_map/ppermute | solution.py:26
  336.3 3.9 collective-permute-start.26
  337.9 6.2 %collective-permute-start.27 = (f32[2,1,32,130]{3,2,1,0:T(8,128)S(1)}, f32[2,1,32,130]{3,2,1,0:T(8,128)S(1)}, u32[]{:S(2)}, u32[]{:S(2)}) collective-permute-start(f32[2,1,32,130]{3,2,1,0:T(8,128)S(1)} %get-tuple-element.528), channel_id=1, source_target_pairs={{1,0},{2,1},{3,2},{5,4},{6,5},{7,6},{9,8},{10,9},{11,10},{13,12},{... | collective-permute-start | bytes 99848 | tf_op jit(solution)/shard_map/ppermute | solution.py:29
  349.8 6.2 %copy-start.6 = (f32[34,34,130]{2,1,0:T(8,128)}, f32[34,34,130]{2,1,0:T(8,128)S(1)}, u32[]{:S(2)}) copy-start(f32[34,34,130]{2,1,0:T(8,128)S(1)} %get-tuple-element.536) | copy-start | bytes 1803364
  (55 other events, 129.8 us)
where the time goes:
time: 458 us; the launch traced here: 450 us
  blocking collectives  203 us (44%)
  other arithmetic  121 us (26%)
  starting transfers between devices  59.7 us (13%)
  waiting for transfers between devices  46.8 us (10%)
  local copies, waits for them, and re-layouts  16.2 us (4%)
    all_gather x11, blocking collectives, entering(): gathered = lax.all_gather(part, axis)  131 us
    psum x1, blocking collectives, per_device(): total = total + lax.psum(zone_part, ('lat', 'dep'))  72 us
    ppermute x14, waiting for transfers between devices, with_halo(): lax.ppermute(lax.slice_in_dim(block, 0, width, axis=dim), axis, backward)  43.5 us
    ppermute x14, starting transfers between devices, with_halo(): lax.ppermute(lax.slice_in_dim(block, block.shape[dim] - width, None, axis...  40.8 us
    mul x12, other arithmetic, heat_pullback(): masks[axis_orientation] * jump * 0.5  24.3 us
    ppermute x14, starting transfers between devices, with_halo(): lax.ppermute(lax.slice_in_dim(block, 0, width, axis=dim), axis, backward)  19 us
    sub x4, other arithmetic, silicon_constants(): rise = jax.nn.sigmoid(lower) - jax.nn.sigmoid(upper)  14.7 us
    another operation x8, other arithmetic, per_device(): both = paired_halo(jnp.stack([scaled, states[step]]))  13.8 us
  transfers between devices with their start and end apart: 28, of which 15 were waited for; matrix products, arithmetic and copies ran while one was open for 1% of the time, Pallas kernels for 0%

commit v1 on v0

v1 whole, which is shorter than its diff:
```python
import math

import jax
import jax.numpy as jnp
from jax import lax
from jax.experimental import pallas as pl
from jax.experimental.pallas import tpu as pltpu
from jax.sharding import PartitionSpec as P


NZONE = 16
CORE = 32
HALO = 8
WIDE = CORE + 2 * HALO
SEED_HALO = 4
SEED_WIDE = CORE + 2 * SEED_HALO
BASE = 8
HIGH = WIDE + 2 * BASE
DT = 0.1
ABSORB_SOLID = 0.004
ABSORB_RISE = 0.026
LOG2E = math.log2(math.e)
EM10 = math.exp(-10.0)
F32 = jnp.float32


def _params():
    return pltpu.CompilerParams(vmem_limit_bytes=16 * 1024 * 1024)


def _vmem(*shape):
    return pltpu.VMEM(shape, F32)


def _full():
    return pl.BlockSpec(memory_space=pltpu.VMEM)


def _smem():
    return pl.BlockSpec(memory_space=pltpu.SMEM)


def _lanes(rows):
    return lax.broadcasted_iota(jnp.int32, (rows, 128), 1)


def _packed(ref, g):
    rows = [ref[8 * sub + g] for sub in range(4)]
    return jnp.concatenate(rows, axis=0).T


def pack_state(d_ref, fluence_ref, h_ref, zones_ref, own, to1, to2, to3, edge, light, zid, light_own, buf, lbuf):
    d = d_ref[0]
    zero = jnp.zeros((HALO, 128), F32)
    for g in range(8):
        buf[g, 0:HALO] = zero
        buf[g, HALO + 128 :] = zero
        packed = _packed(h_ref, g)
        buf[g, HALO : HALO + 128] = packed
        edge[0, g] = packed[0:HALO]
        edge[1, g] = packed[128 - HALO :]
    for k, out in enumerate((own, to1, to2, to3)):
        start = pl.multiple_of(lax.rem(d + k, 4) * CORE, CORE)
        out[...] = buf[:, pl.ds(start, WIDE)]
    zones = zones_ref[...]
    intensity = jnp.zeros(zones.shape, F32)
    for k in range(NZONE):
        intensity = jnp.where(zones == k, fluence_ref[k] * DT, intensity)
    packed = jnp.concatenate([intensity] * 4, axis=0).T
    light[...] = packed
    lbuf[0:HALO] = zero
    lbuf[HALO : HALO + 128] = packed
    lbuf[HALO + 128 :] = zero
    start = pl.multiple_of(d * CORE, CORE)
    light_own[...] = lbuf[pl.ds(start, WIDE)]
    lbuf[0:128] = jnp.concatenate([zones.astype(F32)] * 4, axis=0).T
    zid[...] = lbuf[pl.ds(start, CORE)]


def pack_seed(d_ref, a_ref, edge, light, own, to1, to2, to3, e0, e1, e2, e3, buf, ebuf):
    d = d_ref[0]
    zero = jnp.zeros((SEED_HALO, 128), F32)
    for g in range(8):
        buf[g, 0:SEED_HALO] = zero
        buf[g, SEED_HALO + 128 :] = zero
        packed = _packed(a_ref, g)
        buf[g, SEED_HALO : SEED_HALO + 128] = packed
        ebuf[0, g, 0:8] = edge[0, g]
        ebuf[1, g, 0:8] = edge[1, g]
        ebuf[0, g, 8:12] = packed[0:4]
        ebuf[1, g, 8:12] = packed[124:128]
        part = 4 * (g % 2)
        ebuf[0, g, 12:16] = light[part : part + 4]
        ebuf[1, g, 12:16] = light[120 + part : 124 + part]
    for k, out in enumerate((own, to1, to2, to3)):
        start = pl.multiple_of(lax.rem(d + k, 4) * CORE, CORE)
        out[...] = buf[:, pl.ds(start, SEED_WIDE)]
    for j, out in enumerate((e0, e1, e2, e3)):
        last = (d == (-j) % 4).astype(jnp.int32)
        out[...] = ebuf[last]


def _rows_of(start, count):
    return pl.ds(BASE + start, count)


def _prefix(total, lane):
    below1 = jnp.where(lane >= 32, pltpu.roll(total, 32, 1), 0.0)
    below2 = jnp.where(lane >= 64, pltpu.roll(total, 64, 1), 0.0)
    below3 = jnp.where(lane >= 96, pltpu.roll(total, 96, 1), 0.0)
    return below1 + below2 + below3


def _suffix(total, lane):
    above1 = jnp.where(lane < 96, pltpu.roll(total, 96, 1), 0.0)
    above2 = jnp.where(lane < 64, pltpu.roll(total, 64, 1), 0.0)
    above3 = jnp.where(lane < 32, pltpu.roll(total, 32, 1), 0.0)
    return above1 + above2 + above3


def _all_subs(total):
    pair = total + pltpu.roll(total, 32, 1)
    return pair + pltpu.roll(pair, 64, 1)


def _properties(n, h_ref, t_ref, k_ref, c_ref, r_ref, l_ref, first, count):
    span = _rows_of(first, count)
    lane = _lanes(count)

    def slab(s, carry):
        run = jnp.zeros((count, 128), F32)
        for g in range(8):
            i = s * 8 + g
            h = h_ref[i, span]
            e = jnp.exp2(h * (10.0 * LOG2E) - 10.0 * LOG2E)
            u = 1.0 + e
            v = 1.0 + EM10 * e
            inv = pl.reciprocal(u * v)
            ramp = 0.1 * jnp.log(u * (u * inv))
            t = h - ramp
            m = pl.reciprocal(1.0 + t * t)
            t_ref[n, i, span] = t
            k_ref[n, i, span] = 0.03 + 0.04 * m
            c_ref[n, i, span] = (-0.08 * t) * (m * m)
            r_ref[n, i, span] = e * ((1.0 - EM10) * inv)
            l_ref[n, s * 9 + g, span] = run
            run = run + (ABSORB_SOLID + ABSORB_RISE * ramp)
        above = carry + _prefix(run, lane)
        for g in range(8):
            at = s * 9 + g
            l_ref[n, at, span] = jnp.exp(-(above + l_ref[n, at, span]))
        l_ref[n, s * 9 + 8, span] = jnp.exp(-(above + run))
        return carry + _all_subs(run)

    lax.fori_loop(0, 4, slab, jnp.zeros((count, 128), F32))


def _ghost(ref_rows, lat, d):
    @pl.when(jnp.logical_and(lat == 0, d == 0))
    def _():
        for i in range(32):
            ref_rows(i, HALO - 1)[...] = ref_rows(i, HALO)[...]

    @pl.when(jnp.logical_and(lat == 31, d == 3))
    def _():
        for i in range(32):
            ref_rows(i, HALO + CORE)[...] = ref_rows(i, HALO + CORE - 1)[...]


def _later(load, s, lane):
    here, after = load(s * 8), load(jnp.minimum(s + 1, 3) * 8)
    return pltpu.roll(jnp.where(lane < 32, after, here), 96, 1)


def _earlier(load, s, lane):
    here, before = load(s * 8 + 7), load(jnp.maximum(s - 1, 0) * 8 + 7)
    return pltpu.roll(jnp.where(lane >= 96, before, here), 32, 1)


def _advance(n, h_ref, new_ref, t_ref, k_ref, l_ref, light, first, count):
    span = _rows_of(first, count)
    up, down = _rows_of(first + 1, count), _rows_of(first - 1, count)
    lane = _lanes(count)
    inside = jnp.where(lax.rem(lane, 32) == 31, 0.0, 1.0)

    def slab(s, carry):
        bottom = jnp.logical_and(lane >= 96, s == 3)
        top = jnp.logical_and(lane < 32, s == 0)
        load_t = lambda i: t_ref[n, i, span]
        load_k = lambda i: k_ref[n, i, span]
        t0, k0 = load_t(s * 8), load_k(s * 8)
        t_before, k_before = _earlier(load_t, s, lane), _earlier(load_k, s, lane)
        flux_before = jnp.where(top, 0.0, (k0 + k_before) * (t0 - t_before))
        for g in range(8):
            i = s * 8 + g
            if g < 7:
                t1, k1 = load_t(i + 1), load_k(i + 1)
                flux = (k0 + k1) * (t1 - t0)
            else:
                t1, k1 = _later(load_t, s, lane), _later(load_k, s, lane)
                flux = jnp.where(bottom, -0.05 * t0, (k0 + k1) * (t1 - t0))
            change = flux - flux_before
            across = (k0 + pltpu.roll(k0, 127, 1)) * (pltpu.roll(t0, 127, 1) - t0) * inside
            change = change + (across - pltpu.roll(across, 1, 1))
            t_up, t_down = t_ref[n, i, up], t_ref[n, i, down]
            k_up, k_down = k_ref[n, i, up], k_ref[n, i, down]
            change = change + ((k0 + k_up) * (t_up - t0) - (k0 + k_down) * (t0 - t_down))
            source = light[span] * (l_ref[n, s * 9 + g, span] - l_ref[n, s * 9 + g + 1, span])
            new_ref[i, span] = h_ref[i, span] + (change + source)
            t0, k0, flux_before = t1, k1, flux
        return carry

    lax.fori_loop(0, 4, slab, 0)


def forward(where, own, r1, r2, r3, e0, e1, e2, e3, light_own, t_ref, k_ref, c_ref, r_ref, l_ref, light, ha, hb):
    lat, d = where[0], where[1]
    for k, block in enumerate((own, r1, r2, r3)):
        source = lax.rem(d + 4 - k, 4) * 8
        ha[pl.ds(source, 8), _rows_of(0, WIDE)] = block[...]
    light[0:BASE] = jnp.zeros((BASE, 128), F32)
    light[BASE + WIDE :] = jnp.zeros((BASE, 128), F32)
    light[_rows_of(0, WIDE)] = light_own[...]

    @pl.when(d == 0)
    def _():
        for j, e in enumerate((e0, e1, e2, e3)):
            ha[pl.ds(((-j) % 4) * 8, 8), _rows_of(0, 8)] = e[:, 0:8]
        light[_rows_of(0, 4)] = e0[0, 12:16]
        light[_rows_of(4, 4)] = e0[1, 12:16]

    @pl.when(d == 3)
    def _():
        for j, e in enumerate((e0, e1, e2, e3)):
            ha[pl.ds(((3 - j) % 4) * 8, 8), _rows_of(HALO + CORE, 8)] = e[:, 0:8]
        light[_rows_of(HALO + CORE, 4)] = e0[0, 12:16]
        light[_rows_of(HALO + CORE + 4, 4)] = e0[1, 12:16]

    source, target = ha, hb
    for n in range(4):
        first, count = (0, WIDE) if n < 3 else (SEED_HALO, SEED_WIDE)
        _properties(n, source, t_ref, k_ref, c_ref, r_ref, l_ref, first, count)
        if n < 3:
            _ghost(lambda i, c, n=n: t_ref.at[n, i, pl.ds(BASE + c, 1)], lat, d)
            first, count = (0, WIDE) if n < 2 else (SEED_HALO, SEED_WIDE)
            _advance(n, source, target, t_ref, k_ref, l_ref, light, first, count)
            source, target = target, source


def _retreat(n, a_ref, new_ref, t_ref, k_ref, c_ref, r_ref, l_ref, light, run_ref, first, count):
    span = _rows_of(first, count)
    up, down = _rows_of(first + 1, count), _rows_of(first - 1, count)
    lane = _lanes(count)
    inside = jnp.where(lax.rem(lane, 32) == 31, 0.0, 1.0)
    rows = pl.ds(0, count)
    gain = ABSORB_RISE * light[span]

    def slab(step, state):
        s = 3 - step
        carry, seen = state
        run = jnp.zeros((count, 128), F32)
        for g in reversed(range(8)):
            run_ref[g, rows] = run
            lost = l_ref[n, s * 9 + g, span] - l_ref[n, s * 9 + g + 1, span]
            run = run + a_ref[s * 8 + g, span] * lost
        below = carry + _suffix(run, lane)
        bottom = jnp.logical_and(lane >= 96, s == 3)
        top = jnp.logical_and(lane < 32, s == 0)
        load_a = lambda i: a_ref[i, span]
        load_t = lambda i: t_ref[n, i, span]
        load_k = lambda i: k_ref[n, i, span]
        a0, t0, k0 = load_a(s * 8), load_t(s * 8), load_k(s * 8)
        jump = jnp.where(top, 0.0, _earlier(load_a, s, lane) - a0)
        push_before = jump * (_earlier(load_k, s, lane) + k0)
        share_before = jump * (t0 - _earlier(load_t, s, lane))
        for g in range(8):
            i = s * 8 + g
            if g < 7:
                a1, t1, k1 = load_a(i + 1), load_t(i + 1), load_k(i + 1)
                jump = a0 - a1
                push = jump * (k0 + k1)
                share = jump * (t1 - t0)
            else:
                a1, t1, k1 = _later(load_a, s, lane), _later(load_t, s, lane), _later(load_k, s, lane)
                jump = a0 - a1
                push = jnp.where(bottom, 0.05 * a0, jump * (k0 + k1))
                share = jnp.where(bottom, 0.0, jump * (t1 - t0))
            grad_t = push_before - push
            grad_k = share_before + share
            jump = (a0 - pltpu.roll(a0, 127, 1)) * inside
            push_r = jump * (k0 + pltpu.roll(k0, 127, 1))
            share_r = jump * (pltpu.roll(t0, 127, 1) - t0)
            grad_t = grad_t + (pltpu.roll(push_r, 1, 1) - push_r)
            grad_k = grad_k + (pltpu.roll(share_r, 1, 1) + share_r)
            jump_up = a0 - a_ref[i, up]
            jump_down = a_ref[i, down] - a0
            grad_t = grad_t + (jump_down * (k_ref[n, i, down] + k0) - jump_up * (k0 + k_ref[n, i, up]))
            grad_k = grad_k + (jump_down * (t0 - t_ref[n, i, down]) + jump_up * (t_ref[n, i, up] - t0))
            heat = grad_t + c_ref[n, i, span] * grad_k
            absorbed = gain * (a0 * l_ref[n, s * 9 + g + 1, span] - (below + run_ref[g, rows]))
            new_ref[i, span] = a0 + (heat + r_ref[n, i, span] * (absorbed - heat))
            a0, t0, k0, push_before, share_before = a1, t1, k1, push, share
        return (carry + _all_subs(run), seen + run)

    zero = jnp.zeros((count, 128), F32)
    return lax.fori_loop(0, 4, slab, (zero, zero))[1]


def backward(where, own, r1, r2, r3, e0, e1, e2, e3, t_ref, k_ref, c_ref, r_ref, l_ref, light, zid, a_ref, zpart, ab, run_ref):
    lat, d = where[0], where[1]
    aa = a_ref
    for k, block in enumerate((own, r1, r2, r3)):
        source = lax.rem(d + 4 - k, 4) * 8
        ab[pl.ds(source, 8), _rows_of(SEED_HALO, SEED_WIDE)] = block[...]

    @pl.when(d == 0)
    def _():
        for j, e in enumerate((e0, e1, e2, e3)):
            ab[pl.ds(((-j) % 4) * 8, 8), _rows_of(SEED_HALO, 4)] = e[:, 8:12]

    @pl.when(d == 3)
    def _():
        for j, e in enumerate((e0, e1, e2, e3)):
            ab[pl.ds(((3 - j) % 4) * 8, 8), _rows_of(HALO + CORE, 4)] = e[:, 8:12]

    source, target = ab, aa
    total = jnp.zeros((CORE, 128), F32)
    for n in (3, 2, 1):
        _ghost(lambda i, c, ref=source: ref.at[i, pl.ds(BASE + c, 1)], lat, d)
        seen = _retreat(n, source, target, t_ref, k_ref, c_ref, r_ref, l_ref, light, run_ref, SEED_HALO, SEED_WIDE)
        total = total + seen[HALO - SEED_HALO : HALO - SEED_HALO + CORE]
        source, target = target, source
    _ghost(lambda i, c, ref=source: ref.at[i, pl.ds(BASE + c, 1)], lat, d)
    span = _rows_of(HALO, CORE)

    def slab(s, total):
        for g in range(8):
            at = s * 9 + g
            total = total + source[s * 8 + g, span] * (l_ref[0, at, span] - l_ref[0, at + 1, span])
        return total

    total = lax.fori_loop(0, 4, slab, total) * DT
    zones = zid[...]
    for k in range(NZONE):
        zpart[k : k + 1] = jnp.sum(jnp.where(zones == float(k), total, 0.0), axis=0, keepdims=True)


def last_step(where, a_ref, t_ref, k_ref, c_ref, r_ref, l_ref, light, own, to1, to2, to3, new_ref, run_ref):
    d = where[1]
    _retreat(0, a_ref, new_ref, t_ref, k_ref, c_ref, r_ref, l_ref, light, run_ref, HALO, CORE)
    for k, out in enumerate((own, to1, to2, to3)):
        out[...] = new_ref[pl.ds(lax.rem(d + k, 4) * 8, 8), _rows_of(HALO, CORE)]


def unpack(where, own, r1, r2, r3, out, buf):
    d = where[1]
    for k, block in enumerate((own, r1, r2, r3)):
        start = pl.multiple_of(lax.rem(d + 4 - k, 4) * CORE, CORE)
        buf[:, pl.ds(start, CORE)] = block[...]
    for g in range(8):
        plain = buf[g].T
        for sub in range(4):
            out[8 * sub + g] = plain[32 * sub : 32 * sub + 32]


def _around(x, k):
    return lax.ppermute(x, "dep", [(s, (s + k) % 4) for s in range(4)])


def _edges(x, j):
    pairs = [(l * 4 + (-j) % 4, (l + 1) * 4) for l in range(31)]
    pairs += [(l * 4 + (3 - j) % 4, (l - 1) * 4 + 3) for l in range(1, 32)]
    return lax.ppermute(x, ("lat", "dep"), pairs)


def _place(y, z, core, x):
    return ((y * 4 + z) * 2 + core) * 4 + x


def _meet(v, partner):
    pairs = []
    for y in range(4):
        for z in range(4):
            for core in range(2):
                for x in range(4):
                    pairs.append((_place(y, z, core, x), _place(*partner(y, z, core, x))))
    return v + lax.ppermute(v, ("lat", "dep"), pairs)


def total_of(v):
    for partner in (
        lambda y, z, core, x: (y, z, 1 - core, x),
        lambda y, z, core, x: (y, z ^ 1, core, x),
        lambda y, z, core, x: (y, 3 - z, core, x),
        lambda y, z, core, x: (y ^ 1, z, core, x),
        lambda y, z, core, x: (3 - y, z, core, x),
        lambda y, z, core, x: (y, z, core, x ^ 1),
        lambda y, z, core, x: (y, z, core, 3 - x),
    ):
        v = _meet(v, partner)
    return v


def _shape(*dims):
    return jax.ShapeDtypeStruct(dims, F32)


def per_device(h, zones, fluence, seed):
    d = lax.axis_index("dep")
    where = jnp.stack([lax.axis_index("lat"), d]).astype(jnp.int32)
    dep = d.astype(jnp.int32)[None]
    block = _shape(8, WIDE, 128)
    h_own, h1, h2, h3, edge, light, zid, light_own = pl.pallas_call(
        pack_state,
        out_shape=(block,) * 4 + (_shape(2, 8, 8, 128), _shape(128, 128), _shape(CORE, 128), _shape(WIDE, 128)),
        in_specs=[_smem(), _smem(), _full(), _full()],
        out_specs=(_full(),) * 8,
        scratch_shapes=[_vmem(8, 128 + 2 * HALO, 128), _vmem(128 + 2 * HALO, 128)],
        compiler_params=_params(),
        name="pack_state",
    )(dep, fluence, h, zones)
    h2, h1, h3 = _around(h2, 2), _around(h1, 1), _around(h3, 3)
    seed_block = _shape(8, SEED_WIDE, 128)
    edge_block = _shape(8, 16, 128)
    s_own, s1, s2, s3, *e = pl.pallas_call(
        pack_seed,
        out_shape=(seed_block,) * 4 + (edge_block,) * 4,
        in_specs=[_smem()] + [_full()] * 3,
        out_specs=(_full(),) * 8,
        scratch_shapes=[_vmem(8, 128 + 2 * SEED_HALO, 128), _vmem(2, 8, 16, 128)],
        compiler_params=_params(),
        name="pack_seed",
    )(dep, seed, edge, light)
    e = [_edges(e[j], j) for j in range(4)]
    s2, s1, s3 = _around(s2, 2), _around(s1, 1), _around(s3, 3)
    field = pltpu.VMEM((4, 32, HIGH, 128), F32)
    shade = pltpu.VMEM((4, 36, HIGH, 128), F32)
    states = pl.pallas_call(
        forward,
        out_shape=(field,) * 4 + (shade, pltpu.VMEM((HIGH, 128), F32)),
        in_specs=[_smem()] + [_full()] * 9,
        out_specs=(_full(),) * 6,
        scratch_shapes=[_vmem(32, HIGH, 128)] * 2,
        compiler_params=_params(),
        name="forward",
    )(where, h_own, h1, h2, h3, *e, light_own)
    a, zpart = pl.pallas_call(
        backward,
        out_shape=(pltpu.VMEM((32, HIGH, 128), F32), _shape(NZONE, 128)),
        in_specs=[_smem()] + [_full()] * 15,
        out_specs=(_full(),) * 2,
        scratch_shapes=[_vmem(32, HIGH, 128), _vmem(8, SEED_WIDE, 128)],
        compiler_params=_params(),
        name="backward",
    )(where, s_own, s1, s2, s3, *e, *states, zid)
    piece = _shape(8, CORE, 128)
    o_own, o1, o2, o3 = pl.pallas_call(
        last_step,
        out_shape=(piece,) * 4,
        in_specs=[_smem()] + [_full()] * 7,
        out_specs=(_full(),) * 4,
        scratch_shapes=[_vmem(32, HIGH, 128), _vmem(8, CORE, 128)],
        compiler_params=_params(),
        name="last_step",
    )(where, a, *states)
    o2, o1, o3 = _around(o2, 2), _around(o1, 1), _around(o3, 3)
    total = jnp.sum(total_of(zpart), axis=1)
    out = pl.pallas_call(
        unpack,
        out_shape=_shape(32, 32, 128),
        in_specs=[_smem()] + [_full()] * 4,
        out_specs=_full(),
        scratch_shapes=[_vmem(8, 128, 128)],
        compiler_params=_params(),
        name="unpack",
    )(where, o_own, o1, o2, o3)
    return out, total


def solution(mesh):
    in_specs = (P("dep", None, "lat"), P(None, "lat"), P(), P("dep", None, "lat"))
    out_specs = (P("dep", None, "lat"), P())
    return jax.shard_map(per_device, mesh=mesh, in_specs=in_specs, out_specs=out_specs, check_vma=False)
```

time: 458 us -> 89.2 us (0.19); the launches traced: 450 us -> 88.9 us
  blocking collectives: 203 us -> 0 us
  other arithmetic: 121 us -> 0.72 us
  waiting for transfers between devices: 46.8 us -> 18.6 us
  Pallas kernels: 0 us -> 25.5 us
  starting transfers between devices: 59.7 us -> 39.8 us
  local copies, waits for them, and re-layouts: 16.2 us -> 3.45 us
    all_gather x11 -> x0, blocking collectives: 131 us -> none  [entering(): gathered = lax.all_gather(part, axis)]
    psum x1 -> x0, blocking collectives: 72 us -> none  [per_device(): total = total + lax.psum(zone_part, ('lat', 'dep'))]
    another operation x19 -> x1, other arithmetic: 36.5 us -> 0.07 us  [per_device(): where = jnp.stack([lax.axis_index('lat'), d]).astype(jnp.int32)]
    mul x25 -> x0, other arithmetic: 35.5 us -> none  [the longest x12 24.3 us: heat_pullback(): masks[axis_orientation] * jump * 0.5]
    ppermute x28 -> x20, waiting for transfers between devices: 46.8 us -> 18.6 us  [the longest x7 13.7 us: _meet(): return v + lax.ppermute(v, ('lat', 'dep'), pairs)]
    pallas_call x0 -> x6, Pallas kernels: none -> 25.5 us  [the longest x1 10.5 us: per_device(): pl.pallas_call(forward, out_shape=(field,) * 4 + (shade, pltpu.VMEM((HIGH...]
    ppermute x28 -> x20, starting transfers between devices: 59.7 us -> 39.8 us  [the longest x9 20.9 us: _around(): return lax.ppermute(x, 'dep', [(s, (s + k) % 4) for s in range(4)])]
    sub x4 -> x0, other arithmetic: 14.7 us -> none  [silicon_constants(): rise = jax.nn.sigmoid(lower) - jax.nn.sigmoid(upper)]
  transfers between devices with their start and end apart: 28 -> 20, of which waited for: 15 -> 7; matrix products, arithmetic and copies ran while one was open for 1% -> 1% of each run, Pallas kernels for 0% -> 15%
where the time goes in v1:
time: 89.2 us; the launch traced here: 88.9 us
  starting transfers between devices  39.8 us (45%)
  Pallas kernels  25.5 us (29%)
  waiting for transfers between devices  18.6 us (21%)
  local copies, waits for them, and re-layouts  3.45 us (4%)
    ppermute x9, starting transfers between devices, _around(): return lax.ppermute(x, 'dep', [(s, (s + k) % 4) for s in range(4)])  20.9 us
    ppermute x7, starting transfers between devices, _meet(): return v + lax.ppermute(v, ('lat', 'dep'), pairs)  15.5 us
    ppermute x7, waiting for transfers between devices, _meet(): return v + lax.ppermute(v, ('lat', 'dep'), pairs)  13.7 us
    pallas_call x1, Pallas kernels, per_device(): pl.pallas_call(forward, out_shape=(field,) * 4 + (shade, pltpu.VMEM((HIGH...  10.5 us
    pallas_call x1, Pallas kernels, per_device(): pl.pallas_call(backward, out_shape=(pltpu.VMEM((32, HIGH, 128), F32), _sh...  9.48 us
    ppermute x9, waiting for transfers between devices, _around(): return lax.ppermute(x, 'dep', [(s, (s + k) % 4) for s in range(4)])  4.93 us
    ppermute x4, starting transfers between devices, _edges(): return lax.ppermute(x, ('lat', 'dep'), pairs)  3.46 us
    unnamed x8, local copies, waits for them, and re-layouts  3.45 us
  transfers between devices with their start and end apart: 20, of which 7 were waited for; matrix products, arithmetic and copies ran while one was open for 1% of the time, Pallas kernels for 15%

profile of v1, /device:TPU:0, one launch (start us, length us, event | category | flops | bytes accessed | tf_op | source)
XLA Modules:
  0.0 88.9 jit_solution(10004534504206393265)
XLA Ops:
  0.6 1.0 %copy-done = f32[32,32,128]{2,1,0:T(8,128)S(1)} copy-done((f32[32,32,128]{2,1,0:T(8,128)S(1)}, f32[32,32,128]{2,1,0:T(8,128)}, u32[]{:S(2)}) %copy-start) | copy-done | bytes 524312
  1.7 0.7 copy-done.2
  2.4 0.7 copy-done.3
  3.1 0.8 pack_state.1
  3.9 1.6 %collective-permute-start.7 = (f32[8,48,128]{2,1,0:T(8,128)S(1)}, f32[8,48,128]{2,1,0:T(8,128)S(1)}, u32[]{:S(2)}, u32[]{:S(2)}) collective-permute-start(f32[8,48,128]{2,1,0:T(8,128)S(1)} %get-tuple-element.41), channel_id=1, source_target_pairs={{0,1},{1,2},{2,3},{3,0},{4,5},{5,6},{6,7},{7,4},{8,9},{9,10},{10,1... | collective-permute-start | bytes 589832 | tf_op jit(solution)/shard_map/ppermute | solution.py:367
  5.5 1.0 %copy-done.1 = f32[32,32,128]{2,1,0:T(8,128)S(1)} copy-done((f32[32,32,128]{2,1,0:T(8,128)S(1)}, f32[32,32,128]{2,1,0:T(8,128)}, u32[]{:S(2)}) %copy-start.1) | copy-done | bytes 524312
  6.6 0.2 pack_seed.1
  6.8 1.5 %collective-permute-start.3 = (f32[8,16,128]{2,1,0:T(8,128)S(1)}, f32[8,16,128]{2,1,0:T(8,128)S(1)}, u32[]{:S(2)}, u32[]{:S(2)}) collective-permute-start(f32[8,16,128]{2,1,0:T(8,128)S(1)} %get-tuple-element.36), channel_id=1, source_target_pairs={{0,4},{4,8},{8,12},{12,16},{16,20},{20,24},{24,28},{28,32},{32,36}... | collective-permute-start | bytes 196616 | tf_op jit(solution)/shard_map/ppermute | solution.py:373
  8.3 0.7 collective-permute-start.4
  8.9 0.7 collective-permute-start.5
  9.6 0.7 collective-permute-start.6
  10.3 0.0 collective-permute-done.3.e0
  10.3 7.6 %collective-permute-start.8 = (f32[8,48,128]{2,1,0:T(8,128)S(1)}, f32[8,48,128]{2,1,0:T(8,128)S(1)}, u32[]{:S(2)}, u32[]{:S(2)}) collective-permute-start(f32[8,48,128]{2,1,0:T(8,128)S(1)} %get-tuple-element.42), channel_id=1, source_target_pairs={{0,2},{1,3},{2,0},{3,1},{4,6},{5,7},{6,4},{7,5},{8,10},{9,11},{10,... | collective-permute-start | bytes 589832 | tf_op jit(solution)/shard_map/ppermute | solution.py:367
  17.9 0.0 collective-permute-done.4.e1
  17.9 1.8 %collective-permute-start.9 = (f32[8,48,128]{2,1,0:T(8,128)S(1)}, f32[8,48,128]{2,1,0:T(8,128)S(1)}, u32[]{:S(2)}, u32[]{:S(2)}) collective-permute-start(f32[8,48,128]{2,1,0:T(8,128)S(1)} %get-tuple-element.43), channel_id=1, source_target_pairs={{0,3},{1,0},{2,1},{3,2},{4,7},{5,4},{6,5},{7,6},{8,11},{9,8},{10,9... | collective-permute-start | bytes 589832 | tf_op jit(solution)/shard_map/ppermute | solution.py:367
  19.7 0.0 collective-permute-done.5.e2
  19.7 0.2 collective-permute-start
  19.9 0.0 collective-permute-done.6.e3
  19.9 4.2 %collective-permute-start.1 = (f32[8,40,128]{2,1,0:T(8,128)S(1)}, f32[8,40,128]{2,1,0:T(8,128)S(1)}, u32[]{:S(2)}, u32[]{:S(2)}) collective-permute-start(f32[8,40,128]{2,1,0:T(8,128)S(1)} %get-tuple-element.34), channel_id=1, source_target_pairs={{0,2},{1,3},{2,0},{3,1},{4,6},{5,7},{6,4},{7,5},{8,10},{9,11},{10,... | collective-permute-start | bytes 491528 | tf_op jit(solution)/shard_map/ppermute | solution.py:367
  24.1 0.0 collective-permute-done.7.r1
  24.1 0.0 collective-permute-start.2
  24.1 0.1 pad_add_fusion.where
  24.1 0.0 collective-permute-done.8.r2
  24.1 4.9 %collective-permute-done.9.r3 = f32[8,48,128]{2,1,0:T(8,128)S(1)} collective-permute-done((f32[8,48,128]{2,1,0:T(8,128)S(1)}, f32[8,48,128]{2,1,0:T(8,128)S(1)}, u32[]{:S(2)}, u32[]{:S(2)}) %collective-permute-start.9) | collective-permute-done | bytes 196640 | tf_op jit(solution)/shard_map/ppermute | solution.py:367
  29.1 10.5 %forward.1 = (f32[4,32,64,128]{3,2,1,0:T(8,128)S(1)}, f32[4,32,64,128]{3,2,1,0:T(8,128)S(1)}, f32[4,32,64,128]{3,2,1,0:T(8,128)S(1)}, f32[4,32,64,128]{3,2,1,0:T...) custom-call(s32[2]{0:T(128)S(1)} %pad_add_fusion.where, f32[8,48,128]{2,1,0:T(8,128)S(1)} %get-tuple-element.40.own, ...), custom_call_target="tpu_custom_call" | custom-call | tf_op jit(solution)/shard_map/forward/pallas_call | solution.py:438
  39.5 0.0 collective-permute-done.r1
  39.5 0.0 collective-permute-done.2.r3
  39.5 9.5 %backward.1 = (f32[32,64,128]{2,1,0:T(8,128)S(1)}, f32[16,128]{1,0:T(8,128)S(1)}) custom-call(s32[2]{0:T(128)S(1)} %pad_add_fusion.where, f32[8,40,128]{2,1,0:T(8,128)S(1)} %get-tuple-element.32.own, f32[8,40,128]{2,1,0:T(8,128)S(1)} %collective-permute-done.r1, f32[8,40,128]{2,1,0:T(8,128)S(1)} %collective-permute-done.1.r2, ...), custom_call_target="tpu_custom_call" | custom-call | tf_op jit(solution)/shard_map/backward/pallas_call | solution.py:447
  49.0 1.3 %collective-permute-start.13 = (f32[16,128]{1,0:T(8,128)S(1)}, f32[16,128]{1,0:T(8,128)S(1)}, u32[]{:S(2)}, u32[]{:S(2)}) collective-permute-start(f32[16,128]{1,0:T(8,128)S(1)} %get-tuple-element.57), channel_id=1, source_target_pairs={{0,4},{1,5},{2,6},{3,7},{4,0},{5,1},{6,2},{7,3},{8,12},{9,13},{10,... | collective-permute-start | bytes 24584 | tf_op jit(solution)/shard_map/ppermute | solution.py:387
  50.4 0.8 collective-permute-done.13
  51.2 1.9 %collective-permute-start.14 = (f32[16,128]{1,0:T(8,128)S(1)}, f32[16,128]{1,0:T(8,128)S(1)}, u32[]{:S(2)}, u32[]{:S(2)}) collective-permute-start(f32[16,128]{1,0:T(8,128)S(1)} %add.21), channel_id=1, source_target_pairs={{0,8},{1,9},{2,10},{3,11},{4,12},{5,13},{6,14},{7,15},{8,0},{9,1},... | collective-permute-start | bytes 24584 | tf_op jit(solution)/shard_map/ppermute | solution.py:387
  53.2 1.7 %collective-permute-done.14 = f32[16,128]{1,0:T(8,128)S(1)} collective-permute-done((f32[16,128]{1,0:T(8,128)S(1)}, f32[16,128]{1,0:T(8,128)S(1)}, u32[]{:S(2)}, u32[]{:S(2)}) %collective-permute-start.14) | collective-permute-done | bytes 8224 | tf_op jit(solution)/shard_map/ppermute | solution.py:387
  54.9 3.3 %collective-permute-start.15 = (f32[16,128]{1,0:T(8,128)S(1)}, f32[16,128]{1,0:T(8,128)S(1)}, u32[]{:S(2)}, u32[]{:S(2)}) collective-permute-start(f32[16,128]{1,0:T(8,128)S(1)} %add.22), channel_id=1, source_target_pairs={{0,24},{1,25},{2,26},{3,27},{4,28},{5,29},{6,30},{7,31},{8,16},{9,... | collective-permute-start | bytes 24584 | tf_op jit(solution)/shard_map/ppermute | solution.py:387
  58.1 1.6 %collective-permute-done.15 = f32[16,128]{1,0:T(8,128)S(1)} collective-permute-done((f32[16,128]{1,0:T(8,128)S(1)}, f32[16,128]{1,0:T(8,128)S(1)}, u32[]{:S(2)}, u32[]{:S(2)}) %collective-permute-start.15) | collective-permute-done | bytes 8224 | tf_op jit(solution)/shard_map/ppermute | solution.py:387
  59.8 3.5 %collective-permute-start.16 = (f32[16,128]{1,0:T(8,128)S(1)}, f32[16,128]{1,0:T(8,128)S(1)}, u32[]{:S(2)}, u32[]{:S(2)}) collective-permute-start(f32[16,128]{1,0:T(8,128)S(1)} %add.23), channel_id=1, source_target_pairs={{0,32},{1,33},{2,34},{3,35},{4,36},{5,37},{6,38},{7,39},{8,40},{9,... | collective-permute-start | bytes 24584 | tf_op jit(solution)/shard_map/ppermute | solution.py:387
  63.3 1.6 %collective-permute-done.16 = f32[16,128]{1,0:T(8,128)S(1)} collective-permute-done((f32[16,128]{1,0:T(8,128)S(1)}, f32[16,128]{1,0:T(8,128)S(1)}, u32[]{:S(2)}, u32[]{:S(2)}) %collective-permute-start.16) | collective-permute-done | bytes 8224 | tf_op jit(solution)/shard_map/ppermute | solution.py:387
  64.9 3.5 %collective-permute-start.17 = (f32[16,128]{1,0:T(8,128)S(1)}, f32[16,128]{1,0:T(8,128)S(1)}, u32[]{:S(2)}, u32[]{:S(2)}) collective-permute-start(f32[16,128]{1,0:T(8,128)S(1)} %add.24), channel_id=1, source_target_pairs={{0,96},{1,97},{2,98},{3,99},{4,100},{5,101},{6,102},{7,103},{8,104... | collective-permute-start | bytes 24584 | tf_op jit(solution)/shard_map/ppermute | solution.py:387
  68.4 2.9 %last_step.1 = (f32[8,32,128]{2,1,0:T(8,128)S(1)}, f32[8,32,128]{2,1,0:T(8,128)S(1)}, f32[8,32,128]{2,1,0:T(8,128)S(1)}, f32[8,32,128]{2,1,0:T(8,128)S(1)}) custom-call(s32[2]{0:T(128)S(1)} %pad_add_fusion.where, f32[32,64,128]{2,1,0:T(8,128)S(1)} %get-tuple-element.52.a_ref, f32[4,32,64,128]{3,2,1,0:T(8,128)S(1)} %get-tuple-element.45.t_ref, ...), custom_call_target="tpu_custom_call" | custom-call | tf_op jit(solution)/shard_map/last_step/pallas_call | solution.py:457
  71.4 2.6 %collective-permute-start.10 = (f32[8,32,128]{2,1,0:T(8,128)S(1)}, f32[8,32,128]{2,1,0:T(8,128)S(1)}, u32[]{:S(2)}, u32[]{:S(2)}) collective-permute-start(f32[8,32,128]{2,1,0:T(8,128)S(1)} %get-tuple-element.54), channel_id=1, source_target_pairs={{0,1},{1,2},{2,3},{3,0},{4,5},{5,6},{6,7},{7,4},{8,9},{9,10},{10,1... | collective-permute-start | bytes 393224 | tf_op jit(solution)/shard_map/ppermute | solution.py:367
  73.9 2.8 %collective-permute-start.11 = (f32[8,32,128]{2,1,0:T(8,128)S(1)}, f32[8,32,128]{2,1,0:T(8,128)S(1)}, u32[]{:S(2)}, u32[]{:S(2)}) collective-permute-start(f32[8,32,128]{2,1,0:T(8,128)S(1)} %get-tuple-element.55), channel_id=1, source_target_pairs={{0,2},{1,3},{2,0},{3,1},{4,6},{5,7},{6,4},{7,5},{8,10},{9,11},{10,... | collective-permute-start | bytes 393224 | tf_op jit(solution)/shard_map/ppermute | solution.py:367
  76.7 0.1 collective-permute-start.12
  76.9 0.0 collective-permute-done.17
  76.9 1.9 %collective-permute-start.18 = (f32[16,128]{1,0:T(8,128)S(1)}, f32[16,128]{1,0:T(8,128)S(1)}, u32[]{:S(2)}, u32[]{:S(2)}) collective-permute-start(f32[16,128]{1,0:T(8,128)S(1)} %add.25), channel_id=1, source_target_pairs={{0,1},{1,0},{2,3},{3,2},{4,5},{5,4},{6,7},{7,6},{8,9},{9,8},{10,11... | collective-permute-start | bytes 24584 | tf_op jit(solution)/shard_map/ppermute | solution.py:387
  78.8 3.0 %collective-permute-done.18 = f32[16,128]{1,0:T(8,128)S(1)} collective-permute-done((f32[16,128]{1,0:T(8,128)S(1)}, f32[16,128]{1,0:T(8,128)S(1)}, u32[]{:S(2)}, u32[]{:S(2)}) %collective-permute-start.18) | collective-permute-done | bytes 8224 | tf_op jit(solution)/shard_map/ppermute | solution.py:387
  81.8 4.9 %collective-permute-done.19 = f32[16,128]{1,0:T(8,128)S(1)} collective-permute-done((f32[16,128]{1,0:T(8,128)S(1)}, f32[16,128]{1,0:T(8,128)S(1)}, u32[]{:S(2)}, u32[]{:S(2)}) %collective-permute-start.19) | collective-permute-done | bytes 8224 | tf_op jit(solution)/shard_map/ppermute | solution.py:387
  86.6 0.6 add_reduce_fusion
  87.3 0.0 collective-permute-done.10.r1
  87.3 1.6 %unpack.1 = f32[32,32,128]{2,1,0:T(8,128)} custom-call(s32[2]{0:T(128)S(1)} %pad_add_fusion.where, f32[8,32,128]{2,1,0:T(8,128)S(1)} %get-tuple-element.53.own, f32[8,32,128]{2,1,0:T(8,128)S(1)} %collective-permute-done.10.r1, f32[8,32,128]{2,1,0:T(8,128)S(1)} %collective-permute-done.11.r2, f32[8,32,128]{2,1,0:T(8,128)S(1)} %collective-permute-done.12.r3), custom_call_target="tpu_custom_call" | custom-call | tf_op jit(solution)/shard_map/unpack/pallas_call | solution.py:468
  (14 shorter events, 0.0 us)
Async XLA Ops:
  0.6 1.0 %copy-start = (f32[32,32,128]{2,1,0:T(8,128)S(1)}, f32[32,32,128]{2,1,0:T(8,128)}, u32[]{:S(2)}) copy-start(f32[32,32,128]{2,1,0:T(8,128)} %h_ref.1) | copy-start | bytes 1572868
  1.7 0.7 copy-start.2
  2.4 0.7 copy-start.3
  3.9 20.2 %collective-permute-start.7 = (f32[8,48,128]{2,1,0:T(8,128)S(1)}, f32[8,48,128]{2,1,0:T(8,128)S(1)}, u32[]{:S(2)}, u32[]{:S(2)}) collective-permute-start(f32[8,48,128]{2,1,0:T(8,128)S(1)} %get-tuple-element.41), channel_id=1, source_target_pairs={{0,1},{1,2},{2,3},{3,0},{4,5},{5,6},{6,7},{7,4},{8,9},{9,10},{10,1... | collective-permute-start | bytes 589832 | tf_op jit(solution)/shard_map/ppermute | solution.py:367
  5.5 1.0 %copy-start.1 = (f32[32,32,128]{2,1,0:T(8,128)S(1)}, f32[32,32,128]{2,1,0:T(8,128)}, u32[]{:S(2)}) copy-start(f32[32,32,128]{2,1,0:T(8,128)} %a_ref.1) | copy-start | bytes 1572868
  6.8 3.5 %collective-permute-start.3 = (f32[8,16,128]{2,1,0:T(8,128)S(1)}, f32[8,16,128]{2,1,0:T(8,128)S(1)}, u32[]{:S(2)}, u32[]{:S(2)}) collective-permute-start(f32[8,16,128]{2,1,0:T(8,128)S(1)} %get-tuple-element.36), channel_id=1, source_target_pairs={{0,4},{4,8},{8,12},{12,16},{16,20},{20,24},{24,28},{28,32},{32,36}... | collective-permute-start | bytes 196616 | tf_op jit(solution)/shard_map/ppermute | solution.py:373
  8.3 9.6 %collective-permute-start.4 = (f32[8,16,128]{2,1,0:T(8,128)S(1)}, f32[8,16,128]{2,1,0:T(8,128)S(1)}, u32[]{:S(2)}, u32[]{:S(2)}) collective-permute-start(f32[8,16,128]{2,1,0:T(8,128)S(1)} %get-tuple-element.37), channel_id=1, source_target_pairs={{3,4},{7,8},{11,12},{15,16},{19,20},{23,24},{27,28},{31,32},{35,36... | collective-permute-start | bytes 196616 | tf_op jit(solution)/shard_map/ppermute | solution.py:373
  8.9 10.7 %collective-permute-start.5 = (f32[8,16,128]{2,1,0:T(8,128)S(1)}, f32[8,16,128]{2,1,0:T(8,128)S(1)}, u32[]{:S(2)}, u32[]{:S(2)}) collective-permute-start(f32[8,16,128]{2,1,0:T(8,128)S(1)} %get-tuple-element.38), channel_id=1, source_target_pairs={{2,4},{6,8},{10,12},{14,16},{18,20},{22,24},{26,28},{30,32},{34,36... | collective-permute-start | bytes 196616 | tf_op jit(solution)/shard_map/ppermute | solution.py:373
  9.6 10.3 %collective-permute-start.6 = (f32[8,16,128]{2,1,0:T(8,128)S(1)}, f32[8,16,128]{2,1,0:T(8,128)S(1)}, u32[]{:S(2)}, u32[]{:S(2)}) collective-permute-start(f32[8,16,128]{2,1,0:T(8,128)S(1)} %get-tuple-element.39), channel_id=1, source_target_pairs={{1,4},{5,8},{9,12},{13,16},{17,20},{21,24},{25,28},{29,32},{33,36}... | collective-permute-start | bytes 196616 | tf_op jit(solution)/shard_map/ppermute | solution.py:373
  10.3 13.8 %collective-permute-start.8 = (f32[8,48,128]{2,1,0:T(8,128)S(1)}, f32[8,48,128]{2,1,0:T(8,128)S(1)}, u32[]{:S(2)}, u32[]{:S(2)}) collective-permute-start(f32[8,48,128]{2,1,0:T(8,128)S(1)} %get-tuple-element.42), channel_id=1, source_target_pairs={{0,2},{1,3},{2,0},{3,1},{4,6},{5,7},{6,4},{7,5},{8,10},{9,11},{10,... | collective-permute-start | bytes 589832 | tf_op jit(solution)/shard_map/ppermute | solution.py:367
  17.9 11.2 %collective-permute-start.9 = (f32[8,48,128]{2,1,0:T(8,128)S(1)}, f32[8,48,128]{2,1,0:T(8,128)S(1)}, u32[]{:S(2)}, u32[]{:S(2)}) collective-permute-start(f32[8,48,128]{2,1,0:T(8,128)S(1)} %get-tuple-element.43), channel_id=1, source_target_pairs={{0,3},{1,0},{2,1},{3,2},{4,7},{5,4},{6,5},{7,6},{8,11},{9,8},{10,9... | collective-permute-start | bytes 589832 | tf_op jit(solution)/shard_map/ppermute | solution.py:367
  19.7 19.9 %collective-permute-start = (f32[8,40,128]{2,1,0:T(8,128)S(1)}, f32[8,40,128]{2,1,0:T(8,128)S(1)}, u32[]{:S(2)}, u32[]{:S(2)}) collective-permute-start(f32[8,40,128]{2,1,0:T(8,128)S(1)} %get-tuple-element.33), channel_id=1, source_target_pairs={{0,1},{1,2},{2,3},{3,0},{4,5},{5,6},{6,7},{7,4},{8,9},{9,10},{10,1... | collective-permute-start | bytes 491528 | tf_op jit(solution)/shard_map/ppermute | solution.py:367
  19.9 19.6 %collective-permute-start.1 = (f32[8,40,128]{2,1,0:T(8,128)S(1)}, f32[8,40,128]{2,1,0:T(8,128)S(1)}, u32[]{:S(2)}, u32[]{:S(2)}) collective-permute-start(f32[8,40,128]{2,1,0:T(8,128)S(1)} %get-tuple-element.34), channel_id=1, source_target_pairs={{0,2},{1,3},{2,0},{3,1},{4,6},{5,7},{6,4},{7,5},{8,10},{9,11},{10,... | collective-permute-start | bytes 491528 | tf_op jit(solution)/shard_map/ppermute | solution.py:367
  24.1 15.5 %collective-permute-start.2 = (f32[8,40,128]{2,1,0:T(8,128)S(1)}, f32[8,40,128]{2,1,0:T(8,128)S(1)}, u32[]{:S(2)}, u32[]{:S(2)}) collective-permute-start(f32[8,40,128]{2,1,0:T(8,128)S(1)} %get-tuple-element.35), channel_id=1, source_target_pairs={{0,3},{1,0},{2,1},{3,2},{4,7},{5,4},{6,5},{7,6},{8,11},{9,8},{10,9... | collective-permute-start | bytes 491528 | tf_op jit(solution)/shard_map/ppermute | solution.py:367
  49.0 2.2 %collective-permute-start.13 = (f32[16,128]{1,0:T(8,128)S(1)}, f32[16,128]{1,0:T(8,128)S(1)}, u32[]{:S(2)}, u32[]{:S(2)}) collective-permute-start(f32[16,128]{1,0:T(8,128)S(1)} %get-tuple-element.57), channel_id=1, source_target_pairs={{0,4},{1,5},{2,6},{3,7},{4,0},{5,1},{6,2},{7,3},{8,12},{9,13},{10,... | collective-permute-start | bytes 24584 | tf_op jit(solution)/shard_map/ppermute | solution.py:387
  51.2 3.7 %collective-permute-start.14 = (f32[16,128]{1,0:T(8,128)S(1)}, f32[16,128]{1,0:T(8,128)S(1)}, u32[]{:S(2)}, u32[]{:S(2)}) collective-permute-start(f32[16,128]{1,0:T(8,128)S(1)} %add.21), channel_id=1, source_target_pairs={{0,8},{1,9},{2,10},{3,11},{4,12},{5,13},{6,14},{7,15},{8,0},{9,1},... | collective-permute-start | bytes 24584 | tf_op jit(solution)/shard_map/ppermute | solution.py:387
  54.9 4.9 %collective-permute-start.15 = (f32[16,128]{1,0:T(8,128)S(1)}, f32[16,128]{1,0:T(8,128)S(1)}, u32[]{:S(2)}, u32[]{:S(2)}) collective-permute-start(f32[16,128]{1,0:T(8,128)S(1)} %add.22), channel_id=1, source_target_pairs={{0,24},{1,25},{2,26},{3,27},{4,28},{5,29},{6,30},{7,31},{8,16},{9,... | collective-permute-start | bytes 24584 | tf_op jit(solution)/shard_map/ppermute | solution.py:387
  59.8 5.1 %collective-permute-start.16 = (f32[16,128]{1,0:T(8,128)S(1)}, f32[16,128]{1,0:T(8,128)S(1)}, u32[]{:S(2)}, u32[]{:S(2)}) collective-permute-start(f32[16,128]{1,0:T(8,128)S(1)} %add.23), channel_id=1, source_target_pairs={{0,32},{1,33},{2,34},{3,35},{4,36},{5,37},{6,38},{7,39},{8,40},{9,... | collective-permute-start | bytes 24584 | tf_op jit(solution)/shard_map/ppermute | solution.py:387
  64.9 12.0 %collective-permute-start.17 = (f32[16,128]{1,0:T(8,128)S(1)}, f32[16,128]{1,0:T(8,128)S(1)}, u32[]{:S(2)}, u32[]{:S(2)}) collective-permute-start(f32[16,128]{1,0:T(8,128)S(1)} %add.24), channel_id=1, source_target_pairs={{0,96},{1,97},{2,98},{3,99},{4,100},{5,101},{6,102},{7,103},{8,104... | collective-permute-start | bytes 24584 | tf_op jit(solution)/shard_map/ppermute | solution.py:387
  71.4 15.9 %collective-permute-start.10 = (f32[8,32,128]{2,1,0:T(8,128)S(1)}, f32[8,32,128]{2,1,0:T(8,128)S(1)}, u32[]{:S(2)}, u32[]{:S(2)}) collective-permute-start(f32[8,32,128]{2,1,0:T(8,128)S(1)} %get-tuple-element.54), channel_id=1, source_target_pairs={{0,1},{1,2},{2,3},{3,0},{4,5},{5,6},{6,7},{7,4},{8,9},{9,10},{10,1... | collective-permute-start | bytes 393224 | tf_op jit(solution)/shard_map/ppermute | solution.py:367
  73.9 13.3 %collective-permute-start.11 = (f32[8,32,128]{2,1,0:T(8,128)S(1)}, f32[8,32,128]{2,1,0:T(8,128)S(1)}, u32[]{:S(2)}, u32[]{:S(2)}) collective-permute-start(f32[8,32,128]{2,1,0:T(8,128)S(1)} %get-tuple-element.55), channel_id=1, source_target_pairs={{0,2},{1,3},{2,0},{3,1},{4,6},{5,7},{6,4},{7,5},{8,10},{9,11},{10,... | collective-permute-start | bytes 393224 | tf_op jit(solution)/shard_map/ppermute | solution.py:367
  76.7 10.6 %collective-permute-start.12 = (f32[8,32,128]{2,1,0:T(8,128)S(1)}, f32[8,32,128]{2,1,0:T(8,128)S(1)}, u32[]{:S(2)}, u32[]{:S(2)}) collective-permute-start(f32[8,32,128]{2,1,0:T(8,128)S(1)} %get-tuple-element.56), channel_id=1, source_target_pairs={{0,3},{1,0},{2,1},{3,2},{4,7},{5,4},{6,5},{7,6},{8,11},{9,8},{10,9... | collective-permute-start | bytes 393224 | tf_op jit(solution)/shard_map/ppermute | solution.py:367
  76.9 4.9 %collective-permute-start.18 = (f32[16,128]{1,0:T(8,128)S(1)}, f32[16,128]{1,0:T(8,128)S(1)}, u32[]{:S(2)}, u32[]{:S(2)}) collective-permute-start(f32[16,128]{1,0:T(8,128)S(1)} %add.25), channel_id=1, source_target_pairs={{0,1},{1,0},{2,3},{3,2},{4,5},{5,4},{6,7},{7,6},{8,9},{9,8},{10,11... | collective-permute-start | bytes 24584 | tf_op jit(solution)/shard_map/ppermute | solution.py:387
  81.8 4.9 %collective-permute-start.19 = (f32[16,128]{1,0:T(8,128)S(1)}, f32[16,128]{1,0:T(8,128)S(1)}, u32[]{:S(2)}, u32[]{:S(2)}) collective-permute-start(f32[16,128]{1,0:T(8,128)S(1)} %add.26), channel_id=1, source_target_pairs={{0,3},{1,2},{2,1},{3,0},{4,7},{5,6},{6,5},{7,4},{8,11},{9,10},{10,... | collective-permute-start | bytes 24584 | tf_op jit(solution)/shard_map/ppermute | solution.py:387

commit v2 on v0

v2 whole, which is shorter than its diff:
```python
import math

import jax
import jax.numpy as jnp
from jax import lax
from jax.experimental import pallas as pl
from jax.experimental.pallas import tpu as pltpu
from jax.sharding import PartitionSpec as P


NZONE = 16
CORE = 32
HALO = 8
WIDE = CORE + 2 * HALO
SEED_HALO = 4
SEED_WIDE = CORE + 2 * SEED_HALO
BASE = 8
HIGH = WIDE + 2 * BASE
DT = 0.1
ABSORB_SOLID = 0.004
ABSORB_RISE = 0.026
LOG2E = math.log2(math.e)
EM10 = math.exp(-10.0)
F32 = jnp.float32


def _params():
    return pltpu.CompilerParams(vmem_limit_bytes=16 * 1024 * 1024)


def _vmem(*shape):
    return pltpu.VMEM(shape, F32)


def _full():
    return pl.BlockSpec(memory_space=pltpu.VMEM)


def _any():
    return pl.BlockSpec(memory_space=pl.ANY)


def _lanes():
    return lax.broadcasted_iota(jnp.int32, (8, 128), 1)


def _packed(ref, g, d):
    tiles = []
    for p in range(4):
        rf = lax.rem(p + 4 - d, 4)
        tiles += [ref[8 * sub + g, pl.ds(rf, 8, stride=4)] for sub in range(4)]
    return jnp.concatenate(tiles, axis=0).T


def _surface(ref, rf):
    return jnp.concatenate([ref[pl.ds(rf, 8, stride=4)]] * 16, axis=0).T


def pack(fluence_in, h_in, zones_in, a_in, state, seed, light, zid, to_right, to_left, h, a, zones, flat, zbuf, fluence, sems):
    d = lax.axis_index("dep")
    copies = [
        pltpu.make_async_copy(source, target, sems.at[k])
        for k, (source, target) in enumerate(((h_in, h), (zones_in, zones), (fluence_in, fluence), (a_in, a)))
    ]
    for copy in copies:
        copy.start()
    copies[0].wait()
    for g in range(8):
        packed = _packed(h, g, d)
        state[g] = packed
        to_left[g, 0:8] = packed[0:8]
        to_right[g, 0:8] = packed[120:128]
    copies[1].wait()
    copies[2].wait()
    ids = zones[...]
    intensity = jnp.zeros(ids.shape, F32)
    for k in range(NZONE):
        intensity = jnp.where(ids == k, fluence[k] * DT, intensity)
    flat[0] = intensity
    flat[1] = ids.astype(F32)
    start = pl.multiple_of(d * CORE, CORE)
    for rf in range(4):
        packed = _surface(flat.at[0], rf)
        light[rf] = packed
        for half in range(2):
            to_left[2 * rf + half, 12:16] = packed[4 * half : 4 * half + 4]
            to_right[2 * rf + half, 12:16] = packed[120 + 4 * half : 124 + 4 * half]
        zbuf[...] = _surface(flat.at[1], rf)
        zid[rf] = zbuf[pl.ds(start, CORE)]
    copies[3].wait()
    for g in range(8):
        packed = _packed(a, g, d)
        seed[g] = packed
        to_left[g, 8:12] = packed[0:4]
        to_right[g, 8:12] = packed[124:128]


def insert(state, seed, light, left, right, h0, h1, h2, h3, s0, s1, s2, s3, light_own, hbuf, sbuf, lbuf):
    d = lax.axis_index("dep")
    hbuf[:, 0:8] = left[:, 0:8]
    hbuf[:, 8:136] = state[...]
    hbuf[:, 136:144] = right[:, 0:8]
    for k, out in enumerate((h0, h1, h2, h3)):
        start = pl.multiple_of(lax.rem(d + k, 4) * CORE, CORE)
        out[...] = hbuf[:, pl.ds(start, WIDE)]
    sbuf[:, 0:4] = left[:, 8:12]
    sbuf[:, 4:132] = seed[...]
    sbuf[:, 132:136] = right[:, 8:12]
    for k, out in enumerate((s0, s1, s2, s3)):
        start = pl.multiple_of(lax.rem(d + k, 4) * CORE, CORE)
        out[...] = sbuf[:, pl.ds(start, SEED_WIDE)]
    start = pl.multiple_of(d * CORE, CORE)
    for rf in range(4):
        for half in range(2):
            lbuf[4 * half : 4 * half + 4] = left[2 * rf + half, 12:16]
            lbuf[136 + 4 * half : 140 + 4 * half] = right[2 * rf + half, 12:16]
        lbuf[8:136] = light[rf]
        light_own[rf] = lbuf[pl.ds(start, WIDE)]


def _source_masks():
    part = lax.rem(_lanes() // 32 + 4 - lax.axis_index("dep"), 4)
    return [part == j for j in range(4)]


def _pick(masks, shift, values):
    return jnp.where(
        masks[shift % 4],
        values[0],
        jnp.where(masks[(shift + 1) % 4], values[1], jnp.where(masks[(shift + 2) % 4], values[2], values[3])),
    )


def _gather(blocks, field, first, count):
    masks = _source_masks()

    def tile(i, carry):
        g, c = i // (count // 8), pl.multiple_of(lax.rem(i, count // 8) * 8, 8)
        own, r1, r2, r3 = [block[g, pl.ds(c, 8)] for block in blocks]
        for rf in range(4):
            mixed = _pick(masks, rf, (own, r3, r2, r1))
            field[8 * rf + g, pl.ds(BASE + first + c, 8)] = mixed if rf == 0 else pltpu.roll(mixed, 128 - 32 * rf, 1)
        return carry

    lax.fori_loop(0, count, tile, 0, unroll=2)


class _Tiles:
    def __init__(self, row):
        self.here, self.up, self.down = pl.ds(row, 8), pl.ds(row + 1, 8), pl.ds(row - 1, 8)


def _inclusive(total, lane, reverse):
    for step in (8, 16, 32, 64):
        if reverse:
            total = total + jnp.where(lane < 128 - step, pltpu.roll(total, 128 - step, 1), 0.0)
        else:
            total = total + jnp.where(lane >= step, pltpu.roll(total, step, 1), 0.0)
    return total


def _properties(n, rf, tiles, states, t_ref, k_ref, c_ref, r_ref, l_ref):
    lane = _lanes()
    here = tiles.here
    run = jnp.zeros((8, 128), F32)
    runs = []
    for g in range(8):
        i = 8 * rf + g
        h = states[g]
        e = jnp.exp2(h * (10.0 * LOG2E) - 10.0 * LOG2E)
        u = 1.0 + e
        v = 1.0 + EM10 * e
        inv = pl.reciprocal(u * v)
        ramp = 0.1 * jnp.log(u * (u * inv))
        t = h - ramp
        m = pl.reciprocal(1.0 + t * t)
        t_ref[n, i, here] = t
        k_ref[n, i, here] = 0.03 + 0.04 * m
        c_ref[n, i, here] = (-0.08 * t) * (m * m)
        r_ref[n, i, here] = e * ((1.0 - EM10) * inv)
        runs.append(run)
        run = run + (ABSORB_SOLID * LOG2E + (ABSORB_RISE * LOG2E) * ramp)
    above = _inclusive(run, lane, False) - run
    for g in range(8):
        l_ref[n, 9 * rf + g, here] = jnp.exp2(-(above + runs[g]))
    l_ref[n, 9 * rf + 8, here] = jnp.exp2(-(above + run))


def _advance(n, tiles, h_ref, t_ref, k_ref, l_ref, light, then):
    lane = _lanes()
    inside = lax.rem(lane, 8) < 7
    above_bottom = lane < 120
    here, up, down = tiles.here, tiles.up, tiles.down

    def across(g):
        t3, k3 = t_ref[n, 24 + g, here], k_ref[n, 24 + g, here]
        t0, k0 = pltpu.roll(t_ref[n, g, here], 127, 1), pltpu.roll(k_ref[n, g, here], 127, 1)
        return jnp.where(inside, (k3 + k0) * (t0 - t3), 0.0)

    last = [across(g) for g in range(8)]
    before = [pltpu.roll(f, 1, 1) for f in last]
    for rf in range(4):
        i0 = 8 * rf
        t = [t_ref[n, i0 + g, here] for g in range(8)]
        k = [k_ref[n, i0 + g, here] for g in range(8)]
        end = jnp.where(above_bottom, (k[7] + pltpu.roll(k[0], 120, 1)) * (pltpu.roll(t[0], 120, 1) - t[7]), 0.0)
        flux_before = pltpu.roll(end, 8, 1)
        new = []
        for g in range(8):
            i = i0 + g
            if g < 7:
                flux = (k[g] + k[g + 1]) * (t[g + 1] - t[g])
            else:
                flux = jnp.where(above_bottom, end, -0.05 * t[7])
            if rf < 3:
                side = (k[g] + k_ref[n, i + 8, here]) * (t_ref[n, i + 8, here] - t[g])
            else:
                side = last[g]
            change = (flux - flux_before) + (side - before[g])
            change = change + (
                (k[g] + k_ref[n, i, up]) * (t_ref[n, i, up] - t[g])
                - (k[g] + k_ref[n, i, down]) * (t[g] - t_ref[n, i, down])
            )
            source = light[rf, here] * (l_ref[n, 9 * rf + g, here] - l_ref[n, 9 * rf + g + 1, here])
            new.append(h_ref[i, here] + (change + source))
            flux_before, before[g] = flux, side
        then(rf, new)


def _ghost(ref_rows):
    lat, d = lax.axis_index("lat"), lax.axis_index("dep")

    @pl.when(jnp.logical_and(lat == 0, d == 0))
    def _():
        for i in range(32):
            ref_rows(i, HALO - 1)[...] = ref_rows(i, HALO)[...]

    @pl.when(jnp.logical_and(lat == 31, d == 3))
    def _():
        for i in range(32):
            ref_rows(i, HALO + CORE)[...] = ref_rows(i, HALO + CORE - 1)[...]


def forward(own, r1, r2, r3, light_own, t_ref, k_ref, c_ref, r_ref, l_ref, light, ha, hb):
    _gather((own, r1, r2, r3), ha, 0, WIDE)
    for rf in range(4):
        light[rf, BASE : BASE + WIDE] = light_own[rf]
    fields = (t_ref, k_ref, c_ref, r_ref, l_ref)

    def start(c, carry):
        tiles = _Tiles(BASE + 8 * c)
        for rf in range(4):
            _properties(0, rf, tiles, [ha[8 * rf + g, tiles.here] for g in range(8)], *fields)
        return carry

    lax.fori_loop(0, WIDE // 8, start, 0)
    source, target = ha, hb
    for n in range(3):
        _ghost(lambda i, c, n=n: t_ref.at[n, i, pl.ds(BASE + c, 1)])
        first, count = (0, WIDE) if n < 2 else (SEED_HALO, SEED_WIDE)

        def chunk(c, carry, n=n, first=first, source=source, target=target):
            tiles = _Tiles(BASE + first + 8 * c)

            def then(rf, new):
                for g in range(8):
                    if n < 2:
                        target[8 * rf + g, tiles.here] = new[g]
                _properties(n + 1, rf, tiles, new, *fields)

            _advance(n, tiles, source, t_ref, k_ref, l_ref, light, then)
            return carry

        lax.fori_loop(0, count // 8, chunk, 0)
        source, target = target, source


def _retreat(n, tiles, a_ref, t_ref, k_ref, c_ref, r_ref, l_ref, light, put, seen):
    lane = _lanes()
    inside = lax.rem(lane, 8) < 7
    above_bottom = lane < 120
    here, up, down = tiles.here, tiles.up, tiles.down

    def across(g):
        a3, t3, k3 = a_ref[24 + g, here], t_ref[n, 24 + g, here], k_ref[n, 24 + g, here]
        a0, t0, k0 = [pltpu.roll(x, 127, 1) for x in (a_ref[g, here], t_ref[n, g, here], k_ref[n, g, here])]
        jump = jnp.where(inside, a3 - a0, 0.0)
        return jump * (k3 + k0), jump * (t0 - t3)

    last = [across(g) for g in range(8)]
    before = [(pltpu.roll(push, 1, 1), pltpu.roll(share, 1, 1)) for push, share in last]
    for rf in range(4):
        i0 = 8 * rf
        a = [a_ref[i0 + g, here] for g in range(8)]
        t = [t_ref[n, i0 + g, here] for g in range(8)]
        k = [k_ref[n, i0 + g, here] for g in range(8)]
        run = jnp.zeros((8, 128), F32)
        runs = [None] * 8
        for g in reversed(range(8)):
            runs[g] = run
            run = run + a[g] * (l_ref[n, 9 * rf + g, here] - l_ref[n, 9 * rf + g + 1, here])
        below = _inclusive(run, lane, True) - run
        seen(rf, run)
        gain = ABSORB_RISE * light[rf, here]
        jump = jnp.where(above_bottom, a[7] - pltpu.roll(a[0], 120, 1), 0.0)
        push_end = jump * (k[7] + pltpu.roll(k[0], 120, 1))
        share_end = jump * (pltpu.roll(t[0], 120, 1) - t[7])
        push_before, share_before = pltpu.roll(push_end, 8, 1), pltpu.roll(share_end, 8, 1)
        for g in range(8):
            i = i0 + g
            if g < 7:
                jump = a[g] - a[g + 1]
                push, share = jump * (k[g] + k[g + 1]), jump * (t[g + 1] - t[g])
            else:
                push, share = jnp.where(above_bottom, push_end, 0.05 * a[7]), share_end
            if rf < 3:
                jump = a[g] - a_ref[i + 8, here]
                push_r, share_r = jump * (k[g] + k_ref[n, i + 8, here]), jump * (t_ref[n, i + 8, here] - t[g])
            else:
                push_r, share_r = last[g]
            grad_t = (push_before - push) + (before[g][0] - push_r)
            grad_k = (share_before + share) + (before[g][1] + share_r)
            jump_up = a[g] - a_ref[i, up]
            jump_down = a_ref[i, down] - a[g]
            grad_t = grad_t + (jump_down * (k_ref[n, i, down] + k[g]) - jump_up * (k[g] + k_ref[n, i, up]))
            grad_k = grad_k + (jump_down * (t[g] - t_ref[n, i, down]) + jump_up * (t_ref[n, i, up] - t[g]))
            heat = grad_t + c_ref[n, i, here] * grad_k
            absorbed = gain * (a[g] * l_ref[n, 9 * rf + g + 1, here] - (below + runs[g]))
            put(i, a[g] + (heat + r_ref[n, i, here] * (absorbed - heat)))
            push_before, share_before, before[g] = push, share, (push_r, share_r)


def backward(own, r1, r2, r3, t_ref, k_ref, c_ref, r_ref, l_ref, light, zid, a_ref, zpart, ab, total):
    _gather((own, r1, r2, r3), ab, SEED_HALO, SEED_WIDE)
    fields = (t_ref, k_ref, c_ref, r_ref, l_ref, light)
    total[...] = jnp.zeros(total.shape, F32)
    source, target = ab, a_ref
    for n in (3, 2, 1):
        _ghost(lambda i, c, ref=source: ref.at[i, pl.ds(BASE + c, 1)])

        def chunk(c, carry, n=n, source=source, target=target):
            tiles = _Tiles(BASE + SEED_HALO + 8 * c)

            def put(i, value):
                target[i, tiles.here] = value

            def seen(rf, value):
                total[rf, tiles.here] += value

            _retreat(n, tiles, source, *fields, put, seen)
            return carry

        lax.fori_loop(0, SEED_WIDE // 8, chunk, 0)
        source, target = target, source
    _ghost(lambda i, c, ref=source: ref.at[i, pl.ds(BASE + c, 1)])
    core = pl.ds(BASE + HALO, CORE)
    sums = []
    for rf in range(4):
        value = total[rf, core]
        for g in range(8):
            value = value + source[8 * rf + g, core] * (l_ref[0, 9 * rf + g, core] - l_ref[0, 9 * rf + g + 1, core])
        sums.append(value * DT)
    for z in range(NZONE):
        picked = [jnp.where(zid[rf] == float(z), sums[rf], 0.0) for rf in range(4)]
        zpart[z : z + 1] = jnp.sum((picked[0] + picked[1]) + (picked[2] + picked[3]), axis=0, keepdims=True)


def last_step(a_ref, t_ref, k_ref, c_ref, r_ref, l_ref, light, o0, o1, o2, o3):
    masks = _source_masks()

    def chunk(c, carry):
        tiles = _Tiles(BASE + HALO + 8 * c)
        values = [None] * 32

        def put(i, value):
            values[i] = value

        _retreat(0, tiles, a_ref, t_ref, k_ref, c_ref, r_ref, l_ref, light, put, lambda rf, value: None)
        for g in range(8):
            turned = [values[g]] + [pltpu.roll(values[8 * rf + g], 32 * rf, 1) for rf in (1, 2, 3)]
            for k, out in enumerate((o0, o1, o2, o3)):
                out[g, pl.ds(pl.multiple_of(8 * c, 8), 8)] = _pick(masks, k, turned)
        return carry

    lax.fori_loop(0, CORE // 8, chunk, 0)


def unpack(own, r1, r2, r3, out, buf):
    d = lax.axis_index("dep")
    for k, block in enumerate((own, r1, r2, r3)):
        start = pl.multiple_of(lax.rem(d + 4 - k, 4) * CORE, CORE)
        buf[:, pl.ds(start, CORE)] = block[...]
    for g in range(8):
        plain = buf[g].T
        for p in range(4):
            rf = lax.rem(p + 4 - d, 4)
            for sub in range(4):
                out[8 * sub + g, pl.ds(rf, 8, stride=4)] = plain[32 * p + 8 * sub : 32 * p + 8 * sub + 8]


def _around(x, k):
    return lax.ppermute(x, "dep", [(s, (s + k) % 4) for s in range(4)])


def _place(y, z, core, x):
    return ((y * 4 + z) * 2 + core) * 4 + x


def _meet(v, partner):
    pairs = []
    for y in range(4):
        for z in range(4):
            for core in range(2):
                for x in range(4):
                    pairs.append((_place(y, z, core, x), _place(*partner(y, z, core, x))))
    return v + lax.ppermute(v, ("lat", "dep"), pairs)


def total_of(v):
    for partner in (
        lambda y, z, core, x: (y, z, 1 - core, x),
        lambda y, z, core, x: (y, z ^ 1, core, x),
        lambda y, z, core, x: (y, 3 - z, core, x),
        lambda y, z, core, x: (y ^ 1, z, core, x),
        lambda y, z, core, x: (3 - y, z, core, x),
        lambda y, z, core, x: (y, z, core, x ^ 1),
        lambda y, z, core, x: (y, z, core, 3 - x),
    ):
        v = _meet(v, partner)
    return v


def _shape(*dims):
    return jax.ShapeDtypeStruct(dims, F32)


def _call(kernel, inputs, outs, scratch=(), spaces=None):
    return pl.pallas_call(
        kernel,
        out_shape=tuple(outs),
        in_specs=spaces or [_full()] * len(inputs),
        out_specs=(_full(),) * len(outs),
        scratch_shapes=list(scratch),
        compiler_params=_params(),
        name=kernel.__name__,
    )(*inputs)


def per_device(h, zones, fluence, seed):
    slab = _shape(8, 128, 128)
    edge = _shape(8, 16, 128)
    state, start, light, zid, to_right, to_left = _call(
        pack,
        (fluence, h, zones, seed),
        (slab, slab, _shape(4, 128, 128), _shape(4, CORE, 128), edge, edge),
        (
            _vmem(32, 32, 128),
            _vmem(32, 32, 128),
            pltpu.VMEM((32, 128), jnp.int32),
            _vmem(2, 32, 128),
            _vmem(128, 128),
            pltpu.SMEM((NZONE,), F32),
            pltpu.SemaphoreType.DMA((4,)),
        ),
        [_any()] * 4,
    )
    left = lax.ppermute(to_right, "lat", [(l, l + 1) for l in range(31)])
    right = lax.ppermute(to_left, "lat", [(l + 1, l) for l in range(31)])
    block, seed_block = _shape(8, WIDE, 128), _shape(8, SEED_WIDE, 128)
    h0, h1, h2, h3, s0, s1, s2, s3, light_own = _call(
        insert,
        (state, start, light, left, right),
        (block,) * 4 + (seed_block,) * 4 + (_shape(4, WIDE, 128),),
        (_vmem(8, 144, 128), _vmem(8, 136, 128), _vmem(144, 128)),
    )
    h2, h1, h3 = _around(h2, 2), _around(h1, 1), _around(h3, 3)
    s2, s1, s3 = _around(s2, 2), _around(s1, 1), _around(s3, 3)
    field = _vmem(4, 32, HIGH, 128)
    states = _call(
        forward,
        (h0, h1, h2, h3, light_own),
        (field,) * 4 + (_vmem(4, 36, HIGH, 128), _vmem(4, HIGH, 128)),
        [_vmem(32, HIGH, 128)] * 2,
    )
    a, zpart = _call(
        backward,
        (s0, s1, s2, s3, *states, zid),
        (_vmem(32, HIGH, 128), _shape(NZONE, 128)),
        (_vmem(32, HIGH, 128), _vmem(4, HIGH, 128)),
    )
    piece = _shape(8, CORE, 128)
    o0, o1, o2, o3 = _call(last_step, (a, *states), (piece,) * 4)
    o2, o1, o3 = _around(o2, 2), _around(o1, 1), _around(o3, 3)
    total = jnp.sum(total_of(zpart), axis=1)
    (out,) = _call(unpack, (o0, o1, o2, o3), (_shape(32, 32, 128),), (_vmem(8, 128, 128),))
    return out, total


def solution(mesh):
    in_specs = (P("dep", None, "lat"), P(None, "lat"), P(), P("dep", None, "lat"))
    out_specs = (P("dep", None, "lat"), P())
    return jax.shard_map(per_device, mesh=mesh, in_specs=in_specs, out_specs=out_specs, check_vma=False)
```

time: 458 us -> 88.7 us (0.19); the launches traced: 450 us -> 88.4 us
  blocking collectives: 203 us -> 0 us
  other arithmetic: 121 us -> 0.64 us
  Pallas kernels: 0 us -> 27.9 us
  starting transfers between devices: 59.7 us -> 33.9 us
  waiting for transfers between devices: 46.8 us -> 21.7 us
  local copies, waits for them, and re-layouts: 16.2 us -> 3.45 us
    all_gather x11 -> x0, blocking collectives: 131 us -> none  [entering(): gathered = lax.all_gather(part, axis)]
    psum x1 -> x0, blocking collectives: 72 us -> none  [per_device(): total = total + lax.psum(zone_part, ('lat', 'dep'))]
    another operation x19 -> x0, other arithmetic: 36.5 us -> none  [the longest x8 13.8 us: per_device(): both = paired_halo(jnp.stack([scaled, states[step]]))]
    mul x25 -> x0, other arithmetic: 35.5 us -> none  [the longest x12 24.3 us: heat_pullback(): masks[axis_orientation] * jump * 0.5]
    pallas_call x0 -> x6, Pallas kernels: none -> 27.9 us  [_call(): pl.pallas_call(kernel, out_shape=tuple(outs), in_specs=spaces or [_full()...]
    ppermute x28 -> x18, starting transfers between devices: 59.7 us -> 33.9 us  [the longest x7 16.1 us: _meet(): return v + lax.ppermute(v, ('lat', 'dep'), pairs)]
    ppermute x28 -> x18, waiting for transfers between devices: 46.8 us -> 21.7 us  [the longest x7 13.4 us: _meet(): return v + lax.ppermute(v, ('lat', 'dep'), pairs)]
    sub x4 -> x0, other arithmetic: 14.7 us -> none  [silicon_constants(): rise = jax.nn.sigmoid(lower) - jax.nn.sigmoid(upper)]
  transfers between devices with their start and end apart: 28 -> 18, of which waited for: 15 -> 9; matrix products, arithmetic and copies ran while one was open for 1% -> 1% of each run, Pallas kernels for 0% -> 18%
where the time goes in v2:
time: 88.7 us; the launch traced here: 88.4 us
  starting transfers between devices  33.9 us (38%)
  Pallas kernels  27.9 us (31%)
  waiting for transfers between devices  21.7 us (24%)
  local copies, waits for them, and re-layouts  3.45 us (4%)
    pallas_call x6, Pallas kernels, _call(): pl.pallas_call(kernel, out_shape=tuple(outs), in_specs=spaces or [_full()...  27.9 us
    ppermute x7, starting transfers between devices, _meet(): return v + lax.ppermute(v, ('lat', 'dep'), pairs)  16.1 us
    ppermute x9, starting transfers between devices, _around(): return lax.ppermute(x, 'dep', [(s, (s + k) % 4) for s in range(4)])  15.3 us
    ppermute x7, waiting for transfers between devices, _meet(): return v + lax.ppermute(v, ('lat', 'dep'), pairs)  13.4 us
    ppermute x9, waiting for transfers between devices, _around(): return lax.ppermute(x, 'dep', [(s, (s + k) % 4) for s in range(4)])  4.19 us
    ppermute x1, waiting for transfers between devices, per_device(): right = lax.ppermute(to_left, 'lat', [(l + 1, l) for l in range(31)])  4.07 us
    unnamed x8, local copies, waits for them, and re-layouts  3.45 us
  transfers between devices with their start and end apart: 18, of which 9 were waited for; matrix products, arithmetic and copies ran while one was open for 1% of the time, Pallas kernels for 18%

profile of v2, /device:TPU:0, one launch (start us, length us, event | category | flops | bytes accessed | tf_op | source)
XLA Modules:
  0.0 88.4 jit_solution(3076285529327046361)
XLA Ops:
  0.6 0.0 copy-start
  0.6 1.0 %copy-done = f32[32,32,128]{2,1,0:T(8,128)S(1)} copy-done((f32[32,32,128]{2,1,0:T(8,128)S(1)}, f32[32,32,128]{2,1,0:T(8,128)}, u32[]{:S(2)}) %copy-start) | copy-done | bytes 524312
  1.7 1.0 %copy-done.1 = f32[32,32,128]{2,1,0:T(8,128)S(1)} copy-done((f32[32,32,128]{2,1,0:T(8,128)S(1)}, f32[32,32,128]{2,1,0:T(8,128)}, u32[]{:S(2)}) %copy-start.1) | copy-done | bytes 524312
  2.7 0.7 copy-done.2
  3.4 0.7 copy-done.3
  4.1 1.1 %pack.1 = (f32[8,128,128]{2,1,0:T(8,128)S(1)}, f32[8,128,128]{2,1,0:T(8,128)S(1)}, f32[4,128,128]{2,1,0:T(8,128)S(1)}, f32[4,32,128]{2,1,0:T(8,128)S(1)}, f32[8,...) custom-call(f32[16]{0:T(128)S(1)} %copy-done.3, f32[32,32,128]{2,1,0:T(8,128)S(1)} %copy-done, s32[32,128]{1,0:T(8,128)S(1)} %copy-done.2, ...), custom_call_target="tpu_custom_call" | custom-call | tf_op jit(solution)/shard_map/pack/pallas_call | solution.py:438
  5.2 1.3 %collective-permute-start = (f32[8,16,128]{2,1,0:T(8,128)S(1)}, f32[8,16,128]{2,1,0:T(8,128)S(1)}, u32[]{:S(2)}, u32[]{:S(2)}) collective-permute-start(f32[8,16,128]{2,1,0:T(8,128)S(1)} %get-tuple-element.32), channel_id=1, source_target_pairs={{0,4},{4,8},{8,12},{12,16},{16,20},{20,24},{24,28},{28,32},{32,36}... | collective-permute-start | bytes 196616 | tf_op jit(solution)/shard_map/ppermute | solution.py:467
  6.5 1.3 %collective-permute-start.1 = (f32[8,16,128]{2,1,0:T(8,128)S(1)}, f32[8,16,128]{2,1,0:T(8,128)S(1)}, u32[]{:S(2)}, u32[]{:S(2)}) collective-permute-start(f32[8,16,128]{2,1,0:T(8,128)S(1)} %get-tuple-element.33), channel_id=1, source_target_pairs={{4,0},{8,4},{12,8},{16,12},{20,16},{24,20},{28,24},{32,28},{36,32}... | collective-permute-start | bytes 196616 | tf_op jit(solution)/shard_map/ppermute | solution.py:468
  7.8 0.0 collective-permute-done.left
  7.8 4.1 %collective-permute-done.1.right = f32[8,16,128]{2,1,0:T(8,128)S(1)} collective-permute-done((f32[8,16,128]{2,1,0:T(8,128)S(1)}, f32[8,16,128]{2,1,0:T(8,128)S(1)}, u32[]{:S(2)}, u32[]{:S(2)}) %collective-permute-start.1) | collective-permute-done | bytes 65568 | tf_op jit(solution)/shard_map/ppermute | solution.py:468
  11.8 0.2 insert.1
  12.1 1.6 %collective-permute-start.5 = (f32[8,48,128]{2,1,0:T(8,128)S(1)}, f32[8,48,128]{2,1,0:T(8,128)S(1)}, u32[]{:S(2)}, u32[]{:S(2)}) collective-permute-start(f32[8,48,128]{2,1,0:T(8,128)S(1)} %get-tuple-element.39), channel_id=1, source_target_pairs={{0,1},{1,2},{2,3},{3,0},{4,5},{5,6},{6,7},{7,4},{8,9},{9,10},{10,1... | collective-permute-start | bytes 589832 | tf_op jit(solution)/shard_map/ppermute | solution.py:402
  13.6 2.7 %collective-permute-start.6 = (f32[8,48,128]{2,1,0:T(8,128)S(1)}, f32[8,48,128]{2,1,0:T(8,128)S(1)}, u32[]{:S(2)}, u32[]{:S(2)}) collective-permute-start(f32[8,48,128]{2,1,0:T(8,128)S(1)} %get-tuple-element.40), channel_id=1, source_target_pairs={{0,2},{1,3},{2,0},{3,1},{4,6},{5,7},{6,4},{7,5},{8,10},{9,11},{10,... | collective-permute-start | bytes 589832 | tf_op jit(solution)/shard_map/ppermute | solution.py:402
  16.4 1.4 %collective-permute-start.7 = (f32[8,48,128]{2,1,0:T(8,128)S(1)}, f32[8,48,128]{2,1,0:T(8,128)S(1)}, u32[]{:S(2)}, u32[]{:S(2)}) collective-permute-start(f32[8,48,128]{2,1,0:T(8,128)S(1)} %get-tuple-element.41), channel_id=1, source_target_pairs={{0,3},{1,0},{2,1},{3,2},{4,7},{5,4},{6,5},{7,6},{8,11},{9,8},{10,9... | collective-permute-start | bytes 589832 | tf_op jit(solution)/shard_map/ppermute | solution.py:402
  17.8 0.6 collective-permute-start.2
  18.4 0.9 collective-permute-start.3
  19.3 0.0 collective-permute-done.5.r1
  19.3 1.8 %collective-permute-start.4 = (f32[8,40,128]{2,1,0:T(8,128)S(1)}, f32[8,40,128]{2,1,0:T(8,128)S(1)}, u32[]{:S(2)}, u32[]{:S(2)}) collective-permute-start(f32[8,40,128]{2,1,0:T(8,128)S(1)} %get-tuple-element.37), channel_id=1, source_target_pairs={{0,3},{1,0},{2,1},{3,2},{4,7},{5,4},{6,5},{7,6},{8,11},{9,8},{10,9... | collective-permute-start | bytes 491528 | tf_op jit(solution)/shard_map/ppermute | solution.py:402
  21.1 3.3 %collective-permute-done.6.r2 = f32[8,48,128]{2,1,0:T(8,128)S(1)} collective-permute-done((f32[8,48,128]{2,1,0:T(8,128)S(1)}, f32[8,48,128]{2,1,0:T(8,128)S(1)}, u32[]{:S(2)}, u32[]{:S(2)}) %collective-permute-start.6) | collective-permute-done | bytes 196640 | tf_op jit(solution)/shard_map/ppermute | solution.py:402
  24.4 0.9 collective-permute-done.7.r3
  25.2 14.2 %forward.1 = (f32[4,32,64,128]{3,2,1,0:T(8,128)S(1)}, f32[4,32,64,128]{3,2,1,0:T(8,128)S(1)}, f32[4,32,64,128]{3,2,1,0:T(8,128)S(1)}, f32[4,32,64,128]{3,2,1,0:T...) custom-call(f32[8,48,128]{2,1,0:T(8,128)S(1)} %get-tuple-element.38.own, ...), custom_call_target="tpu_custom_call" | custom-call | tf_op jit(solution)/shard_map/forward/pallas_call | solution.py:438
  39.4 0.0 collective-permute-done.2.r1
  39.4 0.0 collective-permute-done.3.r2
  39.5 0.0 collective-permute-done.4.r3
  39.5 9.4 %backward.1 = (f32[32,64,128]{2,1,0:T(8,128)S(1)}, f32[16,128]{1,0:T(8,128)S(1)}) custom-call(f32[8,40,128]{2,1,0:T(8,128)S(1)} %get-tuple-element.34.own, f32[8,40,128]{2,1,0:T(8,128)S(1)} %collective-permute-done.2.r1, f32[8,40,128]{2,1,0:T(8,128)S(1)} %collective-permute-done.3.r2, f32[8,40,128]{2,1,0:T(8,128)S(1)} %collective-permute-done.4.r3, ...), custom_call_target="tpu_custom_call" | custom-call | tf_op jit(solution)/shard_map/backward/pallas_call | solution.py:438
  48.8 3.2 %collective-permute-start.11 = (f32[16,128]{1,0:T(8,128)S(1)}, f32[16,128]{1,0:T(8,128)S(1)}, u32[]{:S(2)}, u32[]{:S(2)}) collective-permute-start(f32[16,128]{1,0:T(8,128)S(1)} %get-tuple-element.55), channel_id=1, source_target_pairs={{0,4},{1,5},{2,6},{3,7},{4,0},{5,1},{6,2},{7,3},{8,12},{9,13},{10,... | collective-permute-start | bytes 24584 | tf_op jit(solution)/shard_map/ppermute | solution.py:416
  52.0 0.8 collective-permute-done.11
  52.9 1.6 %collective-permute-start.12 = (f32[16,128]{1,0:T(8,128)S(1)}, f32[16,128]{1,0:T(8,128)S(1)}, u32[]{:S(2)}, u32[]{:S(2)}) collective-permute-start(f32[16,128]{1,0:T(8,128)S(1)} %add.21), channel_id=1, source_target_pairs={{0,8},{1,9},{2,10},{3,11},{4,12},{5,13},{6,14},{7,15},{8,0},{9,1},... | collective-permute-start | bytes 24584 | tf_op jit(solution)/shard_map/ppermute | solution.py:416
  54.5 2.0 %collective-permute-done.12 = f32[16,128]{1,0:T(8,128)S(1)} collective-permute-done((f32[16,128]{1,0:T(8,128)S(1)}, f32[16,128]{1,0:T(8,128)S(1)}, u32[]{:S(2)}, u32[]{:S(2)}) %collective-permute-start.12) | collective-permute-done | bytes 8224 | tf_op jit(solution)/shard_map/ppermute | solution.py:416
  56.5 4.2 %collective-permute-start.13 = (f32[16,128]{1,0:T(8,128)S(1)}, f32[16,128]{1,0:T(8,128)S(1)}, u32[]{:S(2)}, u32[]{:S(2)}) collective-permute-start(f32[16,128]{1,0:T(8,128)S(1)} %add.22), channel_id=1, source_target_pairs={{0,24},{1,25},{2,26},{3,27},{4,28},{5,29},{6,30},{7,31},{8,16},{9,... | collective-permute-start | bytes 24584 | tf_op jit(solution)/shard_map/ppermute | solution.py:416
  60.7 1.6 %collective-permute-done.13 = f32[16,128]{1,0:T(8,128)S(1)} collective-permute-done((f32[16,128]{1,0:T(8,128)S(1)}, f32[16,128]{1,0:T(8,128)S(1)}, u32[]{:S(2)}, u32[]{:S(2)}) %collective-permute-start.13) | collective-permute-done | bytes 8224 | tf_op jit(solution)/shard_map/ppermute | solution.py:416
  62.3 1.8 %collective-permute-start.14 = (f32[16,128]{1,0:T(8,128)S(1)}, f32[16,128]{1,0:T(8,128)S(1)}, u32[]{:S(2)}, u32[]{:S(2)}) collective-permute-start(f32[16,128]{1,0:T(8,128)S(1)} %add.23), channel_id=1, source_target_pairs={{0,32},{1,33},{2,34},{3,35},{4,36},{5,37},{6,38},{7,39},{8,40},{9,... | collective-permute-start | bytes 24584 | tf_op jit(solution)/shard_map/ppermute | solution.py:416
  64.2 1.8 %collective-permute-done.14 = f32[16,128]{1,0:T(8,128)S(1)} collective-permute-done((f32[16,128]{1,0:T(8,128)S(1)}, f32[16,128]{1,0:T(8,128)S(1)}, u32[]{:S(2)}, u32[]{:S(2)}) %collective-permute-start.14) | collective-permute-done | bytes 8224 | tf_op jit(solution)/shard_map/ppermute | solution.py:416
  66.0 3.3 %collective-permute-start.15 = (f32[16,128]{1,0:T(8,128)S(1)}, f32[16,128]{1,0:T(8,128)S(1)}, u32[]{:S(2)}, u32[]{:S(2)}) collective-permute-start(f32[16,128]{1,0:T(8,128)S(1)} %add.24), channel_id=1, source_target_pairs={{0,96},{1,97},{2,98},{3,99},{4,100},{5,101},{6,102},{7,103},{8,104... | collective-permute-start | bytes 24584 | tf_op jit(solution)/shard_map/ppermute | solution.py:416
  69.3 2.0 %last_step.1 = (f32[8,32,128]{2,1,0:T(8,128)S(1)}, f32[8,32,128]{2,1,0:T(8,128)S(1)}, f32[8,32,128]{2,1,0:T(8,128)S(1)}, f32[8,32,128]{2,1,0:T(8,128)S(1)}) custom-call(f32[32,64,128]{2,1,0:T(8,128)S(1)} %get-tuple-element.50.a_ref, f32[4,32,64,128]{3,2,1,0:T(8,128)S(1)} %get-tuple-element.43.t_ref, f32[4,32,64,128]{3,2,1,0:T(8,128)S(1)} %get-tuple-element.44.k_ref, ...), custom_call_target="tpu_custom_call" | custom-call | tf_op jit(solution)/shard_map/last_step/pallas_call | solution.py:438
  71.3 3.5 %collective-permute-start.8 = (f32[8,32,128]{2,1,0:T(8,128)S(1)}, f32[8,32,128]{2,1,0:T(8,128)S(1)}, u32[]{:S(2)}, u32[]{:S(2)}) collective-permute-start(f32[8,32,128]{2,1,0:T(8,128)S(1)} %get-tuple-element.52), channel_id=1, source_target_pairs={{0,1},{1,2},{2,3},{3,0},{4,5},{5,6},{6,7},{7,4},{8,9},{9,10},{10,1... | collective-permute-start | bytes 393224 | tf_op jit(solution)/shard_map/ppermute | solution.py:402
  74.8 1.9 %collective-permute-start.9 = (f32[8,32,128]{2,1,0:T(8,128)S(1)}, f32[8,32,128]{2,1,0:T(8,128)S(1)}, u32[]{:S(2)}, u32[]{:S(2)}) collective-permute-start(f32[8,32,128]{2,1,0:T(8,128)S(1)} %get-tuple-element.53), channel_id=1, source_target_pairs={{0,2},{1,3},{2,0},{3,1},{4,6},{5,7},{6,4},{7,5},{8,10},{9,11},{10,... | collective-permute-start | bytes 393224 | tf_op jit(solution)/shard_map/ppermute | solution.py:402
  76.7 0.8 collective-permute-start.10
  77.6 0.0 collective-permute-done.15
  77.6 1.2 %collective-permute-start.16 = (f32[16,128]{1,0:T(8,128)S(1)}, f32[16,128]{1,0:T(8,128)S(1)}, u32[]{:S(2)}, u32[]{:S(2)}) collective-permute-start(f32[16,128]{1,0:T(8,128)S(1)} %add.25), channel_id=1, source_target_pairs={{0,1},{1,0},{2,3},{3,2},{4,5},{5,4},{6,7},{7,6},{8,9},{9,8},{10,11... | collective-permute-start | bytes 24584 | tf_op jit(solution)/shard_map/ppermute | solution.py:416
  78.8 3.0 %collective-permute-done.16 = f32[16,128]{1,0:T(8,128)S(1)} collective-permute-done((f32[16,128]{1,0:T(8,128)S(1)}, f32[16,128]{1,0:T(8,128)S(1)}, u32[]{:S(2)}, u32[]{:S(2)}) %collective-permute-start.16) | collective-permute-done | bytes 8224 | tf_op jit(solution)/shard_map/ppermute | solution.py:416
  81.8 0.8 collective-permute-start.17
  82.6 4.1 %collective-permute-done.17 = f32[16,128]{1,0:T(8,128)S(1)} collective-permute-done((f32[16,128]{1,0:T(8,128)S(1)}, f32[16,128]{1,0:T(8,128)S(1)}, u32[]{:S(2)}, u32[]{:S(2)}) %collective-permute-start.17) | collective-permute-done | bytes 8224 | tf_op jit(solution)/shard_map/ppermute | solution.py:416
  86.7 0.6 add_reduce_fusion
  87.3 0.0 collective-permute-done.8.r1
  87.3 0.0 collective-permute-done.9.r2
  87.3 0.0 collective-permute-done.10.r3
  87.3 1.0 %unpack.1 = f32[32,32,128]{2,1,0:T(8,128)} custom-call(f32[8,32,128]{2,1,0:T(8,128)S(1)} %get-tuple-element.51.own, f32[8,32,128]{2,1,0:T(8,128)S(1)} %collective-permute-done.8.r1, f32[8,32,128]{2,1,0:T(8,128)S(1)} %collective-permute-done.9.r2, f32[8,32,128]{2,1,0:T(8,128)S(1)} %collective-permute-done.10.r3), custom_call_target="tpu_custom_call" | custom-call | tf_op jit(solution)/shard_map/unpack/pallas_call | solution.py:438
  (9 shorter events, 0.0 us)
Async XLA Ops:
  0.6 1.0 %copy-start = (f32[32,32,128]{2,1,0:T(8,128)S(1)}, f32[32,32,128]{2,1,0:T(8,128)}, u32[]{:S(2)}) copy-start(f32[32,32,128]{2,1,0:T(8,128)} %h_in.1) | copy-start | bytes 1572868
  1.7 1.0 %copy-start.1 = (f32[32,32,128]{2,1,0:T(8,128)S(1)}, f32[32,32,128]{2,1,0:T(8,128)}, u32[]{:S(2)}) copy-start(f32[32,32,128]{2,1,0:T(8,128)} %a_in.1) | copy-start | bytes 1572868
  2.7 0.7 copy-start.2
  3.4 0.7 copy-start.3
  5.2 2.6 %collective-permute-start = (f32[8,16,128]{2,1,0:T(8,128)S(1)}, f32[8,16,128]{2,1,0:T(8,128)S(1)}, u32[]{:S(2)}, u32[]{:S(2)}) collective-permute-start(f32[8,16,128]{2,1,0:T(8,128)S(1)} %get-tuple-element.32), channel_id=1, source_target_pairs={{0,4},{4,8},{8,12},{12,16},{16,20},{20,24},{24,28},{28,32},{32,36}... | collective-permute-start | bytes 196616 | tf_op jit(solution)/shard_map/ppermute | solution.py:467
  6.5 5.4 %collective-permute-start.1 = (f32[8,16,128]{2,1,0:T(8,128)S(1)}, f32[8,16,128]{2,1,0:T(8,128)S(1)}, u32[]{:S(2)}, u32[]{:S(2)}) collective-permute-start(f32[8,16,128]{2,1,0:T(8,128)S(1)} %get-tuple-element.33), channel_id=1, source_target_pairs={{4,0},{8,4},{12,8},{16,12},{20,16},{24,20},{28,24},{32,28},{36,32}... | collective-permute-start | bytes 196616 | tf_op jit(solution)/shard_map/ppermute | solution.py:468
  12.1 7.2 %collective-permute-start.5 = (f32[8,48,128]{2,1,0:T(8,128)S(1)}, f32[8,48,128]{2,1,0:T(8,128)S(1)}, u32[]{:S(2)}, u32[]{:S(2)}) collective-permute-start(f32[8,48,128]{2,1,0:T(8,128)S(1)} %get-tuple-element.39), channel_id=1, source_target_pairs={{0,1},{1,2},{2,3},{3,0},{4,5},{5,6},{6,7},{7,4},{8,9},{9,10},{10,1... | collective-permute-start | bytes 589832 | tf_op jit(solution)/shard_map/ppermute | solution.py:402
  13.6 10.8 %collective-permute-start.6 = (f32[8,48,128]{2,1,0:T(8,128)S(1)}, f32[8,48,128]{2,1,0:T(8,128)S(1)}, u32[]{:S(2)}, u32[]{:S(2)}) collective-permute-start(f32[8,48,128]{2,1,0:T(8,128)S(1)} %get-tuple-element.40), channel_id=1, source_target_pairs={{0,2},{1,3},{2,0},{3,1},{4,6},{5,7},{6,4},{7,5},{8,10},{9,11},{10,... | collective-permute-start | bytes 589832 | tf_op jit(solution)/shard_map/ppermute | solution.py:402
  16.4 8.9 %collective-permute-start.7 = (f32[8,48,128]{2,1,0:T(8,128)S(1)}, f32[8,48,128]{2,1,0:T(8,128)S(1)}, u32[]{:S(2)}, u32[]{:S(2)}) collective-permute-start(f32[8,48,128]{2,1,0:T(8,128)S(1)} %get-tuple-element.41), channel_id=1, source_target_pairs={{0,3},{1,0},{2,1},{3,2},{4,7},{5,4},{6,5},{7,6},{8,11},{9,8},{10,9... | collective-permute-start | bytes 589832 | tf_op jit(solution)/shard_map/ppermute | solution.py:402
  17.8 21.7 %collective-permute-start.2 = (f32[8,40,128]{2,1,0:T(8,128)S(1)}, f32[8,40,128]{2,1,0:T(8,128)S(1)}, u32[]{:S(2)}, u32[]{:S(2)}) collective-permute-start(f32[8,40,128]{2,1,0:T(8,128)S(1)} %get-tuple-element.35), channel_id=1, source_target_pairs={{0,1},{1,2},{2,3},{3,0},{4,5},{5,6},{6,7},{7,4},{8,9},{9,10},{10,1... | collective-permute-start | bytes 491528 | tf_op jit(solution)/shard_map/ppermute | solution.py:402
  18.4 21.1 %collective-permute-start.3 = (f32[8,40,128]{2,1,0:T(8,128)S(1)}, f32[8,40,128]{2,1,0:T(8,128)S(1)}, u32[]{:S(2)}, u32[]{:S(2)}) collective-permute-start(f32[8,40,128]{2,1,0:T(8,128)S(1)} %get-tuple-element.36), channel_id=1, source_target_pairs={{0,2},{1,3},{2,0},{3,1},{4,6},{5,7},{6,4},{7,5},{8,10},{9,11},{10,... | collective-permute-start | bytes 491528 | tf_op jit(solution)/shard_map/ppermute | solution.py:402
  19.3 20.2 %collective-permute-start.4 = (f32[8,40,128]{2,1,0:T(8,128)S(1)}, f32[8,40,128]{2,1,0:T(8,128)S(1)}, u32[]{:S(2)}, u32[]{:S(2)}) collective-permute-start(f32[8,40,128]{2,1,0:T(8,128)S(1)} %get-tuple-element.37), channel_id=1, source_target_pairs={{0,3},{1,0},{2,1},{3,2},{4,7},{5,4},{6,5},{7,6},{8,11},{9,8},{10,9... | collective-permute-start | bytes 491528 | tf_op jit(solution)/shard_map/ppermute | solution.py:402
  48.8 4.0 %collective-permute-start.11 = (f32[16,128]{1,0:T(8,128)S(1)}, f32[16,128]{1,0:T(8,128)S(1)}, u32[]{:S(2)}, u32[]{:S(2)}) collective-permute-start(f32[16,128]{1,0:T(8,128)S(1)} %get-tuple-element.55), channel_id=1, source_target_pairs={{0,4},{1,5},{2,6},{3,7},{4,0},{5,1},{6,2},{7,3},{8,12},{9,13},{10,... | collective-permute-start | bytes 24584 | tf_op jit(solution)/shard_map/ppermute | solution.py:416
  52.9 3.7 %collective-permute-start.12 = (f32[16,128]{1,0:T(8,128)S(1)}, f32[16,128]{1,0:T(8,128)S(1)}, u32[]{:S(2)}, u32[]{:S(2)}) collective-permute-start(f32[16,128]{1,0:T(8,128)S(1)} %add.21), channel_id=1, source_target_pairs={{0,8},{1,9},{2,10},{3,11},{4,12},{5,13},{6,14},{7,15},{8,0},{9,1},... | collective-permute-start | bytes 24584 | tf_op jit(solution)/shard_map/ppermute | solution.py:416
  56.5 5.8 %collective-permute-start.13 = (f32[16,128]{1,0:T(8,128)S(1)}, f32[16,128]{1,0:T(8,128)S(1)}, u32[]{:S(2)}, u32[]{:S(2)}) collective-permute-start(f32[16,128]{1,0:T(8,128)S(1)} %add.22), channel_id=1, source_target_pairs={{0,24},{1,25},{2,26},{3,27},{4,28},{5,29},{6,30},{7,31},{8,16},{9,... | collective-permute-start | bytes 24584 | tf_op jit(solution)/shard_map/ppermute | solution.py:416
  62.3 3.7 %collective-permute-start.14 = (f32[16,128]{1,0:T(8,128)S(1)}, f32[16,128]{1,0:T(8,128)S(1)}, u32[]{:S(2)}, u32[]{:S(2)}) collective-permute-start(f32[16,128]{1,0:T(8,128)S(1)} %add.23), channel_id=1, source_target_pairs={{0,32},{1,33},{2,34},{3,35},{4,36},{5,37},{6,38},{7,39},{8,40},{9,... | collective-permute-start | bytes 24584 | tf_op jit(solution)/shard_map/ppermute | solution.py:416
  66.0 11.6 %collective-permute-start.15 = (f32[16,128]{1,0:T(8,128)S(1)}, f32[16,128]{1,0:T(8,128)S(1)}, u32[]{:S(2)}, u32[]{:S(2)}) collective-permute-start(f32[16,128]{1,0:T(8,128)S(1)} %add.24), channel_id=1, source_target_pairs={{0,96},{1,97},{2,98},{3,99},{4,100},{5,101},{6,102},{7,103},{8,104... | collective-permute-start | bytes 24584 | tf_op jit(solution)/shard_map/ppermute | solution.py:416
  71.3 16.0 %collective-permute-start.8 = (f32[8,32,128]{2,1,0:T(8,128)S(1)}, f32[8,32,128]{2,1,0:T(8,128)S(1)}, u32[]{:S(2)}, u32[]{:S(2)}) collective-permute-start(f32[8,32,128]{2,1,0:T(8,128)S(1)} %get-tuple-element.52), channel_id=1, source_target_pairs={{0,1},{1,2},{2,3},{3,0},{4,5},{5,6},{6,7},{7,4},{8,9},{9,10},{10,1... | collective-permute-start | bytes 393224 | tf_op jit(solution)/shard_map/ppermute | solution.py:402
  74.8 12.5 %collective-permute-start.9 = (f32[8,32,128]{2,1,0:T(8,128)S(1)}, f32[8,32,128]{2,1,0:T(8,128)S(1)}, u32[]{:S(2)}, u32[]{:S(2)}) collective-permute-start(f32[8,32,128]{2,1,0:T(8,128)S(1)} %get-tuple-element.53), channel_id=1, source_target_pairs={{0,2},{1,3},{2,0},{3,1},{4,6},{5,7},{6,4},{7,5},{8,10},{9,11},{10,... | collective-permute-start | bytes 393224 | tf_op jit(solution)/shard_map/ppermute | solution.py:402
  76.7 10.6 %collective-permute-start.10 = (f32[8,32,128]{2,1,0:T(8,128)S(1)}, f32[8,32,128]{2,1,0:T(8,128)S(1)}, u32[]{:S(2)}, u32[]{:S(2)}) collective-permute-start(f32[8,32,128]{2,1,0:T(8,128)S(1)} %get-tuple-element.54), channel_id=1, source_target_pairs={{0,3},{1,0},{2,1},{3,2},{4,7},{5,4},{6,5},{7,6},{8,11},{9,8},{10,9... | collective-permute-start | bytes 393224 | tf_op jit(solution)/shard_map/ppermute | solution.py:402
  77.6 4.2 %collective-permute-start.16 = (f32[16,128]{1,0:T(8,128)S(1)}, f32[16,128]{1,0:T(8,128)S(1)}, u32[]{:S(2)}, u32[]{:S(2)}) collective-permute-start(f32[16,128]{1,0:T(8,128)S(1)} %add.25), channel_id=1, source_target_pairs={{0,1},{1,0},{2,3},{3,2},{4,5},{5,4},{6,7},{7,6},{8,9},{9,8},{10,11... | collective-permute-start | bytes 24584 | tf_op jit(solution)/shard_map/ppermute | solution.py:416
  81.8 4.9 %collective-permute-start.17 = (f32[16,128]{1,0:T(8,128)S(1)}, f32[16,128]{1,0:T(8,128)S(1)}, u32[]{:S(2)}, u32[]{:S(2)}) collective-permute-start(f32[16,128]{1,0:T(8,128)S(1)} %add.26), channel_id=1, source_target_pairs={{0,3},{1,2},{2,1},{3,0},{4,7},{5,6},{6,5},{7,4},{8,11},{9,10},{10,... | collective-permute-start | bytes 24584 | tf_op jit(solution)/shard_map/ppermute | solution.py:416

commit v3 on v2

--- a/solution.py
+++ b/solution.py
@@ -9,6 +9,7 @@
 
 
 NZONE = 16
+CP, CF, CF2, CB, CL, UNROLL = 48, 48, 40, 40, 32, False
 CORE = 32
 HALO = 8
 WIDE = CORE + 2 * HALO
@@ -37,11 +38,21 @@
 
 
 def _any():
-    return pl.BlockSpec(memory_space=pl.ANY)
-
-
-def _lanes():
-    return lax.broadcasted_iota(jnp.int32, (8, 128), 1)
+    return pl.BlockSpec(memory_space=pltpu.HBM)
+
+
+def _lanes(rows=8):
+    return lax.broadcasted_iota(jnp.int32, (rows, 128), 1)
+
+
+def _chunks(count, size, unrolled, body):
+    if count == size:
+        body(0)
+    elif unrolled:
+        for c in range(count // size):
+            body(c)
+    else:
+        lax.fori_loop(0, count // size, lambda c, carry: (body(c), carry)[1], 0)
 
 
 def _packed(ref, g, d):
@@ -56,8 +67,9 @@
     return jnp.concatenate([ref[pl.ds(rf, 8, stride=4)]] * 16, axis=0).T
 
 
-def pack(fluence_in, h_in, zones_in, a_in, state, seed, light, zid, to_right, to_left, h, a, zones, flat, zbuf, fluence, sems):
+def pack(fluence_in, h_in, zones_in, a_in, state, seed, light, zid, to_inner, to_outer, edges, h, a, zones, flat, zbuf, fluence, sems):
     d = lax.axis_index("dep")
+    to_left, to_right = edges.at[0], edges.at[1]
     copies = [
         pltpu.make_async_copy(source, target, sems.at[k])
         for k, (source, target) in enumerate(((h_in, h), (zones_in, zones), (fluence_in, fluence), (a_in, a)))
@@ -93,9 +105,16 @@
         seed[g] = packed
         to_left[g, 8:12] = packed[0:4]
         to_right[g, 8:12] = packed[124:128]
-
-
-def insert(state, seed, light, left, right, h0, h1, h2, h3, s0, s1, s2, s3, light_own, hbuf, sbuf, lbuf):
+    odd = lax.rem(lax.axis_index("lat"), 2)
+    to_inner[...] = edges[1 - odd]
+    to_outer[...] = edges[odd]
+
+
+def insert(state, seed, light, inner, outer, h0, h1, h2, h3, s0, s1, s2, s3, light_own, sides, hbuf, sbuf, lbuf):
+    odd = lax.rem(lax.axis_index("lat"), 2)
+    sides[odd] = outer[...]
+    sides[1 - odd] = inner[...]
+    right, left = sides.at[1], sides.at[0]
     d = lax.axis_index("dep")
     hbuf[:, 0:8] = left[:, 0:8]
     hbuf[:, 8:136] = state[...]
@@ -119,7 +138,7 @@
 
 
 def _source_masks():
-    part = lax.rem(_lanes() // 32 + 4 - lax.axis_index("dep"), 4)
+    part = lax.rem(_lanes(8) // 32 + 4 - lax.axis_index("dep"), 4)
     return [part == j for j in range(4)]
 
 
@@ -146,8 +165,9 @@
 
 
 class _Tiles:
-    def __init__(self, row):
-        self.here, self.up, self.down = pl.ds(row, 8), pl.ds(row + 1, 8), pl.ds(row - 1, 8)
+    def __init__(self, row, rows):
+        self.rows = rows
+        self.here, self.up, self.down = pl.ds(row, rows), pl.ds(row + 1, rows), pl.ds(row - 1, rows)
 
 
 def _inclusive(total, lane, reverse):
@@ -160,9 +180,9 @@
 
 
 def _properties(n, rf, tiles, states, t_ref, k_ref, c_ref, r_ref, l_ref):
-    lane = _lanes()
+    lane = _lanes(tiles.rows)
     here = tiles.here
-    run = jnp.zeros((8, 128), F32)
+    run = jnp.zeros((tiles.rows, 128), F32)
     runs = []
     for g in range(8):
         i = 8 * rf + g
@@ -187,7 +207,7 @@
 
 
 def _advance(n, tiles, h_ref, t_ref, k_ref, l_ref, light, then):
-    lane = _lanes()
+    lane = _lanes(tiles.rows)
     inside = lax.rem(lane, 8) < 7
     above_bottom = lane < 120
     here, up, down = tiles.here, tiles.up, tiles.down
@@ -247,20 +267,21 @@
         light[rf, BASE : BASE + WIDE] = light_own[rf]
     fields = (t_ref, k_ref, c_ref, r_ref, l_ref)
 
-    def start(c, carry):
-        tiles = _Tiles(BASE + 8 * c)
+    def start(c):
+        tiles = _Tiles(BASE + CP * c, CP)
         for rf in range(4):
             _properties(0, rf, tiles, [ha[8 * rf + g, tiles.here] for g in range(8)], *fields)
-        return carry
-
-    lax.fori_loop(0, WIDE // 8, start, 0)
+
+    _chunks(WIDE, CP, UNROLL, start)
     source, target = ha, hb
     for n in range(3):
         _ghost(lambda i, c, n=n: t_ref.at[n, i, pl.ds(BASE + c, 1)])
         first, count = (0, WIDE) if n < 2 else (SEED_HALO, SEED_WIDE)
 
-        def chunk(c, carry, n=n, first=first, source=source, target=target):
-            tiles = _Tiles(BASE + first + 8 * c)
+        size = CF if n < 2 else CF2
+
+        def chunk(c, n=n, first=first, source=source, target=target, size=size):
+            tiles = _Tiles(BASE + first + size * c, size)
 
             def then(rf, new):
                 for g in range(8):
@@ -269,14 +290,13 @@
                 _properties(n + 1, rf, tiles, new, *fields)
 
             _advance(n, tiles, source, t_ref, k_ref, l_ref, light, then)
-            return carry
-
-        lax.fori_loop(0, count // 8, chunk, 0)
+
+        _chunks(count, size, UNROLL, chunk)
         source, target = target, source
 
 
 def _retreat(n, tiles, a_ref, t_ref, k_ref, c_ref, r_ref, l_ref, light, put, seen):
-    lane = _lanes()
+    lane = _lanes(tiles.rows)
     inside = lax.rem(lane, 8) < 7
     above_bottom = lane < 120
     here, up, down = tiles.here, tiles.up, tiles.down
@@ -294,7 +314,7 @@
         a = [a_ref[i0 + g, here] for g in range(8)]
         t = [t_ref[n, i0 + g, here] for g in range(8)]
         k = [k_ref[n, i0 + g, here] for g in range(8)]
-        run = jnp.zeros((8, 128), F32)
+        run = jnp.zeros((tiles.rows, 128), F32)
         runs = [None] * 8
         for g in reversed(range(8)):
             runs[g] = run
@@ -338,8 +358,8 @@
     for n in (3, 2, 1):
         _ghost(lambda i, c, ref=source: ref.at[i, pl.ds(BASE + c, 1)])
 
-        def chunk(c, carry, n=n, source=source, target=target):
-            tiles = _Tiles(BASE + SEED_HALO + 8 * c)
+        def chunk(c, n=n, source=source, target=target):
+            tiles = _Tiles(BASE + SEED_HALO + CB * c, CB)
 
             def put(i, value):
                 target[i, tiles.here] = value
@@ -348,9 +368,8 @@
                 total[rf, tiles.here] += value
 
             _retreat(n, tiles, source, *fields, put, seen)
-            return carry
-
-        lax.fori_loop(0, SEED_WIDE // 8, chunk, 0)
+
+        _chunks(SEED_WIDE, CB, UNROLL, chunk)
         source, target = target, source
     _ghost(lambda i, c, ref=source: ref.at[i, pl.ds(BASE + c, 1)])
     core = pl.ds(BASE + HALO, CORE)
@@ -360,16 +379,19 @@
         for g in range(8):
             value = value + source[8 * rf + g, core] * (l_ref[0, 9 * rf + g, core] - l_ref[0, 9 * rf + g + 1, core])
         sums.append(value * DT)
+    rows = []
     for z in range(NZONE):
         picked = [jnp.where(zid[rf] == float(z), sums[rf], 0.0) for rf in range(4)]
-        zpart[z : z + 1] = jnp.sum((picked[0] + picked[1]) + (picked[2] + picked[3]), axis=0, keepdims=True)
+        rows.append(jnp.sum((picked[0] + picked[1]) + (picked[2] + picked[3]), axis=0, keepdims=True))
+    spread = jnp.concatenate(rows + [jnp.zeros((128 - NZONE, 128), F32)], axis=0)
+    zpart[...] = jnp.sum(spread.T, axis=0, keepdims=True)
 
 
 def last_step(a_ref, t_ref, k_ref, c_ref, r_ref, l_ref, light, o0, o1, o2, o3):
-    masks = _source_masks()
-
-    def chunk(c, carry):
-        tiles = _Tiles(BASE + HALO + 8 * c)
+    masks = [jnp.broadcast_to(m[0:1], (CL, 128)) for m in _source_masks()]
+
+    def chunk(c):
+        tiles = _Tiles(BASE + HALO + CL * c, CL)
         values = [None] * 32
 
         def put(i, value):
@@ -379,13 +401,12 @@
         for g in range(8):
             turned = [values[g]] + [pltpu.roll(values[8 * rf + g], 32 * rf, 1) for rf in (1, 2, 3)]
             for k, out in enumerate((o0, o1, o2, o3)):
-                out[g, pl.ds(pl.multiple_of(8 * c, 8), 8)] = _pick(masks, k, turned)
-        return carry
-
-    lax.fori_loop(0, CORE // 8, chunk, 0)
-
-
-def unpack(own, r1, r2, r3, out, buf):
+                out[g, pl.ds(pl.multiple_of(CL * c, 8), CL)] = _pick(masks, k, turned)
+
+    _chunks(CORE, CL, UNROLL, chunk)
+
+
+def unpack(own, r1, r2, r3, parts, out, total, buf):
     d = lax.axis_index("dep")
     for k, block in enumerate((own, r1, r2, r3)):
         start = pl.multiple_of(lax.rem(d + 4 - k, 4) * CORE, CORE)
@@ -396,6 +417,7 @@
             rf = lax.rem(p + 4 - d, 4)
             for sub in range(4):
                 out[8 * sub + g, pl.ds(rf, 8, stride=4)] = plain[32 * p + 8 * sub : 32 * p + 8 * sub + 8]
+    total[...] = jnp.sum(parts[...], axis=0)
 
 
 def _around(x, k):
@@ -414,20 +436,6 @@
                 for x in range(4):
                     pairs.append((_place(y, z, core, x), _place(*partner(y, z, core, x))))
     return v + lax.ppermute(v, ("lat", "dep"), pairs)
-
-
-def total_of(v):
-    for partner in (
-        lambda y, z, core, x: (y, z, 1 - core, x),
-        lambda y, z, core, x: (y, z ^ 1, core, x),
-        lambda y, z, core, x: (y, 3 - z, core, x),
-        lambda y, z, core, x: (y ^ 1, z, core, x),
-        lambda y, z, core, x: (3 - y, z, core, x),
-        lambda y, z, core, x: (y, z, core, x ^ 1),
-        lambda y, z, core, x: (y, z, core, 3 - x),
-    ):
-        v = _meet(v, partner)
-    return v
 
 
 def _shape(*dims):
@@ -449,11 +457,12 @@
 def per_device(h, zones, fluence, seed):
     slab = _shape(8, 128, 128)
     edge = _shape(8, 16, 128)
-    state, start, light, zid, to_right, to_left = _call(
+    state, start, light, zid, to_inner, to_outer = _call(
         pack,
-        (fluence, h, zones, seed),
+        tuple(pltpu.with_memory_space_constraint(x, pltpu.HBM) for x in (fluence, h, zones, seed)),
         (slab, slab, _shape(4, 128, 128), _shape(4, CORE, 128), edge, edge),
         (
+            _vmem(2, 8, 16, 128),
             _vmem(32, 32, 128),
             _vmem(32, 32, 128),
             pltpu.VMEM((32, 128), jnp.int32),
@@ -464,14 +473,14 @@
         ),
         [_any()] * 4,
     )
-    left = lax.ppermute(to_right, "lat", [(l, l + 1) for l in range(31)])
-    right = lax.ppermute(to_left, "lat", [(l + 1, l) for l in range(31)])
+    outer = lax.ppermute(to_outer, "lat", [pair for l in range(1, 31, 2) for pair in ((l, l + 1), (l + 1, l))])
+    inner = lax.ppermute(to_inner, "lat", [pair for l in range(0, 32, 2) for pair in ((l, l + 1), (l + 1, l))])
     block, seed_block = _shape(8, WIDE, 128), _shape(8, SEED_WIDE, 128)
     h0, h1, h2, h3, s0, s1, s2, s3, light_own = _call(
         insert,
-        (state, start, light, left, right),
+        (state, start, light, inner, outer),
         (block,) * 4 + (seed_block,) * 4 + (_shape(4, WIDE, 128),),
-        (_vmem(8, 144, 128), _vmem(8, 136, 128), _vmem(144, 128)),
+        (_vmem(2, 8, 16, 128), _vmem(8, 144, 128), _vmem(8, 136, 128), _vmem(144, 128)),
     )
     h2, h1, h3 = _around(h2, 2), _around(h1, 1), _around(h3, 3)
     s2, s1, s3 = _around(s2, 2), _around(s1, 1), _around(s3, 3)
@@ -485,14 +494,15 @@
     a, zpart = _call(
         backward,
         (s0, s1, s2, s3, *states, zid),
-        (_vmem(32, HIGH, 128), _shape(NZONE, 128)),
+        (_vmem(32, HIGH, 128), _shape(1, 128)),
         (_vmem(32, HIGH, 128), _vmem(4, HIGH, 128)),
     )
     piece = _shape(8, CORE, 128)
     o0, o1, o2, o3 = _call(last_step, (a, *states), (piece,) * 4)
     o2, o1, o3 = _around(o2, 2), _around(o1, 1), _around(o3, 3)
-    total = jnp.sum(total_of(zpart), axis=1)
-    (out,) = _call(unpack, (o0, o1, o2, o3), (_shape(32, 32, 128),), (_vmem(8, 128, 128),))
+    parts = lax.all_to_all(jnp.broadcast_to(zpart[None], (128, 1, 128)), ("lat", "dep"), 0, 0)
+    out, total = _call(unpack, (o0, o1, o2, o3, parts), (_shape(32, 32, 128), _shape(1, 128)), (_vmem(8, 128, 128),))
+    total = total[0, :NZONE]
     return out, total
 
 

time: 88.7 us -> 67.6 us (0.76)
  the two profiles are of different devices: /device:TPU:0 before, /device:TPU:1 now
where the time goes in v3:
time: 67.6 us; the launch traced here: 67.5 us
  blocking collectives  20.8 us (31%)
  Pallas kernels  20.7 us (31%)
  starting transfers between devices  16.8 us (25%)
  waiting for transfers between devices  7.93 us (12%)
  between operations  0.71 us (1%)
    all_to_all x1, blocking collectives, per_device(): lax.all_to_all(jnp.broadcast_to(zpart[None], (128, 1, 128)), ('lat', 'dep...  20.8 us
    pallas_call x6, Pallas kernels, _call(): pl.pallas_call(kernel, out_shape=tuple(outs), in_specs=spaces or [_full()...  20.7 us
    ppermute x9, starting transfers between devices, _around(): return lax.ppermute(x, 'dep', [(s, (s + k) % 4) for s in range(4)])  11.8 us
    ppermute x9, waiting for transfers between devices, _around(): return lax.ppermute(x, 'dep', [(s, (s + k) % 4) for s in range(4)])  5.9 us
    ppermute x1, starting transfers between devices, per_device(): lax.ppermute(to_outer, 'lat', [pair for l in range(1, 31, 2) for pair in...  3.53 us
    ppermute x1, waiting for transfers between devices, per_device(): lax.ppermute(to_outer, 'lat', [pair for l in range(1, 31, 2) for pair in...  2.03 us
    ppermute x1, starting transfers between devices, per_device(): lax.ppermute(to_inner, 'lat', [pair for l in range(0, 32, 2) for pair in...  1.5 us
  transfers between devices with their start and end apart: 11, of which 3 were waited for; matrix products, arithmetic and copies ran while one was open for 0% of the time, Pallas kernels for 13%

profile of v3, /device:TPU:1, one launch (start us, length us, event | category | flops | bytes accessed | tf_op | source)
XLA Modules:
  0.0 67.5 jit_solution(9190692766692457139)
XLA Ops:
  0.6 1.7 %pack.1 = (f32[8,128,128]{2,1,0:T(8,128)S(1)}, f32[8,128,128]{2,1,0:T(8,128)S(1)}, f32[4,128,128]{2,1,0:T(8,128)S(1)}, f32[4,32,128]{2,1,0:T(8,128)S(1)}, f32[8,...) custom-call(f32[16]{0:T(128)} %fluence_in.1, f32[32,32,128]{2,1,0:T(8,128)} %h_in.1, s32[32,128]{1,0:T(8,128)} %zones_in.1, ...), custom_call_target="tpu_custom_call" | custom-call | tf_op jit(solution)/shard_map/pack/pallas_call | solution.py:446
  2.4 1.5 %collective-permute-start = (f32[8,16,128]{2,1,0:T(8,128)S(1)}, f32[8,16,128]{2,1,0:T(8,128)S(1)}, u32[]{:S(2)}, u32[]{:S(2)}) collective-permute-start(f32[8,16,128]{2,1,0:T(8,128)S(1)} %get-tuple-element.34), channel_id=1, source_target_pairs={{0,4},{4,0},{8,12},{12,8},{16,20},{20,16},{24,28},{28,24},{32,36},... | collective-permute-start | bytes 196616 | tf_op jit(solution)/shard_map/ppermute | solution.py:477
  3.9 3.5 %collective-permute-start.1 = (f32[8,16,128]{2,1,0:T(8,128)S(1)}, f32[8,16,128]{2,1,0:T(8,128)S(1)}, u32[]{:S(2)}, u32[]{:S(2)}) collective-permute-start(f32[8,16,128]{2,1,0:T(8,128)S(1)} %get-tuple-element.35), channel_id=1, source_target_pairs={{4,8},{8,4},{12,16},{16,12},{20,24},{24,20},{28,32},{32,28},{36,40... | collective-permute-start | bytes 196616 | tf_op jit(solution)/shard_map/ppermute | solution.py:476
  7.4 0.0 collective-permute-done.inner
  7.4 2.0 %collective-permute-done.1.outer = f32[8,16,128]{2,1,0:T(8,128)S(1)} collective-permute-done((f32[8,16,128]{2,1,0:T(8,128)S(1)}, f32[8,16,128]{2,1,0:T(8,128)S(1)}, u32[]{:S(2)}, u32[]{:S(2)}) %collective-permute-start.1) | collective-permute-done | bytes 65568 | tf_op jit(solution)/shard_map/ppermute | solution.py:476
  9.5 0.2 insert.1
  9.7 1.7 %collective-permute-start.5 = (f32[8,48,128]{2,1,0:T(8,128)S(1)}, f32[8,48,128]{2,1,0:T(8,128)S(1)}, u32[]{:S(2)}, u32[]{:S(2)}) collective-permute-start(f32[8,48,128]{2,1,0:T(8,128)S(1)} %get-tuple-element.41), channel_id=1, source_target_pairs={{0,1},{1,2},{2,3},{3,0},{4,5},{5,6},{6,7},{7,4},{8,9},{9,10},{10,1... | collective-permute-start | bytes 589832 | tf_op jit(solution)/shard_map/ppermute | solution.py:424
  11.3 2.5 %collective-permute-start.6 = (f32[8,48,128]{2,1,0:T(8,128)S(1)}, f32[8,48,128]{2,1,0:T(8,128)S(1)}, u32[]{:S(2)}, u32[]{:S(2)}) collective-permute-start(f32[8,48,128]{2,1,0:T(8,128)S(1)} %get-tuple-element.42), channel_id=1, source_target_pairs={{0,2},{1,3},{2,0},{3,1},{4,6},{5,7},{6,4},{7,5},{8,10},{9,11},{10,... | collective-permute-start | bytes 589832 | tf_op jit(solution)/shard_map/ppermute | solution.py:424
  13.8 1.1 %collective-permute-start.7 = (f32[8,48,128]{2,1,0:T(8,128)S(1)}, f32[8,48,128]{2,1,0:T(8,128)S(1)}, u32[]{:S(2)}, u32[]{:S(2)}) collective-permute-start(f32[8,48,128]{2,1,0:T(8,128)S(1)} %get-tuple-element.43), channel_id=1, source_target_pairs={{0,3},{1,0},{2,1},{3,2},{4,7},{5,4},{6,5},{7,6},{8,11},{9,8},{10,9... | collective-permute-start | bytes 589832 | tf_op jit(solution)/shard_map/ppermute | solution.py:424
  14.9 0.3 collective-permute-start.2
  15.3 0.9 %collective-permute-start.3 = (f32[8,40,128]{2,1,0:T(8,128)S(1)}, f32[8,40,128]{2,1,0:T(8,128)S(1)}, u32[]{:S(2)}, u32[]{:S(2)}) collective-permute-start(f32[8,40,128]{2,1,0:T(8,128)S(1)} %get-tuple-element.38), channel_id=1, source_target_pairs={{0,2},{1,3},{2,0},{3,1},{4,6},{5,7},{6,4},{7,5},{8,10},{9,11},{10,... | collective-permute-start | bytes 491528 | tf_op jit(solution)/shard_map/ppermute | solution.py:424
  16.1 2.8 %collective-permute-done.5.r1 = f32[8,48,128]{2,1,0:T(8,128)S(1)} collective-permute-done((f32[8,48,128]{2,1,0:T(8,128)S(1)}, f32[8,48,128]{2,1,0:T(8,128)S(1)}, u32[]{:S(2)}, u32[]{:S(2)}) %collective-permute-start.5) | collective-permute-done | bytes 196640 | tf_op jit(solution)/shard_map/ppermute | solution.py:424
  19.0 0.6 collective-permute-start.4
  19.6 3.0 %collective-permute-done.6.r2 = f32[8,48,128]{2,1,0:T(8,128)S(1)} collective-permute-done((f32[8,48,128]{2,1,0:T(8,128)S(1)}, f32[8,48,128]{2,1,0:T(8,128)S(1)}, u32[]{:S(2)}, u32[]{:S(2)}) %collective-permute-start.6) | collective-permute-done | bytes 196640 | tf_op jit(solution)/shard_map/ppermute | solution.py:424
  22.6 0.0 collective-permute-done.7.r3
  22.6 8.5 %forward.1 = (f32[4,32,64,128]{3,2,1,0:T(8,128)S(1)}, f32[4,32,64,128]{3,2,1,0:T(8,128)S(1)}, f32[4,32,64,128]{3,2,1,0:T(8,128)S(1)}, f32[4,32,64,128]{3,2,1,0:T...) custom-call(f32[8,48,128]{2,1,0:T(8,128)S(1)} %get-tuple-element.40.own, ...), custom_call_target="tpu_custom_call" | custom-call | tf_op jit(solution)/shard_map/forward/pallas_call | solution.py:446
  31.2 0.0 collective-permute-done.2.r1
  31.2 0.0 collective-permute-done.3.r2
  31.2 0.0 collective-permute-done.4.r3
  31.2 7.4 %backward.1 = (f32[32,64,128]{2,1,0:T(8,128)S(1)}, f32[1,128]{1,0:T(1,128)S(1)}) custom-call(f32[8,40,128]{2,1,0:T(8,128)S(1)} %get-tuple-element.36.own, f32[8,40,128]{2,1,0:T(8,128)S(1)} %collective-permute-done.2.r1, f32[8,40,128]{2,1,0:T(8,128)S(1)} %collective-permute-done.3.r2, f32[8,40,128]{2,1,0:T(8,128)S(1)} %collective-permute-done.4.r3, ...), custom_call_target="tpu_custom_call" | custom-call | tf_op jit(solution)/shard_map/backward/pallas_call | solution.py:446
  38.6 1.7 %last_step.1 = (f32[8,32,128]{2,1,0:T(8,128)S(1)}, f32[8,32,128]{2,1,0:T(8,128)S(1)}, f32[8,32,128]{2,1,0:T(8,128)S(1)}, f32[8,32,128]{2,1,0:T(8,128)S(1)}) custom-call(f32[32,64,128]{2,1,0:T(8,128)S(1)} %get-tuple-element.52.a_ref, f32[4,32,64,128]{3,2,1,0:T(8,128)S(1)} %get-tuple-element.45.t_ref, f32[4,32,64,128]{3,2,1,0:T(8,128)S(1)} %get-tuple-element.46.k_ref, ...), custom_call_target="tpu_custom_call" | custom-call | tf_op jit(solution)/shard_map/last_step/pallas_call | solution.py:446
  40.3 1.4 %collective-permute-start.8 = (f32[8,32,128]{2,1,0:T(8,128)S(1)}, f32[8,32,128]{2,1,0:T(8,128)S(1)}, u32[]{:S(2)}, u32[]{:S(2)}) collective-permute-start(f32[8,32,128]{2,1,0:T(8,128)S(1)} %get-tuple-element.54), channel_id=1, source_target_pairs={{0,1},{1,2},{2,3},{3,0},{4,5},{5,6},{6,7},{7,4},{8,9},{9,10},{10,1... | collective-permute-start | bytes 393224 | tf_op jit(solution)/shard_map/ppermute | solution.py:424
  41.8 2.7 %collective-permute-start.9 = (f32[8,32,128]{2,1,0:T(8,128)S(1)}, f32[8,32,128]{2,1,0:T(8,128)S(1)}, u32[]{:S(2)}, u32[]{:S(2)}) collective-permute-start(f32[8,32,128]{2,1,0:T(8,128)S(1)} %get-tuple-element.55), channel_id=1, source_target_pairs={{0,2},{1,3},{2,0},{3,1},{4,6},{5,7},{6,4},{7,5},{8,10},{9,11},{10,... | collective-permute-start | bytes 393224 | tf_op jit(solution)/shard_map/ppermute | solution.py:424
  44.5 0.5 collective-permute-start.10
  45.1 20.8 %all_to_all.5.parts = f32[128,1,128]{2,1,0:T(1,128)S(1)} all-to-all(f32[128,1,128]{2,1,0:T(1,128)S(1)} %broadcast_in_dim.9), channel_id=1, replica_groups=mesh['lat'=32,'dep'=4] {'lat','dep'}, dimensions={0} | all-to-all | bytes 131072 | tf_op jit(solution)/shard_map/all_to_all | solution.py:503
  65.9 0.0 collective-permute-done.8.r1
  65.9 0.0 collective-permute-done.9.r2
  65.9 0.0 collective-permute-done.10.r3
  65.9 1.1 %unpack.1 = (f32[32,32,128]{2,1,0:T(8,128)}, f32[1,128]{1,0:T(1,128)S(1)}) custom-call(f32[8,32,128]{2,1,0:T(8,128)S(1)} %get-tuple-element.53.own, f32[8,32,128]{2,1,0:T(8,128)S(1)} %collective-permute-done.8.r1, f32[8,32,128]{2,1,0:T(8,128)S(1)} %collective-permute-done.9.r2, f32[8,32,128]{2,1,0:T(8,128)S(1)} %collective-permute-done.10.r3, ...), custom_call_target="tpu_custom_call" | custom-call | tf_op jit(solution)/shard_map/unpack/pallas_call | solution.py:446
  67.0 0.5 slice_bitcast_fusion
  (1 shorter events, 0.0 us)
Async XLA Ops:
  2.4 5.0 %collective-permute-start = (f32[8,16,128]{2,1,0:T(8,128)S(1)}, f32[8,16,128]{2,1,0:T(8,128)S(1)}, u32[]{:S(2)}, u32[]{:S(2)}) collective-permute-start(f32[8,16,128]{2,1,0:T(8,128)S(1)} %get-tuple-element.34), channel_id=1, source_target_pairs={{0,4},{4,0},{8,12},{12,8},{16,20},{20,16},{24,28},{28,24},{32,36},... | collective-permute-start | bytes 196616 | tf_op jit(solution)/shard_map/ppermute | solution.py:477
  3.9 5.6 %collective-permute-start.1 = (f32[8,16,128]{2,1,0:T(8,128)S(1)}, f32[8,16,128]{2,1,0:T(8,128)S(1)}, u32[]{:S(2)}, u32[]{:S(2)}) collective-permute-start(f32[8,16,128]{2,1,0:T(8,128)S(1)} %get-tuple-element.35), channel_id=1, source_target_pairs={{4,8},{8,4},{12,16},{16,12},{20,24},{24,20},{28,32},{32,28},{36,40... | collective-permute-start | bytes 196616 | tf_op jit(solution)/shard_map/ppermute | solution.py:476
  9.7 9.3 %collective-permute-start.5 = (f32[8,48,128]{2,1,0:T(8,128)S(1)}, f32[8,48,128]{2,1,0:T(8,128)S(1)}, u32[]{:S(2)}, u32[]{:S(2)}) collective-permute-start(f32[8,48,128]{2,1,0:T(8,128)S(1)} %get-tuple-element.41), channel_id=1, source_target_pairs={{0,1},{1,2},{2,3},{3,0},{4,5},{5,6},{6,7},{7,4},{8,9},{9,10},{10,1... | collective-permute-start | bytes 589832 | tf_op jit(solution)/shard_map/ppermute | solution.py:424
  11.3 11.3 %collective-permute-start.6 = (f32[8,48,128]{2,1,0:T(8,128)S(1)}, f32[8,48,128]{2,1,0:T(8,128)S(1)}, u32[]{:S(2)}, u32[]{:S(2)}) collective-permute-start(f32[8,48,128]{2,1,0:T(8,128)S(1)} %get-tuple-element.42), channel_id=1, source_target_pairs={{0,2},{1,3},{2,0},{3,1},{4,6},{5,7},{6,4},{7,5},{8,10},{9,11},{10,... | collective-permute-start | bytes 589832 | tf_op jit(solution)/shard_map/ppermute | solution.py:424
  13.8 8.8 %collective-permute-start.7 = (f32[8,48,128]{2,1,0:T(8,128)S(1)}, f32[8,48,128]{2,1,0:T(8,128)S(1)}, u32[]{:S(2)}, u32[]{:S(2)}) collective-permute-start(f32[8,48,128]{2,1,0:T(8,128)S(1)} %get-tuple-element.43), channel_id=1, source_target_pairs={{0,3},{1,0},{2,1},{3,2},{4,7},{5,4},{6,5},{7,6},{8,11},{9,8},{10,9... | collective-permute-start | bytes 589832 | tf_op jit(solution)/shard_map/ppermute | solution.py:424
  14.9 16.2 %collective-permute-start.2 = (f32[8,40,128]{2,1,0:T(8,128)S(1)}, f32[8,40,128]{2,1,0:T(8,128)S(1)}, u32[]{:S(2)}, u32[]{:S(2)}) collective-permute-start(f32[8,40,128]{2,1,0:T(8,128)S(1)} %get-tuple-element.37), channel_id=1, source_target_pairs={{0,1},{1,2},{2,3},{3,0},{4,5},{5,6},{6,7},{7,4},{8,9},{9,10},{10,1... | collective-permute-start | bytes 491528 | tf_op jit(solution)/shard_map/ppermute | solution.py:424
  15.3 15.9 %collective-permute-start.3 = (f32[8,40,128]{2,1,0:T(8,128)S(1)}, f32[8,40,128]{2,1,0:T(8,128)S(1)}, u32[]{:S(2)}, u32[]{:S(2)}) collective-permute-start(f32[8,40,128]{2,1,0:T(8,128)S(1)} %get-tuple-element.38), channel_id=1, source_target_pairs={{0,2},{1,3},{2,0},{3,1},{4,6},{5,7},{6,4},{7,5},{8,10},{9,11},{10,... | collective-permute-start | bytes 491528 | tf_op jit(solution)/shard_map/ppermute | solution.py:424
  19.0 12.2 %collective-permute-start.4 = (f32[8,40,128]{2,1,0:T(8,128)S(1)}, f32[8,40,128]{2,1,0:T(8,128)S(1)}, u32[]{:S(2)}, u32[]{:S(2)}) collective-permute-start(f32[8,40,128]{2,1,0:T(8,128)S(1)} %get-tuple-element.39), channel_id=1, source_target_pairs={{0,3},{1,0},{2,1},{3,2},{4,7},{5,4},{6,5},{7,6},{8,11},{9,8},{10,9... | collective-permute-start | bytes 491528 | tf_op jit(solution)/shard_map/ppermute | solution.py:424
  40.3 25.6 %collective-permute-start.8 = (f32[8,32,128]{2,1,0:T(8,128)S(1)}, f32[8,32,128]{2,1,0:T(8,128)S(1)}, u32[]{:S(2)}, u32[]{:S(2)}) collective-permute-start(f32[8,32,128]{2,1,0:T(8,128)S(1)} %get-tuple-element.54), channel_id=1, source_target_pairs={{0,1},{1,2},{2,3},{3,0},{4,5},{5,6},{6,7},{7,4},{8,9},{9,10},{10,1... | collective-permute-start | bytes 393224 | tf_op jit(solution)/shard_map/ppermute | solution.py:424
  41.8 24.1 %collective-permute-start.9 = (f32[8,32,128]{2,1,0:T(8,128)S(1)}, f32[8,32,128]{2,1,0:T(8,128)S(1)}, u32[]{:S(2)}, u32[]{:S(2)}) collective-permute-start(f32[8,32,128]{2,1,0:T(8,128)S(1)} %get-tuple-element.55), channel_id=1, source_target_pairs={{0,2},{1,3},{2,0},{3,1},{4,6},{5,7},{6,4},{7,5},{8,10},{9,11},{10,... | collective-permute-start | bytes 393224 | tf_op jit(solution)/shard_map/ppermute | solution.py:424
  44.5 21.4 %collective-permute-start.10 = (f32[8,32,128]{2,1,0:T(8,128)S(1)}, f32[8,32,128]{2,1,0:T(8,128)S(1)}, u32[]{:S(2)}, u32[]{:S(2)}) collective-permute-start(f32[8,32,128]{2,1,0:T(8,128)S(1)} %get-tuple-element.56), channel_id=1, source_target_pairs={{0,3},{1,0},{2,1},{3,2},{4,7},{5,4},{6,5},{7,6},{8,11},{9,8},{10,9... | collective-permute-start | bytes 393224 | tf_op jit(solution)/shard_map/ppermute | solution.py:424

commit v4 on v3

v4 whole, which is shorter than its diff:
```python
import math

import jax
import jax.numpy as jnp
from jax import lax
from jax.experimental import pallas as pl
from jax.experimental.pallas import tpu as pltpu
from jax.sharding import PartitionSpec as P


NZONE = 16
CORE = 32
HALO = 8
WIDE = CORE + 2 * HALO
SEED_HALO = 4
SEED_WIDE = CORE + 2 * SEED_HALO
BASE = 8
HIGH = WIDE + 2 * BASE
DT = 0.1
ABSORB_SOLID = 0.004
ABSORB_RISE = 0.026
LOG2E = math.log2(math.e)
EM10 = math.exp(-10.0)
F32 = jnp.float32


def _params():
    return pltpu.CompilerParams(vmem_limit_bytes=16 * 1024 * 1024)


def _group(d):
    return jnp.where(lax.rem(lax.axis_index("lat"), 2) == 0, d, 3 - d)


def _columns(d):
    return pl.ds(pl.multiple_of(_group(d) * CORE, CORE), CORE)


def _vmem(*shape):
    return pltpu.VMEM(shape, F32)


def _full():
    return pl.BlockSpec(memory_space=pltpu.VMEM)


def _lanes(rows=8):
    return lax.broadcasted_iota(jnp.int32, (rows, 128), 1)


def _packed(ref, g, d):
    tiles = []
    for p in range(4):
        rf = lax.rem(p + 4 - d, 4)
        tiles += [ref[8 * sub + g, pl.ds(rf, 8, stride=4)] for sub in range(4)]
    return jnp.concatenate(tiles, axis=0).T


def _surface(ref, rf):
    return jnp.concatenate([ref[pl.ds(rf, 8, stride=4)]] * 16, axis=0).T


def pack_state(h_in, h0, h1, h2, h3, h, buf, sem):
    d = lax.axis_index("dep")
    copy = pltpu.make_async_copy(h_in, h, sem)
    copy.start()
    copy.wait()
    for g in range(8):
        buf[g] = _packed(h, g, d)
    for k, out in enumerate((h0, h1, h2, h3)):
        out[...] = buf[:, _columns(lax.rem(d + k, 4))]


def pack_rest(fluence_in, zones_in, a_in, seed, light, zid, to_inner, to_outer, edges, a, zones, flat, zbuf, fluence, sems):
    d = lax.axis_index("dep")
    to_left, to_right = edges.at[0], edges.at[1]
    copies = [
        pltpu.make_async_copy(source, target, sems.at[k])
        for k, (source, target) in enumerate(((fluence_in, fluence), (zones_in, zones), (a_in, a)))
    ]
    for copy in copies:
        copy.start()
    copies[0].wait()
    copies[1].wait()
    ids = zones[...]
    intensity = jnp.zeros(ids.shape, F32)
    for k in range(NZONE):
        intensity = jnp.where(ids == k, fluence[k] * DT, intensity)
    flat[0] = intensity
    flat[1] = ids.astype(F32)
    for rf in range(4):
        packed = _surface(flat.at[0], rf)
        light[rf] = packed
        for half in range(2):
            to_left[2 * rf + half, 4:8] = packed[4 * half : 4 * half + 4]
            to_right[2 * rf + half, 4:8] = packed[120 + 4 * half : 124 + 4 * half]
        zbuf[...] = _surface(flat.at[1], rf)
        zid[rf] = zbuf[_columns(d)]
    copies[2].wait()
    for g in range(8):
        packed = _packed(a, g, d)
        seed[g] = packed
        to_left[g, 0:4] = packed[0:4]
        to_right[g, 0:4] = packed[124:128]
    odd = lax.rem(lax.axis_index("lat"), 2)
    to_inner[...] = edges[1 - odd]
    to_outer[...] = edges[odd]


def insert(seed, light, inner, outer, s0, s1, s2, s3, light_own, sides, sbuf, lbuf):
    d = lax.axis_index("dep")
    odd = lax.rem(lax.axis_index("lat"), 2)
    sides[odd] = outer[...]
    sides[1 - odd] = inner[...]
    left, right = sides.at[0], sides.at[1]
    sbuf[:, 0:4] = left[:, 0:4]
    sbuf[:, 4:132] = seed[...]
    sbuf[:, 132:136] = right[:, 0:4]
    for k, out in enumerate((s0, s1, s2, s3)):
        start = pl.multiple_of(_group(lax.rem(d + k, 4)) * CORE, CORE)
        out[...] = sbuf[:, pl.ds(start, SEED_WIDE)]
    start = pl.multiple_of(_group(d) * CORE, CORE)
    for rf in range(4):
        for half in range(2):
            lbuf[4 * half : 4 * half + 4] = left[2 * rf + half, 4:8]
            lbuf[136 + 4 * half : 140 + 4 * half] = right[2 * rf + half, 4:8]
        lbuf[8:136] = light[rf]
        light_own[rf, 0:BASE] = jnp.zeros((BASE, 128), F32)
        light_own[rf, BASE : BASE + WIDE] = lbuf[pl.ds(start, WIDE)]
        light_own[rf, BASE + WIDE :] = jnp.zeros((BASE, 128), F32)


def _source_masks():
    part = lax.rem(_lanes(8) // 32 + 4 - lax.axis_index("dep"), 4)
    return [part == j for j in range(4)]


def _pick(masks, shift, values):
    return jnp.where(
        masks[shift % 4],
        values[0],
        jnp.where(masks[(shift + 1) % 4], values[1], jnp.where(masks[(shift + 2) % 4], values[2], values[3])),
    )


def _gather(blocks, field, first, count):
    masks = [jnp.broadcast_to(m[0:1], (count, 128)) for m in _source_masks()]
    for g in range(8):
        own, r1, r2, r3 = [block[g] for block in blocks]
        for rf in range(4):
            mixed = _pick(masks, rf, (own, r3, r2, r1))
            field[8 * rf + g, pl.ds(BASE + first, count)] = mixed if rf == 0 else pltpu.roll(mixed, 128 - 32 * rf, 1)


class _Tiles:
    def __init__(self, row, rows, exact):
        self.rows, self.exact = rows, exact
        self.here, self.up, self.down = pl.ds(row, rows), pl.ds(row + 1, rows), pl.ds(row - 1, rows)


def _inclusive(total, lane, reverse):
    a = lax.broadcasted_iota(jnp.int32, (128, 128), 0)
    b = lax.broadcasted_iota(jnp.int32, (128, 128), 1)
    same = lax.rem(a, 8) == lax.rem(b, 8)
    tri = jnp.where(jnp.logical_and(same, a >= b if reverse else a <= b), 1.0, 0.0).astype(jnp.bfloat16)
    high = total.astype(jnp.bfloat16)
    low = (total - high.astype(F32)).astype(jnp.bfloat16)
    return jnp.dot(high, tri, preferred_element_type=F32) + jnp.dot(low, tri, preferred_element_type=F32)


def _properties(n, rf, tiles, states, t_ref, k_ref, c_ref, r_ref, l_ref):
    lane = _lanes(tiles.rows)
    here = tiles.here
    run = jnp.zeros((tiles.rows, 128), F32)
    runs = []
    for g in range(8):
        i = 8 * rf + g
        h = states[g]
        e = jnp.exp2(h * (10.0 * LOG2E) - 10.0 * LOG2E)
        u = 1.0 + e
        v = 1.0 + EM10 * e
        inv = pl.reciprocal(u * v)
        ramp = 0.1 * jnp.log(u * (u * inv))
        t = h - ramp
        m = pl.reciprocal(1.0 + t * t)
        t_ref[n, i, here] = t
        k_ref[n, i, here] = 0.03 + 0.04 * m
        c_ref[n, i, here] = (-0.08 * t) * (m * m)
        r_ref[n, i, here] = e * ((1.0 - EM10) * inv)
        runs.append(run)
        run = run + (ABSORB_SOLID * LOG2E + (ABSORB_RISE * LOG2E) * ramp)
    above = _inclusive(run, lane, False) - run
    for g in range(8):
        l_ref[n, 9 * rf + g, here] = jnp.exp2(-(above + runs[g]))
    l_ref[n, 9 * rf + 8, here] = jnp.exp2(-(above + run))


def _advance(n, tiles, h_ref, t_ref, k_ref, l_ref, light, then):
    lane = _lanes(tiles.rows)
    inside = lax.rem(lane, 8) < 7
    above_bottom = lane < 120
    here, up, down = tiles.here, tiles.up, tiles.down

    def across(g):
        t3, k3 = t_ref[n, 24 + g, here], k_ref[n, 24 + g, here]
        t0, k0 = pltpu.roll(t_ref[n, g, here], 127, 1), pltpu.roll(k_ref[n, g, here], 127, 1)
        return jnp.where(inside, (k3 + k0) * (t0 - t3), 0.0)

    last = [across(g) for g in range(8)]
    before = [pltpu.roll(f, 1, 1) for f in last]
    for rf in range(4):
        i0 = 8 * rf
        t = [t_ref[n, i0 + g, here] for g in range(8)]
        k = [k_ref[n, i0 + g, here] for g in range(8)]
        end = jnp.where(above_bottom, (k[7] + pltpu.roll(k[0], 120, 1)) * (pltpu.roll(t[0], 120, 1) - t[7]), 0.0)
        flux_before = pltpu.roll(end, 8, 1)
        new = []
        for g in range(8):
            i = i0 + g
            if g < 7:
                flux = (k[g] + k[g + 1]) * (t[g + 1] - t[g])
            else:
                flux = jnp.where(above_bottom, end, -0.05 * t[7])
            if rf < 3:
                side = (k[g] + k_ref[n, i + 8, here]) * (t_ref[n, i + 8, here] - t[g])
            else:
                side = last[g]
            change = (flux - flux_before) + (side - before[g])
            col = (k[g] + k_ref[n, i, up]) * (t_ref[n, i, up] - t[g])
            if tiles.exact:
                col_before = (k_ref[n, i, down] + k[g]) * (t[g] - t_ref[n, i, down])
            else:
                col_before = pltpu.roll(col, 1, 0)
            change = change + (col - col_before)
            source = light[rf, here] * (l_ref[n, 9 * rf + g, here] - l_ref[n, 9 * rf + g + 1, here])
            new.append(h_ref[i, here] + (change + source))
            flux_before, before[g] = flux, side
        then(rf, new)


def _ghost(ref_rows):
    lat, group = lax.axis_index("lat"), _group(lax.axis_index("dep"))

    @pl.when(jnp.logical_and(lat == 0, group == 0))
    def _():
        for i in range(32):
            ref_rows(i, HALO - 1)[...] = ref_rows(i, HALO)[...]

    @pl.when(jnp.logical_and(lat == 31, group == 3))
    def _():
        for i in range(32):
            ref_rows(i, HALO + CORE)[...] = ref_rows(i, HALO + CORE - 1)[...]


def gather_state(own, r1, r2, r3, h0, to_inner, to_outer):
    _gather((own, r1, r2, r3), h0, HALO, CORE)
    odd = lax.rem(_group(lax.axis_index("dep")), 2)
    first, last = BASE + HALO, BASE + CORE
    to_inner[...] = h0[:, pl.ds(pl.multiple_of(jnp.where(odd == 1, first, last), 8), HALO)]
    to_outer[...] = h0[:, pl.ds(pl.multiple_of(jnp.where(odd == 1, last, first), 8), HALO)]


def forward_core(h0, light, h1, h2, t_ref, k_ref, c_ref, r_ref, l_ref):
    fields = (t_ref, k_ref, c_ref, r_ref, l_ref)
    tiles = _Tiles(BASE + HALO, CORE, False)
    for rf in range(4):
        _properties(0, rf, tiles, [h0[8 * rf + g, tiles.here] for g in range(8)], *fields)
    for n, source, target in ((0, h0, h1), (1, h1, h2), (2, h2, None)):

        def then(rf, new, n=n, target=target):
            if target is not None:
                for g in range(8):
                    target[8 * rf + g, tiles.here] = new[g]
            _properties(n + 1, rf, tiles, new, *fields)

        _advance(n, tiles, source, t_ref, k_ref, l_ref, light, then)


def forward_sides(inner, outer, light, *refs):
    h0, h1, h2, t_ref, k_ref, c_ref, r_ref, l_ref = refs[8:]
    fields = (t_ref, k_ref, c_ref, r_ref, l_ref)
    even = lax.rem(_group(lax.axis_index("dep")), 2) == 0

    @pl.when(even)
    def _():
        h0[:, BASE : BASE + HALO] = outer[...]
        h0[:, BASE + HALO + CORE : BASE + WIDE] = inner[...]

    @pl.when(jnp.logical_not(even))
    def _():
        h0[:, BASE : BASE + HALO] = inner[...]
        h0[:, BASE + HALO + CORE : BASE + WIDE] = outer[...]

    for first in (0, HALO + CORE):
        tiles = _Tiles(BASE + first, HALO, False)
        for rf in range(4):
            _properties(0, rf, tiles, [h0[8 * rf + g, tiles.here] for g in range(8)], *fields)
    for n, source, target in ((0, h0, h1), (1, h1, h2), (2, h2, None)):
        _ghost(lambda i, c, n=n: t_ref.at[n, i, pl.ds(BASE + c, 1)])
        for first in (n + 1, HALO + CORE - 1 - n):
            tiles = _Tiles(BASE + first, HALO, True)

            def then(rf, new, n=n, target=target, tiles=tiles):
                if target is not None:
                    for g in range(8):
                        target[8 * rf + g, tiles.here] = new[g]
                _properties(n + 1, rf, tiles, new, *fields)

            _advance(n, tiles, source, t_ref, k_ref, l_ref, light, then)


def _retreat(n, tiles, a_ref, t_ref, k_ref, c_ref, r_ref, l_ref, light, put, seen):
    lane = _lanes(tiles.rows)
    inside = lax.rem(lane, 8) < 7
    above_bottom = lane < 120
    here, up, down = tiles.here, tiles.up, tiles.down

    def across(g):
        a3, t3, k3 = a_ref[24 + g, here], t_ref[n, 24 + g, here], k_ref[n, 24 + g, here]
        a0, t0, k0 = [pltpu.roll(x, 127, 1) for x in (a_ref[g, here], t_ref[n, g, here], k_ref[n, g, here])]
        jump = jnp.where(inside, a3 - a0, 0.0)
        return jump * (k3 + k0), jump * (t0 - t3)

    last = [across(g) for g in range(8)]
    before = [(pltpu.roll(push, 1, 1), pltpu.roll(share, 1, 1)) for push, share in last]
    for rf in range(4):
        i0 = 8 * rf
        a = [a_ref[i0 + g, here] for g in range(8)]
        t = [t_ref[n, i0 + g, here] for g in range(8)]
        k = [k_ref[n, i0 + g, here] for g in range(8)]
        run = jnp.zeros((tiles.rows, 128), F32)
        runs = [None] * 8
        for g in reversed(range(8)):
            runs[g] = run
            run = run + a[g] * (l_ref[n, 9 * rf + g, here] - l_ref[n, 9 * rf + g + 1, here])
        below = _inclusive(run, lane, True) - run
        seen(rf, run)
        gain = ABSORB_RISE * light[rf, here]
        jump = jnp.where(above_bottom, a[7] - pltpu.roll(a[0], 120, 1), 0.0)
        push_end = jump * (k[7] + pltpu.roll(k[0], 120, 1))
        share_end = jump * (pltpu.roll(t[0], 120, 1) - t[7])
        push_before, share_before = pltpu.roll(push_end, 8, 1), pltpu.roll(share_end, 8, 1)
        for g in range(8):
            i = i0 + g
            if g < 7:
                jump = a[g] - a[g + 1]
                push, share = jump * (k[g] + k[g + 1]), jump * (t[g + 1] - t[g])
            else:
                push, share = jnp.where(above_bottom, push_end, 0.05 * a[7]), share_end
            if rf < 3:
                jump = a[g] - a_ref[i + 8, here]
                push_r, share_r = jump * (k[g] + k_ref[n, i + 8, here]), jump * (t_ref[n, i + 8, here] - t[g])
            else:
                push_r, share_r = last[g]
            grad_t = (push_before - push) + (before[g][0] - push_r)
            grad_k = (share_before + share) + (before[g][1] + share_r)
            jump = a[g] - a_ref[i, up]
            push_c, share_c = jump * (k[g] + k_ref[n, i, up]), jump * (t_ref[n, i, up] - t[g])
            if tiles.exact:
                jump = a_ref[i, down] - a[g]
                push_d, share_d = jump * (k_ref[n, i, down] + k[g]), jump * (t[g] - t_ref[n, i, down])
            else:
                push_d, share_d = pltpu.roll(push_c, 1, 0), pltpu.roll(share_c, 1, 0)
            grad_t = grad_t + (push_d - push_c)
            grad_k = grad_k + (share_d + share_c)
            heat = grad_t + c_ref[n, i, here] * grad_k
            absorbed = gain * (a[g] * l_ref[n, 9 * rf + g + 1, here] - (below + runs[g]))
            put(i, a[g] + (heat + r_ref[n, i, here] * (absorbed - heat)))
            push_before, share_before, before[g] = push, share, (push_r, share_r)


def backward(own, r1, r2, r3, t_ref, k_ref, c_ref, r_ref, l_ref, light, zid, a_ref, zpart, total):
    _gather((own, r1, r2, r3), a_ref.at[0], SEED_HALO, SEED_WIDE)
    fields = (t_ref, k_ref, c_ref, r_ref, l_ref, light)
    total[...] = jnp.zeros(total.shape, F32)

    def step(i, carry):
        n, at = 3 - i, lax.rem(i, 2)
        source, target = a_ref.at[at], a_ref.at[1 - at]
        _ghost(lambda j, c: source.at[j, pl.ds(BASE + c, 1)])
        tiles = _Tiles(BASE + SEED_HALO, SEED_WIDE, False)

        def put(j, value):
            target[j, tiles.here] = value

        def seen(rf, value):
            total[rf, tiles.here] += value

        _retreat(n, tiles, source, *fields, put, seen)
        return carry

    lax.fori_loop(0, 3, step, 0)
    source = a_ref.at[1]
    _ghost(lambda j, c: source.at[j, pl.ds(BASE + c, 1)])
    core = pl.ds(BASE + HALO, CORE)
    sums = []
    for rf in range(4):
        value = total[rf, core]
        for g in range(8):
            value = value + source[8 * rf + g, core] * (l_ref[0, 9 * rf + g, core] - l_ref[0, 9 * rf + g + 1, core])
        sums.append(value * DT)
    rows = []
    for z in range(NZONE):
        picked = [jnp.where(zid[rf] == float(z), sums[rf], 0.0) for rf in range(4)]
        rows.append(jnp.sum((picked[0] + picked[1]) + (picked[2] + picked[3]), axis=0, keepdims=True))
    spread = jnp.concatenate(rows + [jnp.zeros((128 - NZONE, 128), F32)], axis=0)
    zpart[...] = jnp.sum(spread.T, axis=0, keepdims=True)


def last_step(a_ref, t_ref, k_ref, c_ref, r_ref, l_ref, light, o0, o1, o2, o3):
    masks = [jnp.broadcast_to(m[0:1], (CORE, 128)) for m in _source_masks()]
    values = [None] * 32

    def put(i, value):
        values[i] = value

    tiles = _Tiles(BASE + HALO, CORE, True)
    _retreat(0, tiles, a_ref.at[1], t_ref, k_ref, c_ref, r_ref, l_ref, light, put, lambda rf, value: None)
    for g in range(8):
        turned = [values[g]] + [pltpu.roll(values[8 * rf + g], 32 * rf, 1) for rf in (1, 2, 3)]
        for k, out in enumerate((o0, o1, o2, o3)):
            out[g] = _pick(masks, k, turned)


def unpack(own, r1, r2, r3, parts, out, total, buf):
    d = lax.axis_index("dep")
    for k, block in enumerate((own, r1, r2, r3)):
        buf[:, _columns(lax.rem(d + 4 - k, 4))] = block[...]
    for g in range(8):
        plain = buf[g].T
        for p in range(4):
            rf = lax.rem(p + 4 - d, 4)
            for sub in range(4):
                out[8 * sub + g, pl.ds(rf, 8, stride=4)] = plain[32 * p + 8 * sub : 32 * p + 8 * sub + 8]
    total[...] = jnp.sum(parts[...], axis=(0, 1))[:NZONE]


def _around(x, k):
    return lax.ppermute(x, "dep", [(s, (s + k) % 4) for s in range(4)])


def _place(y, z, core, x):
    return ((y * 4 + z) * 2 + core) * 4 + x


def _meet(v, partner):
    pairs = []
    for y in range(4):
        for z in range(4):
            for core in range(2):
                for x in range(4):
                    pairs.append((_place(y, z, core, x), _place(*partner(y, z, core, x))))
    return v + lax.ppermute(v, ("lat", "dep"), pairs)


def _shape(*dims):
    return jax.ShapeDtypeStruct(dims, F32)


def _call(kernel, inputs, outs, scratch=(), aliases=None, cost=None):
    return pl.pallas_call(
        kernel,
        out_shape=tuple(outs),
        in_specs=[_full()] * len(inputs),
        out_specs=(_full(),) * len(outs),
        scratch_shapes=list(scratch),
        input_output_aliases=aliases or {},
        cost_estimate=cost,
        compiler_params=_params(),
        name=kernel.__name__,
    )(*inputs)


def _call_hbm(kernel, inputs, outs, scratch):
    return pl.pallas_call(
        kernel,
        out_shape=tuple(outs),
        in_specs=[pl.BlockSpec(memory_space=pltpu.HBM)] * len(inputs),
        out_specs=(_full(),) * len(outs),
        scratch_shapes=list(scratch),
        compiler_params=_params(),
        name=kernel.__name__,
    )(*[pltpu.with_memory_space_constraint(x, pltpu.HBM) for x in inputs])


def _swap(x, axes, places, first):
    return lax.ppermute(
        x, axes, [pair for a, b in list(zip(places, places[1:], strict=False))[first::2] for pair in ((a, b), (b, a))]
    )


def per_device(h, zones, fluence, seed):
    piece = _shape(8, CORE, 128)
    h0, h1, h2, h3 = _call_hbm(
        pack_state, (h,), (piece,) * 4, (_vmem(32, 32, 128), _vmem(8, 128, 128), pltpu.SemaphoreType.DMA)
    )
    h2, h1, h3 = _around(h2, 2), _around(h1, 1), _around(h3, 3)
    edge = _shape(8, 8, 128)
    start, light, zid, to_inner, to_outer = _call_hbm(
        pack_rest,
        (fluence, zones, seed),
        (_shape(8, 128, 128), _shape(4, 128, 128), _shape(4, CORE, 128), edge, edge),
        (
            _vmem(2, 8, 8, 128),
            _vmem(32, 32, 128),
            pltpu.VMEM((32, 128), jnp.int32),
            _vmem(2, 32, 128),
            _vmem(128, 128),
            pltpu.SMEM((NZONE,), F32),
            pltpu.SemaphoreType.DMA((3,)),
        ),
    )
    line = range(32)
    outer, inner = _swap(to_outer, "lat", line, 1), _swap(to_inner, "lat", line, 0)
    one = _vmem(32, HIGH, 128)
    side = _shape(32, HALO, 128)
    inner, outer, h0 = lax.optimization_barrier((inner, outer, h0))
    state, to_inner, to_outer = _call(gather_state, (h0, h1, h2, h3), (one, side, side))
    axes = ("lat", "dep")
    line = [4 * l + (c if l % 2 == 0 else 3 - c) for l in range(32) for c in range(4)]
    seed_block = _shape(8, SEED_WIDE, 128)
    start, to_inner = lax.optimization_barrier((start, to_inner))
    s0, s1, s2, s3, light = _call(
        insert,
        (start, light, inner, outer),
        (seed_block,) * 4 + (_shape(4, HIGH, 128),),
        (_vmem(2, 8, 8, 128), _vmem(8, 136, 128), _vmem(144, 128)),
    )
    outer, inner = _swap(to_outer, axes, line, 1), _swap(to_inner, axes, line, 0)
    s2, s1, s3 = _around(s2, 2), _around(s1, 1), _around(s3, 3)
    field = _vmem(4, 32, HIGH, 128)
    fields = (one,) * 2 + (field,) * 4 + (_vmem(4, 36, HIGH, 128),)
    states = _call(forward_core, (state, light), fields, cost=pl.CostEstimate(flops=1000, bytes_accessed=1000, transcendentals=0))
    states = _call(
        forward_sides,
        (inner, outer, light, state, *states),
        (one,) + fields,
        (),
        {3 + i: i for i in range(8)},
        pl.CostEstimate(flops=10000000000, bytes_accessed=100000000, transcendentals=0),
    )[3:]
    a, zpart = _call(
        backward,
        (s0, s1, s2, s3, *states, light, zid),
        (_vmem(2, 32, HIGH, 128), _shape(1, 128)),
        (_vmem(4, HIGH, 128),),
    )
    o0, o1, o2, o3 = _call(last_step, (a, *states, light), (piece,) * 4)
    o2, o1, o3 = _around(o2, 2), _around(o1, 1), _around(o3, 3)
    parts = lax.all_to_all(jnp.broadcast_to(zpart[None], (128, 1, 128)), axes, 0, 0)
    out, total = _call(unpack, (o0, o1, o2, o3, parts), (_shape(32, 32, 128), _shape(NZONE)), (_vmem(8, 128, 128),))
    return out, total


def solution(mesh):
    in_specs = (P("dep", None, "lat"), P(None, "lat"), P(), P("dep", None, "lat"))
    out_specs = (P("dep", None, "lat"), P())
    return jax.shard_map(per_device, mesh=mesh, in_specs=in_specs, out_specs=out_specs, check_vma=False)
```

time: 67.6 us -> 61.3 us (0.907)
  waiting for transfers between devices: 7.93 us -> 1.79 us
  starting transfers between devices: 16.8 us -> 22.7 us
  Pallas kernels: 20.7 us -> 15.9 us
  blocking collectives: 20.8 us -> 19.9 us
    ppermute x9, waiting for transfers between devices: 5.9 us -> 0.02 us  [_around(): return lax.ppermute(x, 'dep', [(s, (s + k) % 4) for s in range(4)])]
    pallas_call x6 -> x9, Pallas kernels: 20.7 us -> 15.9 us  [the longest x7 13.3 us: _call(): pl.pallas_call(kernel, out_shape=tuple(outs), in_specs=[_full()] * len(in...]
    ppermute x2 -> x4, starting transfers between devices: 5.03 us -> 9.16 us  [_swap(): lax.ppermute(x, axes, [pair for a, b in list(zip(places, places[1:], stri...]
    ppermute x9, starting transfers between devices: 11.8 us -> 13.6 us  [_around(): return lax.ppermute(x, 'dep', [(s, (s + k) % 4) for s in range(4)])]
    all_to_all x1, blocking collectives: 20.8 us -> 19.9 us  [per_device(): lax.all_to_all(jnp.broadcast_to(zpart[None], (128, 1, 128)), axes, 0, 0)]
    ppermute x2 -> x4, waiting for transfers between devices: 2.03 us -> 1.77 us  [_swap(): lax.ppermute(x, axes, [pair for a, b in list(zip(places, places[1:], stri...]
  transfers between devices with their start and end apart: 11 -> 13, of which waited for: 3 -> 1; matrix products, arithmetic and copies ran while one was open for 0% -> 0% of each run, Pallas kernels for 13% -> 13%
where the time goes in v4:
time: 61.3 us; the launch traced here: 61.1 us
  starting transfers between devices  22.7 us (37%)
  blocking collectives  19.9 us (32%)
  Pallas kernels  15.9 us (26%)
  waiting for transfers between devices  1.79 us (3%)
  between operations  0.77 us (1%)
    all_to_all x1, blocking collectives, per_device(): lax.all_to_all(jnp.broadcast_to(zpart[None], (128, 1, 128)), axes, 0, 0)  19.9 us
    ppermute x9, starting transfers between devices, _around(): return lax.ppermute(x, 'dep', [(s, (s + k) % 4) for s in range(4)])  13.6 us
    pallas_call x7, Pallas kernels, _call(): pl.pallas_call(kernel, out_shape=tuple(outs), in_specs=[_full()] * len(in...  13.3 us
    ppermute x4, starting transfers between devices, _swap(): lax.ppermute(x, axes, [pair for a, b in list(zip(places, places[1:], stri...  9.16 us
    pallas_call x2, Pallas kernels, _call_hbm(): pl.pallas_call(kernel, out_shape=tuple(outs), in_specs=[pl.BlockSpec(memo...  2.58 us
    ppermute x4, waiting for transfers between devices, _swap(): lax.ppermute(x, axes, [pair for a, b in list(zip(places, places[1:], stri...  1.77 us
  transfers between devices with their start and end apart: 13, of which 1 were waited for; matrix products, arithmetic and copies ran while one was open for 0% of the time, Pallas kernels for 13%

profile of v4, /device:TPU:1, one launch (start us, length us, event | category | flops | bytes accessed | tf_op | source)
XLA Modules:
  0.0 61.1 jit_solution(16892199525993081597)
XLA Ops:
  0.6 1.3 %pack_state.1 = (f32[8,32,128]{2,1,0:T(8,128)S(1)}, f32[8,32,128]{2,1,0:T(8,128)S(1)}, f32[8,32,128]{2,1,0:T(8,128)S(1)}, f32[8,32,128]{2,1,0:T(8,128)S(1)}) custom-call(f32[32,32,128]{2,1,0:T(8,128)} %h_in.1), custom_call_target="tpu_custom_call" | custom-call | tf_op jit(solution)/shard_map/pack_state/pallas_call | solution.py:475
  1.9 2.1 %collective-permute-start.2 = (f32[8,32,128]{2,1,0:T(8,128)S(1)}, f32[8,32,128]{2,1,0:T(8,128)S(1)}, u32[]{:S(2)}, u32[]{:S(2)}) collective-permute-start(f32[8,32,128]{2,1,0:T(8,128)S(1)} %get-tuple-element.47), channel_id=1, source_target_pairs={{0,1},{1,2},{2,3},{3,0},{4,5},{5,6},{6,7},{7,4},{8,9},{9,10},{10,1... | collective-permute-start | bytes 393224 | tf_op jit(solution)/shard_map/ppermute | solution.py:439
  4.0 2.5 %collective-permute-start.3 = (f32[8,32,128]{2,1,0:T(8,128)S(1)}, f32[8,32,128]{2,1,0:T(8,128)S(1)}, u32[]{:S(2)}, u32[]{:S(2)}) collective-permute-start(f32[8,32,128]{2,1,0:T(8,128)S(1)} %get-tuple-element.48), channel_id=1, source_target_pairs={{0,2},{1,3},{2,0},{3,1},{4,6},{5,7},{6,4},{7,5},{8,10},{9,11},{10,... | collective-permute-start | bytes 393224 | tf_op jit(solution)/shard_map/ppermute | solution.py:439
  6.5 1.2 %collective-permute-start.4 = (f32[8,32,128]{2,1,0:T(8,128)S(1)}, f32[8,32,128]{2,1,0:T(8,128)S(1)}, u32[]{:S(2)}, u32[]{:S(2)}) collective-permute-start(f32[8,32,128]{2,1,0:T(8,128)S(1)} %get-tuple-element.49), channel_id=1, source_target_pairs={{0,3},{1,0},{2,1},{3,2},{4,7},{5,4},{6,5},{7,6},{8,11},{9,8},{10,9... | collective-permute-start | bytes 393224 | tf_op jit(solution)/shard_map/ppermute | solution.py:439
  7.6 1.3 %pack_rest.1 = (f32[8,128,128]{2,1,0:T(8,128)S(1)}, f32[4,128,128]{2,1,0:T(8,128)S(1)}, f32[4,32,128]{2,1,0:T(8,128)S(1)}, f32[8,8,128]{2,1,0:T(8,128)S(1)}, f32[8,8,128]{2,1,0:T(8,128)S(1)}) custom-call(f32[16]{0:T(128)} %fluence_in.1, s32[32,128]{1,0:T(8,128)} %zones_in.1, f32[32,32,128]{2,1,0:T(8,128)} %a_in.1), custom_call_target="tpu_custom_call" | custom-call | tf_op jit(solution)/shard_map/pack_rest/pallas_call | solution.py:475
  8.9 1.6 %collective-permute-start = (f32[8,8,128]{2,1,0:T(8,128)S(1)}, f32[8,8,128]{2,1,0:T(8,128)S(1)}, u32[]{:S(2)}, u32[]{:S(2)}) collective-permute-start(f32[8,8,128]{2,1,0:T(8,128)S(1)} %get-tuple-element.43), channel_id=1, source_target_pairs={{0,4},{4,0},{8,12},{12,8},{16,20},{20,16},{24,28},{28,24},{32,36},... | collective-permute-start | bytes 98312 | tf_op jit(solution)/shard_map/ppermute | solution.py:487
  10.5 3.4 %collective-permute-start.1 = (f32[8,8,128]{2,1,0:T(8,128)S(1)}, f32[8,8,128]{2,1,0:T(8,128)S(1)}, u32[]{:S(2)}, u32[]{:S(2)}) collective-permute-start(f32[8,8,128]{2,1,0:T(8,128)S(1)} %get-tuple-element.44), channel_id=1, source_target_pairs={{4,8},{8,4},{12,16},{16,12},{20,24},{24,20},{28,32},{32,28},{36,40... | collective-permute-start | bytes 98312 | tf_op jit(solution)/shard_map/ppermute | solution.py:487
  14.0 0.0 collective-permute-done.inner
  14.0 1.8 %collective-permute-done.1.outer = f32[8,8,128]{2,1,0:T(8,128)S(1)} collective-permute-done((f32[8,8,128]{2,1,0:T(8,128)S(1)}, f32[8,8,128]{2,1,0:T(8,128)S(1)}, u32[]{:S(2)}, u32[]{:S(2)}) %collective-permute-start.1) | collective-permute-done | bytes 32800 | tf_op jit(solution)/shard_map/ppermute | solution.py:487
  15.8 0.0 collective-permute-done.2.r1
  15.8 0.0 collective-permute-done.3.r2
  15.8 0.0 collective-permute-done.4.r3
  15.8 0.2 gather_state.1
  16.0 0.4 collective-permute-start.8
  16.4 3.7 %collective-permute-start.9 = (f32[32,8,128]{2,1,0:T(8,128)S(1)}, f32[32,8,128]{2,1,0:T(8,128)S(1)}, u32[]{:S(2)}, u32[]{:S(2)}) collective-permute-start(f32[32,8,128]{2,1,0:T(8,128)S(1)} %get-tuple-element.60), channel_id=1, source_target_pairs={{1,2},{2,1},{3,7},{7,3},{6,5},{5,6},{4,8},{8,4},{9,10},{10,9},{11,... | collective-permute-start | bytes 393224 | tf_op jit(solution)/shard_map/ppermute | solution.py:487
  20.1 0.1 insert.1
  20.3 0.1 collective-permute-start.5
  20.3 1.2 %collective-permute-start.6 = (f32[8,40,128]{2,1,0:T(8,128)S(1)}, f32[8,40,128]{2,1,0:T(8,128)S(1)}, u32[]{:S(2)}, u32[]{:S(2)}) collective-permute-start(f32[8,40,128]{2,1,0:T(8,128)S(1)} %get-tuple-element.57), channel_id=1, source_target_pairs={{0,2},{1,3},{2,0},{3,1},{4,6},{5,7},{6,4},{7,5},{8,10},{9,11},{10,... | collective-permute-start | bytes 491528 | tf_op jit(solution)/shard_map/ppermute | solution.py:439
  21.5 2.0 %collective-permute-start.7 = (f32[8,40,128]{2,1,0:T(8,128)S(1)}, f32[8,40,128]{2,1,0:T(8,128)S(1)}, u32[]{:S(2)}, u32[]{:S(2)}) collective-permute-start(f32[8,40,128]{2,1,0:T(8,128)S(1)} %get-tuple-element.58), channel_id=1, source_target_pairs={{0,3},{1,0},{2,1},{3,2},{4,7},{5,4},{6,5},{7,6},{8,11},{9,8},{10,9... | collective-permute-start | bytes 491528 | tf_op jit(solution)/shard_map/ppermute | solution.py:439
  23.5 3.6 %forward_core.1 = (f32[32,64,128]{2,1,0:T(8,128)S(1)}, f32[32,64,128]{2,1,0:T(8,128)S(1)}, f32[4,32,64,128]{3,2,1,0:T(8,128)S(1)}, f32[4,32,64,128]{3,2,1,0:T(8,...) custom-call(f32[32,64,128]{2,1,0:T(8,128)S(1)} %get-tuple-element.62.h0.ref, ...), custom_call_target="tpu_custom_call" | custom-call | flops 1000 | bytes 1000 | tf_op jit(solution)/shard_map/forward_core/pallas_call | solution.py:461
  27.1 0.0 collective-permute-done.8.inner
  27.1 0.0 collective-permute-done.9.outer
  27.1 2.6 %forward_sides.1 = (f32[32,64,128]{2,1,0:T(8,128)S(1)}, f32[32,64,128]{2,1,0:T(8,128)S(1)}, f32[32,64,128]{2,1,0:T(8,128)S(1)}, f32[4,32,64,128]{3,2,1,0:T(8,128...) custom-call(f32[32,8,128]{2,1,0:T(8,128)S(1)} %collective-permute-do, ...), custom_call_target="tpu_custom_call", output_to_operand_aliasing={{0}: (3, {}), {1}: (4, {}), {2}: (5, {}), {3}: (6, {}), {4}... | custom-call | flops 10000000000 | bytes 100000000 | tf_op jit(solution)/shard_map/forward_sides/pallas_call | solution.py:461
  29.8 0.0 collective-permute-done.5.r1
  29.8 0.0 collective-permute-done.6.r2
  29.8 0.0 collective-permute-done.7.r3
  29.8 4.6 %backward.1 = (f32[2,32,64,128]{3,2,1,0:T(8,128)S(1)}, f32[1,128]{1,0:T(1,128)S(1)}) custom-call(f32[8,40,128]{2,1,0:T(8,128)S(1)} %get-tuple-element.55.own, f32[8,40,128]{2,1,0:T(8,128)S(1)} %collective-permute-done.5.r1, f32[8,40,128]{2,1,0:T(8,128)S(1)} %collective-permute-done.6.r2, f32[8,40,128]{2,1,0:T(8,128)S(1)} %collective-permute-done.7.r3, ...), custom_call_target="tpu_custom_call" | custom-call | tf_op jit(solution)/shard_map/backward/pallas_call | solution.py:461
  34.4 1.0 %last_step.1 = (f32[8,32,128]{2,1,0:T(8,128)S(1)}, f32[8,32,128]{2,1,0:T(8,128)S(1)}, f32[8,32,128]{2,1,0:T(8,128)S(1)}, f32[8,32,128]{2,1,0:T(8,128)S(1)}) custom-call(f32[2,32,64,128]{3,2,1,0:T(8,128)S(1)} %get-tuple-element.76.a_ref, f32[4,32,64,128]{3,2,1,0:T(8,128)S(1)} %get-tuple-element.70.t_ref, f32[4,32,64,128]{3,2,1,0:T(8,128)S(1)} %get-tuple-element.71.k_ref, ...), custom_call_target="tpu_custom_call" | custom-call | tf_op jit(solution)/shard_map/last_step/pallas_call | solution.py:461
  35.5 1.1 %collective-permute-start.10 = (f32[8,32,128]{2,1,0:T(8,128)S(1)}, f32[8,32,128]{2,1,0:T(8,128)S(1)}, u32[]{:S(2)}, u32[]{:S(2)}) collective-permute-start(f32[8,32,128]{2,1,0:T(8,128)S(1)} %get-tuple-element.78), channel_id=1, source_target_pairs={{0,1},{1,2},{2,3},{3,0},{4,5},{5,6},{6,7},{7,4},{8,9},{9,10},{10,1... | collective-permute-start | bytes 393224 | tf_op jit(solution)/shard_map/ppermute | solution.py:439
  36.6 2.3 %collective-permute-start.11 = (f32[8,32,128]{2,1,0:T(8,128)S(1)}, f32[8,32,128]{2,1,0:T(8,128)S(1)}, u32[]{:S(2)}, u32[]{:S(2)}) collective-permute-start(f32[8,32,128]{2,1,0:T(8,128)S(1)} %get-tuple-element.79), channel_id=1, source_target_pairs={{0,2},{1,3},{2,0},{3,1},{4,6},{5,7},{6,4},{7,5},{8,10},{9,11},{10,... | collective-permute-start | bytes 393224 | tf_op jit(solution)/shard_map/ppermute | solution.py:439
  38.9 1.2 %collective-permute-start.12 = (f32[8,32,128]{2,1,0:T(8,128)S(1)}, f32[8,32,128]{2,1,0:T(8,128)S(1)}, u32[]{:S(2)}, u32[]{:S(2)}) collective-permute-start(f32[8,32,128]{2,1,0:T(8,128)S(1)} %get-tuple-element.80), channel_id=1, source_target_pairs={{0,3},{1,0},{2,1},{3,2},{4,7},{5,4},{6,5},{7,6},{8,11},{9,8},{10,9... | collective-permute-start | bytes 393224 | tf_op jit(solution)/shard_map/ppermute | solution.py:439
  40.1 19.9 %all_to_all.5.parts = f32[128,1,128]{2,1,0:T(1,128)S(1)} all-to-all(f32[128,1,128]{2,1,0:T(1,128)S(1)} %broadcast_in_dim.9), channel_id=1, replica_groups=mesh['lat'=32,'dep'=4] {'lat','dep'}, dimensions={0} | all-to-all | bytes 131072 | tf_op jit(solution)/shard_map/all_to_all | solution.py:550
  60.0 0.0 collective-permute-done.10.r1
  60.0 0.0 collective-permute-done.11.r2
  60.0 0.0 collective-permute-done.12.r3
  60.1 1.1 %unpack.1 = (f32[32,32,128]{2,1,0:T(8,128)}, f32[16]{0:T(128)}) custom-call(f32[8,32,128]{2,1,0:T(8,128)S(1)} %get-tuple-element.77.own, f32[8,32,128]{2,1,0:T(8,128)S(1)} %collective-permute-done.10.r1, f32[8,32,128]{2,1,0:T(8,128)S(1)} %collective-permute-done.11.r2, f32[8,32,128]{2,1,0:T(8,128)S(1)} %collective-permute-done.12.r3, ...), custom_call_target="tpu_custom_call" | custom-call | tf_op jit(solution)/shard_map/unpack/pallas_call | solution.py:461
  (1 shorter events, 0.0 us)
Async XLA Ops:
  1.9 13.8 %collective-permute-start.2 = (f32[8,32,128]{2,1,0:T(8,128)S(1)}, f32[8,32,128]{2,1,0:T(8,128)S(1)}, u32[]{:S(2)}, u32[]{:S(2)}) collective-permute-start(f32[8,32,128]{2,1,0:T(8,128)S(1)} %get-tuple-element.47), channel_id=1, source_target_pairs={{0,1},{1,2},{2,3},{3,0},{4,5},{5,6},{6,7},{7,4},{8,9},{9,10},{10,1... | collective-permute-start | bytes 393224 | tf_op jit(solution)/shard_map/ppermute | solution.py:439
  4.0 11.7 %collective-permute-start.3 = (f32[8,32,128]{2,1,0:T(8,128)S(1)}, f32[8,32,128]{2,1,0:T(8,128)S(1)}, u32[]{:S(2)}, u32[]{:S(2)}) collective-permute-start(f32[8,32,128]{2,1,0:T(8,128)S(1)} %get-tuple-element.48), channel_id=1, source_target_pairs={{0,2},{1,3},{2,0},{3,1},{4,6},{5,7},{6,4},{7,5},{8,10},{9,11},{10,... | collective-permute-start | bytes 393224 | tf_op jit(solution)/shard_map/ppermute | solution.py:439
  6.5 9.3 %collective-permute-start.4 = (f32[8,32,128]{2,1,0:T(8,128)S(1)}, f32[8,32,128]{2,1,0:T(8,128)S(1)}, u32[]{:S(2)}, u32[]{:S(2)}) collective-permute-start(f32[8,32,128]{2,1,0:T(8,128)S(1)} %get-tuple-element.49), channel_id=1, source_target_pairs={{0,3},{1,0},{2,1},{3,2},{4,7},{5,4},{6,5},{7,6},{8,11},{9,8},{10,9... | collective-permute-start | bytes 393224 | tf_op jit(solution)/shard_map/ppermute | solution.py:439
  8.9 5.1 %collective-permute-start = (f32[8,8,128]{2,1,0:T(8,128)S(1)}, f32[8,8,128]{2,1,0:T(8,128)S(1)}, u32[]{:S(2)}, u32[]{:S(2)}) collective-permute-start(f32[8,8,128]{2,1,0:T(8,128)S(1)} %get-tuple-element.43), channel_id=1, source_target_pairs={{0,4},{4,0},{8,12},{12,8},{16,20},{20,16},{24,28},{28,24},{32,36},... | collective-permute-start | bytes 98312 | tf_op jit(solution)/shard_map/ppermute | solution.py:487
  10.5 5.2 %collective-permute-start.1 = (f32[8,8,128]{2,1,0:T(8,128)S(1)}, f32[8,8,128]{2,1,0:T(8,128)S(1)}, u32[]{:S(2)}, u32[]{:S(2)}) collective-permute-start(f32[8,8,128]{2,1,0:T(8,128)S(1)} %get-tuple-element.44), channel_id=1, source_target_pairs={{4,8},{8,4},{12,16},{16,12},{20,24},{24,20},{28,32},{32,28},{36,40... | collective-permute-start | bytes 98312 | tf_op jit(solution)/shard_map/ppermute | solution.py:487
  16.0 11.1 %collective-permute-start.8 = (f32[32,8,128]{2,1,0:T(8,128)S(1)}, f32[32,8,128]{2,1,0:T(8,128)S(1)}, u32[]{:S(2)}, u32[]{:S(2)}) collective-permute-start(f32[32,8,128]{2,1,0:T(8,128)S(1)} %get-tuple-element.59), channel_id=1, source_target_pairs={{0,1},{1,0},{2,3},{3,2},{7,6},{6,7},{5,4},{4,5},{8,9},{9,8},{10,11... | collective-permute-start | bytes 393224 | tf_op jit(solution)/shard_map/ppermute | solution.py:487
  16.4 10.7 %collective-permute-start.9 = (f32[32,8,128]{2,1,0:T(8,128)S(1)}, f32[32,8,128]{2,1,0:T(8,128)S(1)}, u32[]{:S(2)}, u32[]{:S(2)}) collective-permute-start(f32[32,8,128]{2,1,0:T(8,128)S(1)} %get-tuple-element.60), channel_id=1, source_target_pairs={{1,2},{2,1},{3,7},{7,3},{6,5},{5,6},{4,8},{8,4},{9,10},{10,9},{11,... | collective-permute-start | bytes 393224 | tf_op jit(solution)/shard_map/ppermute | solution.py:487
  20.3 9.5 %collective-permute-start.5 = (f32[8,40,128]{2,1,0:T(8,128)S(1)}, f32[8,40,128]{2,1,0:T(8,128)S(1)}, u32[]{:S(2)}, u32[]{:S(2)}) collective-permute-start(f32[8,40,128]{2,1,0:T(8,128)S(1)} %get-tuple-element.56), channel_id=1, source_target_pairs={{0,1},{1,2},{2,3},{3,0},{4,5},{5,6},{6,7},{7,4},{8,9},{9,10},{10,1... | collective-permute-start | bytes 491528 | tf_op jit(solution)/shard_map/ppermute | solution.py:439
  20.3 9.5 %collective-permute-start.6 = (f32[8,40,128]{2,1,0:T(8,128)S(1)}, f32[8,40,128]{2,1,0:T(8,128)S(1)}, u32[]{:S(2)}, u32[]{:S(2)}) collective-permute-start(f32[8,40,128]{2,1,0:T(8,128)S(1)} %get-tuple-element.57), channel_id=1, source_target_pairs={{0,2},{1,3},{2,0},{3,1},{4,6},{5,7},{6,4},{7,5},{8,10},{9,11},{10,... | collective-permute-start | bytes 491528 | tf_op jit(solution)/shard_map/ppermute | solution.py:439
  21.5 8.3 %collective-permute-start.7 = (f32[8,40,128]{2,1,0:T(8,128)S(1)}, f32[8,40,128]{2,1,0:T(8,128)S(1)}, u32[]{:S(2)}, u32[]{:S(2)}) collective-permute-start(f32[8,40,128]{2,1,0:T(8,128)S(1)} %get-tuple-element.58), channel_id=1, source_target_pairs={{0,3},{1,0},{2,1},{3,2},{4,7},{5,4},{6,5},{7,6},{8,11},{9,8},{10,9... | collective-permute-start | bytes 491528 | tf_op jit(solution)/shard_map/ppermute | solution.py:439
  35.5 24.6 %collective-permute-start.10 = (f32[8,32,128]{2,1,0:T(8,128)S(1)}, f32[8,32,128]{2,1,0:T(8,128)S(1)}, u32[]{:S(2)}, u32[]{:S(2)}) collective-permute-start(f32[8,32,128]{2,1,0:T(8,128)S(1)} %get-tuple-element.78), channel_id=1, source_target_pairs={{0,1},{1,2},{2,3},{3,0},{4,5},{5,6},{6,7},{7,4},{8,9},{9,10},{10,1... | collective-permute-start | bytes 393224 | tf_op jit(solution)/shard_map/ppermute | solution.py:439
  36.6 23.5 %collective-permute-start.11 = (f32[8,32,128]{2,1,0:T(8,128)S(1)}, f32[8,32,128]{2,1,0:T(8,128)S(1)}, u32[]{:S(2)}, u32[]{:S(2)}) collective-permute-start(f32[8,32,128]{2,1,0:T(8,128)S(1)} %get-tuple-element.79), channel_id=1, source_target_pairs={{0,2},{1,3},{2,0},{3,1},{4,6},{5,7},{6,4},{7,5},{8,10},{9,11},{10,... | collective-permute-start | bytes 393224 | tf_op jit(solution)/shard_map/ppermute | solution.py:439
  38.9 21.2 %collective-permute-start.12 = (f32[8,32,128]{2,1,0:T(8,128)S(1)}, f32[8,32,128]{2,1,0:T(8,128)S(1)}, u32[]{:S(2)}, u32[]{:S(2)}) collective-permute-start(f32[8,32,128]{2,1,0:T(8,128)S(1)} %get-tuple-element.80), channel_id=1, source_target_pairs={{0,3},{1,0},{2,1},{3,2},{4,7},{5,4},{6,5},{7,6},{8,11},{9,8},{10,9... | collective-permute-start | bytes 393224 | tf_op jit(solution)/shard_map/ppermute | solution.py:439

commit v5 on v4

v5 whole, which is shorter than its diff:
```python
import math

import jax
import jax.numpy as jnp
from jax import lax
from jax.experimental import pallas as pl
from jax.experimental.pallas import tpu as pltpu
from jax.sharding import PartitionSpec as P


NZONE = 16
CORE = 32
HALO = 8
WIDE = CORE + 2 * HALO
SEED_HALO = 4
SEED_WIDE = CORE + 2 * SEED_HALO
BASE = 8
HIGH = WIDE + 2 * BASE
DT = 0.1
ABSORB_SOLID = 0.004
ABSORB_RISE = 0.026
LOG2E = math.log2(math.e)
EM10 = math.exp(-10.0)
F32 = jnp.float32


def _params():
    return pltpu.CompilerParams(vmem_limit_bytes=16 * 1024 * 1024)


def _group(d):
    return jnp.where(lax.rem(lax.axis_index("lat"), 2) == 0, d, 3 - d)


def _columns(d):
    return pl.ds(pl.multiple_of(_group(d) * CORE, CORE), CORE)


def _vmem(*shape):
    return pltpu.VMEM(shape, F32)


def _full():
    return pl.BlockSpec(memory_space=pltpu.VMEM)


def _lanes(rows=8):
    return lax.broadcasted_iota(jnp.int32, (rows, 128), 1)


def _packed(ref, g, d):
    tiles = []
    for p in range(4):
        rf = lax.rem(p + 4 - d, 4)
        tiles += [ref[8 * sub + g, pl.ds(rf, 8, stride=4)] for sub in range(4)]
    return jnp.concatenate(tiles, axis=0).T


def _surface(ref, rf):
    return jnp.concatenate([ref[pl.ds(rf, 8, stride=4)]] * 16, axis=0).T


def pack_state(h_in, h0, h1, h2, h3, h, buf, sem):
    d = lax.axis_index("dep")
    copy = pltpu.make_async_copy(h_in, h, sem)
    copy.start()
    copy.wait()
    for g in range(8):
        buf[g] = _packed(h, g, d)
    for k, out in enumerate((h0, h1, h2, h3)):
        out[...] = buf[:, _columns(lax.rem(d + k, 4))]


def pack_rest(fluence_in, zones_in, a_in, s0, s1, s2, s3, light, zid, a, zones, flat, buf, zbuf, fluence, sems):
    d = lax.axis_index("dep")
    copies = [
        pltpu.make_async_copy(source, target, sems.at[k])
        for k, (source, target) in enumerate(((fluence_in, fluence), (zones_in, zones), (a_in, a)))
    ]
    for copy in copies:
        copy.start()
    copies[0].wait()
    copies[1].wait()
    ids = zones[...]
    intensity = jnp.zeros(ids.shape, F32)
    for k in range(NZONE):
        intensity = jnp.where(ids == k, fluence[k] * DT, intensity)
    flat[0] = intensity
    flat[1] = ids.astype(F32)
    blank = jnp.zeros((BASE + HALO, 128), F32)
    for rf in range(4):
        zbuf[0] = _surface(flat.at[0], rf)
        light[rf, 0 : BASE + HALO] = blank
        light[rf, BASE + HALO : BASE + HALO + CORE] = zbuf[0, _columns(d)]
        light[rf, BASE + HALO + CORE :] = blank
        zbuf[1] = _surface(flat.at[1], rf)
        zid[rf] = zbuf[1, _columns(d)]
    copies[2].wait()
    for g in range(8):
        buf[g] = _packed(a, g, d)
    for k, out in enumerate((s0, s1, s2, s3)):
        out[...] = buf[:, _columns(lax.rem(d + k, 4))]


def _source_masks():
    part = lax.rem(_lanes(8) // 32 + 4 - lax.axis_index("dep"), 4)
    return [part == j for j in range(4)]


def _pick(masks, shift, values):
    return jnp.where(
        masks[shift % 4],
        values[0],
        jnp.where(masks[(shift + 1) % 4], values[1], jnp.where(masks[(shift + 2) % 4], values[2], values[3])),
    )


def _gather(blocks, field, first, count):
    masks = [jnp.broadcast_to(m[0:1], (count, 128)) for m in _source_masks()]
    for g in range(8):
        own, r1, r2, r3 = [block[g] for block in blocks]
        for rf in range(4):
            mixed = _pick(masks, rf, (own, r3, r2, r1))
            field[8 * rf + g, pl.ds(BASE + first, count)] = mixed if rf == 0 else pltpu.roll(mixed, 128 - 32 * rf, 1)


class _Tiles:
    def __init__(self, starts, count, exact):
        self.starts, self.count, self.exact = starts, count, exact
        self.rows = count * len(starts)

    def load(self, ref, *lead, shift=0):
        parts = [ref[(*lead, pl.ds(BASE + start + shift, self.count))] for start in self.starts]
        return parts[0] if len(parts) == 1 else jnp.concatenate(parts, axis=0)

    def store(self, value, ref, *lead):
        for k, start in enumerate(self.starts):
            ref[(*lead, pl.ds(BASE + start, self.count))] = value[k * self.count : (k + 1) * self.count]


def _inclusive(total, lane, reverse):
    a = lax.broadcasted_iota(jnp.int32, (128, 128), 0)
    b = lax.broadcasted_iota(jnp.int32, (128, 128), 1)
    same = lax.rem(a, 8) == lax.rem(b, 8)
    tri = jnp.where(jnp.logical_and(same, a >= b if reverse else a <= b), 1.0, 0.0).astype(jnp.bfloat16)
    high = total.astype(jnp.bfloat16)
    low = (total - high.astype(F32)).astype(jnp.bfloat16)
    return jnp.dot(high, tri, preferred_element_type=F32) + jnp.dot(low, tri, preferred_element_type=F32)


def _properties(n, rf, tiles, states, t_ref, k_ref, c_ref, r_ref, l_ref):
    lane = _lanes(tiles.rows)
    run = jnp.zeros((tiles.rows, 128), F32)
    runs = []
    for g in range(8):
        i = 8 * rf + g
        h = states[g]
        e = jnp.exp2(h * (10.0 * LOG2E) - 10.0 * LOG2E)
        u = 1.0 + e
        v = 1.0 + EM10 * e
        inv = pl.reciprocal(u * v)
        ramp = 0.1 * jnp.log(u * (u * inv))
        t = h - ramp
        m = pl.reciprocal(1.0 + t * t)
        tiles.store(t, t_ref, n, i)
        tiles.store(0.03 + 0.04 * m, k_ref, n, i)
        tiles.store((-0.08 * t) * (m * m), c_ref, n, i)
        tiles.store(e * ((1.0 - EM10) * inv), r_ref, n, i)
        runs.append(run)
        run = run + (ABSORB_SOLID * LOG2E + (ABSORB_RISE * LOG2E) * ramp)
    above = _inclusive(run, lane, False) - run
    for g in range(8):
        tiles.store(jnp.exp2(-(above + runs[g])), l_ref, n, 9 * rf + g)
    tiles.store(jnp.exp2(-(above + run)), l_ref, n, 9 * rf + 8)


def _advance(n, tiles, h_ref, t_ref, k_ref, l_ref, light, then):
    lane = _lanes(tiles.rows)
    inside = lax.rem(lane, 8) < 7
    above_bottom = lane < 120

    def across(g):
        t3, k3 = tiles.load(t_ref, n, 24 + g), tiles.load(k_ref, n, 24 + g)
        t0, k0 = pltpu.roll(tiles.load(t_ref, n, g), 127, 1), pltpu.roll(tiles.load(k_ref, n, g), 127, 1)
        return jnp.where(inside, (k3 + k0) * (t0 - t3), 0.0)

    last = [across(g) for g in range(8)]
    before = [pltpu.roll(f, 1, 1) for f in last]
    for rf in range(4):
        i0 = 8 * rf
        t = [tiles.load(t_ref, n, i0 + g) for g in range(8)]
        k = [tiles.load(k_ref, n, i0 + g) for g in range(8)]
        end = jnp.where(above_bottom, (k[7] + pltpu.roll(k[0], 120, 1)) * (pltpu.roll(t[0], 120, 1) - t[7]), 0.0)
        flux_before = pltpu.roll(end, 8, 1)
        new = []
        for g in range(8):
            i = i0 + g
            if g < 7:
                flux = (k[g] + k[g + 1]) * (t[g + 1] - t[g])
            else:
                flux = jnp.where(above_bottom, end, -0.05 * t[7])
            if rf < 3:
                side = (k[g] + tiles.load(k_ref, n, i + 8)) * (tiles.load(t_ref, n, i + 8) - t[g])
            else:
                side = last[g]
            change = (flux - flux_before) + (side - before[g])
            col = (k[g] + tiles.load(k_ref, n, i, shift=1)) * (tiles.load(t_ref, n, i, shift=1) - t[g])
            if tiles.exact:
                col_before = (tiles.load(k_ref, n, i, shift=-1) + k[g]) * (t[g] - tiles.load(t_ref, n, i, shift=-1))
            else:
                col_before = pltpu.roll(col, 1, 0)
            change = change + (col - col_before)
            source = tiles.load(light, rf) * (tiles.load(l_ref, n, 9 * rf + g) - tiles.load(l_ref, n, 9 * rf + g + 1))
            new.append(tiles.load(h_ref, i) + (change + source))
            flux_before, before[g] = flux, side
        then(rf, new)


def _ghost(ref_rows):
    lat, group = lax.axis_index("lat"), _group(lax.axis_index("dep"))

    @pl.when(jnp.logical_and(lat == 0, group == 0))
    def _():
        for i in range(32):
            ref_rows(i, HALO - 1)[...] = ref_rows(i, HALO)[...]

    @pl.when(jnp.logical_and(lat == 31, group == 3))
    def _():
        for i in range(32):
            ref_rows(i, HALO + CORE)[...] = ref_rows(i, HALO + CORE - 1)[...]


def gather_state(own, r1, r2, r3, h0):
    _gather((own, r1, r2, r3), h0, HALO, CORE)


def gather_seed(own, r1, r2, r3, h0, light, a_ref, to_inner, to_outer, edges):
    _gather((own, r1, r2, r3), a_ref.at[0], HALO, CORE)
    for side, first, seed_first in ((0, HALO, HALO), (1, CORE, HALO + CORE - SEED_HALO)):
        edges[side, 0:32] = h0[:, BASE + first : BASE + first + HALO]
        for i in range(32):
            edges[side, 32 + i // 2, pl.ds(4 * (i % 2), 4)] = a_ref[0, i, pl.ds(BASE + seed_first, SEED_HALO)]
        edges[side, 48:52] = light[:, BASE + first : BASE + first + HALO]
    odd = lax.rem(_group(lax.axis_index("dep")), 2)
    to_inner[...] = edges[1 - odd]
    to_outer[...] = edges[odd]


def forward_core(h0, light, h1, h2, t_ref, k_ref, c_ref, r_ref, l_ref):
    fields = (t_ref, k_ref, c_ref, r_ref, l_ref)
    tiles = _Tiles((HALO,), CORE, False)
    for rf in range(4):
        _properties(0, rf, tiles, [tiles.load(h0, 8 * rf + g) for g in range(8)], *fields)
    for n, source, target in ((0, h0, h1), (1, h1, h2), (2, h2, None)):

        def then(rf, new, n=n, target=target):
            if target is not None:
                for g in range(8):
                    tiles.store(new[g], target, 8 * rf + g)
            _properties(n + 1, rf, tiles, new, *fields)

        _advance(n, tiles, source, t_ref, k_ref, l_ref, light, then)


def _retreat(n, tiles, a_ref, t_ref, k_ref, c_ref, r_ref, l_ref, light, put):
    lane = _lanes(tiles.rows)
    inside = lax.rem(lane, 8) < 7
    above_bottom = lane < 120

    def across(g):
        a3, t3, k3 = tiles.load(a_ref, 24 + g), tiles.load(t_ref, n, 24 + g), tiles.load(k_ref, n, 24 + g)
        a0, t0, k0 = [pltpu.roll(x, 127, 1) for x in (tiles.load(a_ref, g), tiles.load(t_ref, n, g), tiles.load(k_ref, n, g))]
        jump = jnp.where(inside, a3 - a0, 0.0)
        return jump * (k3 + k0), jump * (t0 - t3)

    last = [across(g) for g in range(8)]
    before = [(pltpu.roll(push, 1, 1), pltpu.roll(share, 1, 1)) for push, share in last]
    for rf in range(4):
        i0 = 8 * rf
        a = [tiles.load(a_ref, i0 + g) for g in range(8)]
        t = [tiles.load(t_ref, n, i0 + g) for g in range(8)]
        k = [tiles.load(k_ref, n, i0 + g) for g in range(8)]
        run = jnp.zeros((tiles.rows, 128), F32)
        runs = [None] * 8
        for g in reversed(range(8)):
            runs[g] = run
            run = run + a[g] * (tiles.load(l_ref, n, 9 * rf + g) - tiles.load(l_ref, n, 9 * rf + g + 1))
        below = _inclusive(run, lane, True) - run
        gain = ABSORB_RISE * tiles.load(light, rf)
        jump = jnp.where(above_bottom, a[7] - pltpu.roll(a[0], 120, 1), 0.0)
        push_end = jump * (k[7] + pltpu.roll(k[0], 120, 1))
        share_end = jump * (pltpu.roll(t[0], 120, 1) - t[7])
        push_before, share_before = pltpu.roll(push_end, 8, 1), pltpu.roll(share_end, 8, 1)
        for g in range(8):
            i = i0 + g
            if g < 7:
                jump = a[g] - a[g + 1]
                push, share = jump * (k[g] + k[g + 1]), jump * (t[g + 1] - t[g])
            else:
                push, share = jnp.where(above_bottom, push_end, 0.05 * a[7]), share_end
            if rf < 3:
                jump = a[g] - tiles.load(a_ref, i + 8)
                push_r, share_r = jump * (k[g] + tiles.load(k_ref, n, i + 8)), jump * (tiles.load(t_ref, n, i + 8) - t[g])
            else:
                push_r, share_r = last[g]
            grad_t = (push_before - push) + (before[g][0] - push_r)
            grad_k = (share_before + share) + (before[g][1] + share_r)
            jump = a[g] - tiles.load(a_ref, i, shift=1)
            push_c, share_c = jump * (k[g] + tiles.load(k_ref, n, i, shift=1)), jump * (tiles.load(t_ref, n, i, shift=1) - t[g])
            if tiles.exact:
                jump = tiles.load(a_ref, i, shift=-1) - a[g]
                push_d, share_d = jump * (tiles.load(k_ref, n, i, shift=-1) + k[g]), jump * (t[g] - tiles.load(t_ref, n, i, shift=-1))
            else:
                push_d, share_d = pltpu.roll(push_c, 1, 0), pltpu.roll(share_c, 1, 0)
            grad_t = grad_t + (push_d - push_c)
            grad_k = grad_k + (share_d + share_c)
            heat = grad_t + tiles.load(c_ref, n, i) * grad_k
            absorbed = gain * (a[g] * tiles.load(l_ref, n, 9 * rf + g + 1) - (below + runs[g]))
            put(i, a[g] + (heat + tiles.load(r_ref, n, i) * (absorbed - heat)))
            push_before, share_before, before[g] = push, share, (push_r, share_r)


def backward_core(a_in, t_ref, k_ref, c_ref, r_ref, l_ref, light, a_ref):
    tiles = _Tiles((HALO,), CORE, False)

    def step(i, carry):
        def put(j, value):
            tiles.store(value, a_ref, i + 1, j)

        _retreat(3 - i, tiles, a_ref.at[i], t_ref, k_ref, c_ref, r_ref, l_ref, light, put)
        return carry

    lax.fori_loop(0, 3, step, 0)


def sides(inner, outer, zid, *refs):
    zpart, h0, h1, h2, t_ref, k_ref, c_ref, r_ref, l_ref, light, a_ref = refs[10:]
    fields = (t_ref, k_ref, c_ref, r_ref, l_ref)
    even = lax.rem(_group(lax.axis_index("dep")), 2) == 0

    def place(left, right):
        for edge, first, seed_first in ((left, 0, SEED_HALO), (right, HALO + CORE, HALO + CORE)):
            h0[:, BASE + first : BASE + first + HALO] = edge[0:32]
            for i in range(32):
                a_ref[0, i, pl.ds(BASE + seed_first, SEED_HALO)] = edge[32 + i // 2, pl.ds(4 * (i % 2), 4)]
            light[:, BASE + first : BASE + first + HALO] = edge[48:52]

    @pl.when(even)
    def _():
        place(outer, inner)

    @pl.when(jnp.logical_not(even))
    def _():
        place(inner, outer)

    tiles = _Tiles((0, HALO + CORE), HALO, True)
    for rf in range(4):
        _properties(0, rf, tiles, [tiles.load(h0, 8 * rf + g) for g in range(8)], *fields)
    for n, source, target in ((0, h0, h1), (1, h1, h2), (2, h2, None)):
        _ghost(lambda i, c, n=n: t_ref.at[n, i, pl.ds(BASE + c, 1)])
        tiles = _Tiles((n + 1, HALO + CORE - 1 - n), HALO, True)

        def then(rf, new, n=n, target=target, tiles=tiles):
            if target is not None:
                for g in range(8):
                    tiles.store(new[g], target, 8 * rf + g)
            _properties(n + 1, rf, tiles, new, *fields)

        _advance(n, tiles, source, t_ref, k_ref, l_ref, light, then)
    for m in range(3):
        _ghost(lambda i, c, m=m: a_ref.at[m, i, pl.ds(BASE + c, 1)])
        tiles = _Tiles((SEED_HALO + m, HALO + CORE - SEED_HALO - m), HALO, True)

        def put(j, value, m=m, tiles=tiles):
            tiles.store(value, a_ref, m + 1, j)

        _retreat(3 - m, tiles, a_ref.at[m], *fields, light, put)
    _ghost(lambda i, c: a_ref.at[3, i, pl.ds(BASE + c, 1)])
    core = pl.ds(BASE + HALO, CORE)
    rows = []
    sums = []
    for rf in range(4):
        value = jnp.zeros((CORE, 128), F32)
        for n in range(4):
            for g in range(8):
                lost = l_ref[n, 9 * rf + g, core] - l_ref[n, 9 * rf + g + 1, core]
                value = value + a_ref[3 - n, 8 * rf + g, core] * lost
        sums.append(value * DT)
    for z in range(NZONE):
        picked = [jnp.where(zid[rf] == float(z), sums[rf], 0.0) for rf in range(4)]
        rows.append(jnp.sum((picked[0] + picked[1]) + (picked[2] + picked[3]), axis=0, keepdims=True))
    spread = jnp.concatenate(rows + [jnp.zeros((128 - NZONE, 128), F32)], axis=0)
    zpart[...] = jnp.sum(spread.T, axis=0, keepdims=True)


def last_step(a_ref, t_ref, k_ref, c_ref, r_ref, l_ref, light, o0, o1, o2, o3):
    masks = [jnp.broadcast_to(m[0:1], (CORE, 128)) for m in _source_masks()]
    values = [None] * 32

    def put(i, value):
        values[i] = value

    tiles = _Tiles((HALO,), CORE, True)
    _retreat(0, tiles, a_ref.at[3], t_ref, k_ref, c_ref, r_ref, l_ref, light, put)
    for g in range(8):
        turned = [values[g]] + [pltpu.roll(values[8 * rf + g], 32 * rf, 1) for rf in (1, 2, 3)]
        for k, out in enumerate((o0, o1, o2, o3)):
            out[g] = _pick(masks, k, turned)


def unpack(own, r1, r2, r3, parts, out, total, buf):
    d = lax.axis_index("dep")
    for k, block in enumerate((own, r1, r2, r3)):
        buf[:, _columns(lax.rem(d + 4 - k, 4))] = block[...]
    for g in range(8):
        plain = buf[g].T
        for p in range(4):
            rf = lax.rem(p + 4 - d, 4)
            for sub in range(4):
                out[8 * sub + g, pl.ds(rf, 8, stride=4)] = plain[32 * p + 8 * sub : 32 * p + 8 * sub + 8]
    total[...] = jnp.sum(parts[...], axis=(0, 1))[:NZONE]


def _around(x, k):
    return lax.ppermute(x, "dep", [(s, (s + k) % 4) for s in range(4)])


def _place(y, z, core, x):
    return ((y * 4 + z) * 2 + core) * 4 + x


def _meet(v, partner):
    pairs = []
    for y in range(4):
        for z in range(4):
            for core in range(2):
                for x in range(4):
                    pairs.append((_place(y, z, core, x), _place(*partner(y, z, core, x))))
    return v + lax.ppermute(v, ("lat", "dep"), pairs)


def _shape(*dims):
    return jax.ShapeDtypeStruct(dims, F32)


def _call(kernel, inputs, outs, scratch=(), aliases=None, cost=None):
    return pl.pallas_call(
        kernel,
        out_shape=tuple(outs),
        in_specs=[_full()] * len(inputs),
        out_specs=(_full(),) * len(outs),
        scratch_shapes=list(scratch),
        input_output_aliases=aliases or {},
        cost_estimate=cost,
        compiler_params=_params(),
        name=kernel.__name__,
    )(*inputs)


def _call_hbm(kernel, inputs, outs, scratch):
    return pl.pallas_call(
        kernel,
        out_shape=tuple(outs),
        in_specs=[pl.BlockSpec(memory_space=pltpu.HBM)] * len(inputs),
        out_specs=(_full(),) * len(outs),
        scratch_shapes=list(scratch),
        compiler_params=_params(),
        name=kernel.__name__,
    )(*[pltpu.with_memory_space_constraint(x, pltpu.HBM) for x in inputs])


def _swap(x, axes, places, first):
    return lax.ppermute(
        x, axes, [pair for a, b in list(zip(places, places[1:], strict=False))[first::2] for pair in ((a, b), (b, a))]
    )


def per_device(h, zones, fluence, seed):
    piece = _shape(8, CORE, 128)
    h0, h1, h2, h3 = _call_hbm(
        pack_state, (h,), (piece,) * 4, (_vmem(32, 32, 128), _vmem(8, 128, 128), pltpu.SemaphoreType.DMA)
    )
    h2, h1, h3 = _around(h2, 2), _around(h1, 1), _around(h3, 3)
    surface = _vmem(4, HIGH, 128)
    s0, s1, s2, s3, light, zid = _call_hbm(
        pack_rest,
        (fluence, zones, seed),
        (piece,) * 4 + (surface, _shape(4, CORE, 128)),
        (
            _vmem(32, 32, 128),
            pltpu.VMEM((32, 128), jnp.int32),
            _vmem(2, 32, 128),
            _vmem(8, 128, 128),
            _vmem(2, 128, 128),
            pltpu.SMEM((NZONE,), F32),
            pltpu.SemaphoreType.DMA((3,)),
        ),
    )
    s2, s1, s3 = _around(s2, 2), _around(s1, 1), _around(s3, 3)
    one, four = _vmem(32, HIGH, 128), _vmem(4, 32, HIGH, 128)
    fields = (one, one, four, four, four, four, _vmem(4, 36, HIGH, 128))
    (state,) = _call(gather_state, (h0, h1, h2, h3), (one,))
    states = _call(forward_core, (state, light), fields)
    edge = _shape(52, HALO, 128)
    s0, light, *states = lax.optimization_barrier((s0, light, *states))
    a, to_inner, to_outer = _call(
        gather_seed, (s0, s1, s2, s3, state, light), (four, edge, edge), (_vmem(2, 52, HALO, 128),)
    )
    axes = ("lat", "dep")
    line = [4 * l + (c if l % 2 == 0 else 3 - c) for l in range(32) for c in range(4)]
    outer, inner = _swap(to_outer, axes, line, 1), _swap(to_inner, axes, line, 0)
    (a,) = _call(backward_core, (a, *states[2:], light), (four,), (), {0: 0})
    zpart, *states = _call(
        sides,
        (inner, outer, zid, state, *states, light, a),
        (_shape(1, 128), one) + fields + (surface, four),
        (),
        {3 + i: 1 + i for i in range(10)},
    )
    o0, o1, o2, o3 = _call(last_step, (states[9], *states[3:9]), (piece,) * 4)
    o2, o1, o3 = _around(o2, 2), _around(o1, 1), _around(o3, 3)
    parts = lax.all_to_all(jnp.broadcast_to(zpart[None], (128, 1, 128)), axes, 0, 0)
    out, total = _call(unpack, (o0, o1, o2, o3, parts), (_shape(32, 32, 128), _shape(NZONE)), (_vmem(8, 128, 128),))
    return out, total


def solution(mesh):
    in_specs = (P("dep", None, "lat"), P(None, "lat"), P(), P("dep", None, "lat"))
    out_specs = (P("dep", None, "lat"), P())
    return jax.shard_map(per_device, mesh=mesh, in_specs=in_specs, out_specs=out_specs, check_vma=False)
```

time: 61.3 us -> 60 us (0.979)
  starting transfers between devices: 22.7 us -> 18.1 us
  Pallas kernels: 15.9 us -> 18 us
  blocking collectives: 19.9 us -> 20.6 us
    ppermute x4 -> x2, starting transfers between devices: 9.16 us -> 6.38 us  [_swap(): lax.ppermute(x, axes, [pair for a, b in list(zip(places, places[1:], stri...]
    pallas_call x7, Pallas kernels: 13.3 us -> 15.4 us  [_call(): pl.pallas_call(kernel, out_shape=tuple(outs), in_specs=[_full()] * len(in...]
    ppermute x9, waiting for transfers between devices: 0.02 us -> 2.01 us  [_around(): return lax.ppermute(x, 'dep', [(s, (s + k) % 4) for s in range(4)])]
    ppermute x9, starting transfers between devices: 13.6 us -> 11.7 us  [_around(): return lax.ppermute(x, 'dep', [(s, (s + k) % 4) for s in range(4)])]
    ppermute x4 -> x2, waiting for transfers between devices: 1.77 us -> 0.32 us  [_swap(): lax.ppermute(x, axes, [pair for a, b in list(zip(places, places[1:], stri...]
    all_to_all x1, blocking collectives: 19.9 us -> 20.6 us  [per_device(): lax.all_to_all(jnp.broadcast_to(zpart[None], (128, 1, 128)), axes, 0, 0)]
  transfers between devices with their start and end apart: 13 -> 11, of which waited for: 1 -> 3; matrix products, arithmetic and copies ran while one was open for 0% -> 0% of each run, Pallas kernels for 13% -> 14%
where the time goes in v5:
time: 60 us; the launch traced here: 59.8 us
  blocking collectives  20.6 us (34%)
  starting transfers between devices  18.1 us (30%)
  Pallas kernels  18 us (30%)
  waiting for transfers between devices  2.34 us (4%)
  between operations  0.73 us (1%)
    all_to_all x1, blocking collectives, per_device(): lax.all_to_all(jnp.broadcast_to(zpart[None], (128, 1, 128)), axes, 0, 0)  20.6 us
    pallas_call x7, Pallas kernels, _call(): pl.pallas_call(kernel, out_shape=tuple(outs), in_specs=[_full()] * len(in...  15.4 us
    ppermute x9, starting transfers between devices, _around(): return lax.ppermute(x, 'dep', [(s, (s + k) % 4) for s in range(4)])  11.7 us
    ppermute x2, starting transfers between devices, _swap(): lax.ppermute(x, axes, [pair for a, b in list(zip(places, places[1:], stri...  6.38 us
    pallas_call x2, Pallas kernels, _call_hbm(): pl.pallas_call(kernel, out_shape=tuple(outs), in_specs=[pl.BlockSpec(memo...  2.61 us
    ppermute x9, waiting for transfers between devices, _around(): return lax.ppermute(x, 'dep', [(s, (s + k) % 4) for s in range(4)])  2.01 us
  transfers between devices with their start and end apart: 11, of which 3 were waited for; matrix products, arithmetic and copies ran while one was open for 0% of the time, Pallas kernels for 14%

profile of v5, /device:TPU:1, one launch (start us, length us, event | category | flops | bytes accessed | tf_op | source)
XLA Modules:
  0.0 59.8 jit_solution(3733094758458864339)
XLA Ops:
  0.6 1.3 %pack_state.1 = (f32[8,32,128]{2,1,0:T(8,128)S(1)}, f32[8,32,128]{2,1,0:T(8,128)S(1)}, f32[8,32,128]{2,1,0:T(8,128)S(1)}, f32[8,32,128]{2,1,0:T(8,128)S(1)}) custom-call(f32[32,32,128]{2,1,0:T(8,128)} %h_in.1), custom_call_target="tpu_custom_call" | custom-call | tf_op jit(solution)/shard_map/pack_state/pallas_call | solution.py:461
  1.9 2.1 %collective-permute-start = (f32[8,32,128]{2,1,0:T(8,128)S(1)}, f32[8,32,128]{2,1,0:T(8,128)S(1)}, u32[]{:S(2)}, u32[]{:S(2)}) collective-permute-start(f32[8,32,128]{2,1,0:T(8,128)S(1)} %get-tuple-element.46), channel_id=1, source_target_pairs={{0,1},{1,2},{2,3},{3,0},{4,5},{5,6},{6,7},{7,4},{8,9},{9,10},{10,1... | collective-permute-start | bytes 393224 | tf_op jit(solution)/shard_map/ppermute | solution.py:425
  4.0 2.5 %collective-permute-start.1 = (f32[8,32,128]{2,1,0:T(8,128)S(1)}, f32[8,32,128]{2,1,0:T(8,128)S(1)}, u32[]{:S(2)}, u32[]{:S(2)}) collective-permute-start(f32[8,32,128]{2,1,0:T(8,128)S(1)} %get-tuple-element.47), channel_id=1, source_target_pairs={{0,2},{1,3},{2,0},{3,1},{4,6},{5,7},{6,4},{7,5},{8,10},{9,11},{10,... | collective-permute-start | bytes 393224 | tf_op jit(solution)/shard_map/ppermute | solution.py:425
  6.5 1.2 %collective-permute-start.2 = (f32[8,32,128]{2,1,0:T(8,128)S(1)}, f32[8,32,128]{2,1,0:T(8,128)S(1)}, u32[]{:S(2)}, u32[]{:S(2)}) collective-permute-start(f32[8,32,128]{2,1,0:T(8,128)S(1)} %get-tuple-element.48), channel_id=1, source_target_pairs={{0,3},{1,0},{2,1},{3,2},{4,7},{5,4},{6,5},{7,6},{8,11},{9,8},{10,9... | collective-permute-start | bytes 393224 | tf_op jit(solution)/shard_map/ppermute | solution.py:425
  7.6 1.3 %pack_rest.1 = (f32[8,32,128]{2,1,0:T(8,128)S(1)}, f32[8,32,128]{2,1,0:T(8,128)S(1)}, f32[8,32,128]{2,1,0:T(8,128)S(1)}, f32[8,32,128]{2,1,0:T(8,128)S(1)}, f32[...) custom-call(f32[16]{0:T(128)} %fluence_in.1, s32[32,128]{1,0:T(8,128)} %zones_in.1, f32[32,32,128]{2,1,0:T(8,128)} %a_in.1), custom_call_target="tpu_custom_call" | custom-call | tf_op jit(solution)/shard_map/pack_rest/pallas_call | solution.py:461
  9.0 0.4 collective-permute-start.3
  9.4 0.9 %collective-permute-start.4 = (f32[8,32,128]{2,1,0:T(8,128)S(1)}, f32[8,32,128]{2,1,0:T(8,128)S(1)}, u32[]{:S(2)}, u32[]{:S(2)}) collective-permute-start(f32[8,32,128]{2,1,0:T(8,128)S(1)} %get-tuple-element.58), channel_id=1, source_target_pairs={{0,2},{1,3},{2,0},{3,1},{4,6},{5,7},{6,4},{7,5},{8,10},{9,11},{10,... | collective-permute-start | bytes 393224 | tf_op jit(solution)/shard_map/ppermute | solution.py:425
  10.2 0.0 collective-permute-done.r1
  10.2 1.6 %collective-permute-start.5 = (f32[8,32,128]{2,1,0:T(8,128)S(1)}, f32[8,32,128]{2,1,0:T(8,128)S(1)}, u32[]{:S(2)}, u32[]{:S(2)}) collective-permute-start(f32[8,32,128]{2,1,0:T(8,128)S(1)} %get-tuple-element.59), channel_id=1, source_target_pairs={{0,3},{1,0},{2,1},{3,2},{4,7},{5,4},{6,5},{7,6},{8,11},{9,8},{10,9... | collective-permute-start | bytes 393224 | tf_op jit(solution)/shard_map/ppermute | solution.py:425
  11.8 0.4 collective-permute-done.1.r2
  12.2 0.0 collective-permute-done.2.r3
  12.2 0.2 gather_state.1.h0.refs_0_
  12.4 3.8 %forward_core.1 = (f32[32,64,128]{2,1,0:T(8,128)S(1)}, f32[32,64,128]{2,1,0:T(8,128)S(1)}, f32[4,32,64,128]{3,2,1,0:T(8,128)S(1)}, f32[4,32,64,128]{3,2,1,0:T(8,...) custom-call(f32[32,64,128]{2,1,0:T(8,128)S(1)} %gather_state.1.h0.refs_0_, ...), custom_call_target="tpu_custom_call" | custom-call | tf_op jit(solution)/shard_map/forward_core/pallas_call | solution.py:447
  16.2 0.0 collective-permute-done.3.r1
  16.2 1.6 %collective-permute-done.4.r2 = f32[8,32,128]{2,1,0:T(8,128)S(1)} collective-permute-done((f32[8,32,128]{2,1,0:T(8,128)S(1)}, f32[8,32,128]{2,1,0:T(8,128)S(1)}, u32[]{:S(2)}, u32[]{:S(2)}) %collective-permute-start.4) | collective-permute-done | bytes 131104 | tf_op jit(solution)/shard_map/ppermute | solution.py:425
  17.8 0.0 collective-permute-done.5.r3
  17.8 0.3 gather_seed.1
  18.1 0.1 collective-permute-start.6
  18.2 6.2 %collective-permute-start.7 = (f32[52,8,128]{2,1,0:T(8,128)S(1)}, f32[52,8,128]{2,1,0:T(8,128)S(1)}, u32[]{:S(2)}, u32[]{:S(2)}) collective-permute-start(f32[52,8,128]{2,1,0:T(8,128)S(1)} %get-tuple-element.62), channel_id=1, source_target_pairs={{1,2},{2,1},{3,7},{7,3},{6,5},{5,6},{4,8},{8,4},{9,10},{10,9},{11,... | collective-permute-start | bytes 638984 | tf_op jit(solution)/shard_map/ppermute | solution.py:473
  24.5 3.2 %backward_core.1.refs_9_ = f32[4,32,64,128]{3,2,1,0:T(8,128)S(1)} custom-call(f32[4,32,64,128]{3,2,1,0:T(8,128)S(1)} %get-tuple-element.71.a_in, f32[4,32,64,128]{3,2,1,0:T(8,128)S(1)} %get-tuple-element.66.t_ref.refs_3_, f32[4,32,64,128]{3,2,1,0:T(8,128)S(1)} %get-tuple-element.67.k_ref.refs_4_, ...), custom_call_target="tpu_custom_call", output_to_operand_aliasing={{}: (0, {})} | custom-call | tf_op jit(solution)/shard_map/backward_core/pallas_call | solution.py:447
  27.6 0.0 collective-permute-done.6.inner
  27.7 0.3 collective-permute-done.7.outer
  28.0 5.6 %sides.1 = (f32[1,128]{1,0:T(1,128)S(1)}, f32[32,64,128]{2,1,0:T(8,128)S(1)}, f32[32,64,128]{2,1,0:T(8,128)S(1)}, f32[32,64,128]{2,1,0:T(8,128)S(1)}, f32[4,32,6...) custom-call(f32[52,8,128]{2,1,0:T(8,128)S(1)} %collective-permute-do, ...), custom_call_target="tpu_custom_call", output_to_operand_aliasing={{1}: (3, {}), {2}: (4, {}), {3}: (5, {}), {4}: (6, {}), {5}... | custom-call | tf_op jit(solution)/shard_map/sides/pallas_call | solution.py:447
  33.6 1.3 %last_step.1 = (f32[8,32,128]{2,1,0:T(8,128)S(1)}, f32[8,32,128]{2,1,0:T(8,128)S(1)}, f32[8,32,128]{2,1,0:T(8,128)S(1)}, f32[8,32,128]{2,1,0:T(8,128)S(1)}) custom-call(f32[4,32,64,128]{3,2,1,0:T(8,128)S(1)} %get-tuple-element.72.a_ref, f32[4,32,64,128]{3,2,1,0:T(8,128)S(1)} %get-tuple-element.73.t_ref, f32[4,32,64,128]{3,2,1,0:T(8,128)S(1)} %get-tuple-element.74.k_ref, ...), custom_call_target="tpu_custom_call" | custom-call | tf_op jit(solution)/shard_map/last_step/pallas_call | solution.py:447
  34.9 0.1 collective-permute-start.8
  35.0 1.1 %collective-permute-start.9 = (f32[8,32,128]{2,1,0:T(8,128)S(1)}, f32[8,32,128]{2,1,0:T(8,128)S(1)}, u32[]{:S(2)}, u32[]{:S(2)}) collective-permute-start(f32[8,32,128]{2,1,0:T(8,128)S(1)} %get-tuple-element.81), channel_id=1, source_target_pairs={{0,2},{1,3},{2,0},{3,1},{4,6},{5,7},{6,4},{7,5},{8,10},{9,11},{10,... | collective-permute-start | bytes 393224 | tf_op jit(solution)/shard_map/ppermute | solution.py:425
  36.1 2.0 %collective-permute-start.10 = (f32[8,32,128]{2,1,0:T(8,128)S(1)}, f32[8,32,128]{2,1,0:T(8,128)S(1)}, u32[]{:S(2)}, u32[]{:S(2)}) collective-permute-start(f32[8,32,128]{2,1,0:T(8,128)S(1)} %get-tuple-element.82), channel_id=1, source_target_pairs={{0,3},{1,0},{2,1},{3,2},{4,7},{5,4},{6,5},{7,6},{8,11},{9,8},{10,9... | collective-permute-start | bytes 393224 | tf_op jit(solution)/shard_map/ppermute | solution.py:425
  38.1 20.6 %all_to_all.5.parts = f32[128,1,128]{2,1,0:T(1,128)S(1)} all-to-all(f32[128,1,128]{2,1,0:T(1,128)S(1)} %broadcast_in_dim.9), channel_id=1, replica_groups=mesh['lat'=32,'dep'=4] {'lat','dep'}, dimensions={0} | all-to-all | bytes 131072 | tf_op jit(solution)/shard_map/all_to_all | solution.py:522
  58.7 0.0 collective-permute-done.8.r1
  58.7 0.0 collective-permute-done.9.r2
  58.7 0.0 collective-permute-done.10.r3
  58.7 1.1 %unpack.1 = (f32[32,32,128]{2,1,0:T(8,128)}, f32[16]{0:T(128)}) custom-call(f32[8,32,128]{2,1,0:T(8,128)S(1)} %get-tuple-element.79.own, f32[8,32,128]{2,1,0:T(8,128)S(1)} %collective-permute-done.8.r1, f32[8,32,128]{2,1,0:T(8,128)S(1)} %collective-permute-done.9.r2, f32[8,32,128]{2,1,0:T(8,128)S(1)} %collective-permute-done.10.r3, ...), custom_call_target="tpu_custom_call" | custom-call | tf_op jit(solution)/shard_map/unpack/pallas_call | solution.py:447
  (1 shorter events, 0.0 us)
Async XLA Ops:
  1.9 8.3 %collective-permute-start = (f32[8,32,128]{2,1,0:T(8,128)S(1)}, f32[8,32,128]{2,1,0:T(8,128)S(1)}, u32[]{:S(2)}, u32[]{:S(2)}) collective-permute-start(f32[8,32,128]{2,1,0:T(8,128)S(1)} %get-tuple-element.46), channel_id=1, source_target_pairs={{0,1},{1,2},{2,3},{3,0},{4,5},{5,6},{6,7},{7,4},{8,9},{9,10},{10,1... | collective-permute-start | bytes 393224 | tf_op jit(solution)/shard_map/ppermute | solution.py:425
  4.0 8.2 %collective-permute-start.1 = (f32[8,32,128]{2,1,0:T(8,128)S(1)}, f32[8,32,128]{2,1,0:T(8,128)S(1)}, u32[]{:S(2)}, u32[]{:S(2)}) collective-permute-start(f32[8,32,128]{2,1,0:T(8,128)S(1)} %get-tuple-element.47), channel_id=1, source_target_pairs={{0,2},{1,3},{2,0},{3,1},{4,6},{5,7},{6,4},{7,5},{8,10},{9,11},{10,... | collective-permute-start | bytes 393224 | tf_op jit(solution)/shard_map/ppermute | solution.py:425
  6.5 5.7 %collective-permute-start.2 = (f32[8,32,128]{2,1,0:T(8,128)S(1)}, f32[8,32,128]{2,1,0:T(8,128)S(1)}, u32[]{:S(2)}, u32[]{:S(2)}) collective-permute-start(f32[8,32,128]{2,1,0:T(8,128)S(1)} %get-tuple-element.48), channel_id=1, source_target_pairs={{0,3},{1,0},{2,1},{3,2},{4,7},{5,4},{6,5},{7,6},{8,11},{9,8},{10,9... | collective-permute-start | bytes 393224 | tf_op jit(solution)/shard_map/ppermute | solution.py:425
  9.0 7.2 %collective-permute-start.3 = (f32[8,32,128]{2,1,0:T(8,128)S(1)}, f32[8,32,128]{2,1,0:T(8,128)S(1)}, u32[]{:S(2)}, u32[]{:S(2)}) collective-permute-start(f32[8,32,128]{2,1,0:T(8,128)S(1)} %get-tuple-element.57), channel_id=1, source_target_pairs={{0,1},{1,2},{2,3},{3,0},{4,5},{5,6},{6,7},{7,4},{8,9},{9,10},{10,1... | collective-permute-start | bytes 393224 | tf_op jit(solution)/shard_map/ppermute | solution.py:425
  9.4 8.5 %collective-permute-start.4 = (f32[8,32,128]{2,1,0:T(8,128)S(1)}, f32[8,32,128]{2,1,0:T(8,128)S(1)}, u32[]{:S(2)}, u32[]{:S(2)}) collective-permute-start(f32[8,32,128]{2,1,0:T(8,128)S(1)} %get-tuple-element.58), channel_id=1, source_target_pairs={{0,2},{1,3},{2,0},{3,1},{4,6},{5,7},{6,4},{7,5},{8,10},{9,11},{10,... | collective-permute-start | bytes 393224 | tf_op jit(solution)/shard_map/ppermute | solution.py:425
  10.2 7.6 %collective-permute-start.5 = (f32[8,32,128]{2,1,0:T(8,128)S(1)}, f32[8,32,128]{2,1,0:T(8,128)S(1)}, u32[]{:S(2)}, u32[]{:S(2)}) collective-permute-start(f32[8,32,128]{2,1,0:T(8,128)S(1)} %get-tuple-element.59), channel_id=1, source_target_pairs={{0,3},{1,0},{2,1},{3,2},{4,7},{5,4},{6,5},{7,6},{8,11},{9,8},{10,9... | collective-permute-start | bytes 393224 | tf_op jit(solution)/shard_map/ppermute | solution.py:425
  18.1 9.6 %collective-permute-start.6 = (f32[52,8,128]{2,1,0:T(8,128)S(1)}, f32[52,8,128]{2,1,0:T(8,128)S(1)}, u32[]{:S(2)}, u32[]{:S(2)}) collective-permute-start(f32[52,8,128]{2,1,0:T(8,128)S(1)} %get-tuple-element.61), channel_id=1, source_target_pairs={{0,1},{1,0},{2,3},{3,2},{7,6},{6,7},{5,4},{4,5},{8,9},{9,8},{10,11... | collective-permute-start | bytes 638984 | tf_op jit(solution)/shard_map/ppermute | solution.py:473
  18.2 9.8 %collective-permute-start.7 = (f32[52,8,128]{2,1,0:T(8,128)S(1)}, f32[52,8,128]{2,1,0:T(8,128)S(1)}, u32[]{:S(2)}, u32[]{:S(2)}) collective-permute-start(f32[52,8,128]{2,1,0:T(8,128)S(1)} %get-tuple-element.62), channel_id=1, source_target_pairs={{1,2},{2,1},{3,7},{7,3},{6,5},{5,6},{4,8},{8,4},{9,10},{10,9},{11,... | collective-permute-start | bytes 638984 | tf_op jit(solution)/shard_map/ppermute | solution.py:473
  34.9 23.8 %collective-permute-start.8 = (f32[8,32,128]{2,1,0:T(8,128)S(1)}, f32[8,32,128]{2,1,0:T(8,128)S(1)}, u32[]{:S(2)}, u32[]{:S(2)}) collective-permute-start(f32[8,32,128]{2,1,0:T(8,128)S(1)} %get-tuple-element.80), channel_id=1, source_target_pairs={{0,1},{1,2},{2,3},{3,0},{4,5},{5,6},{6,7},{7,4},{8,9},{9,10},{10,1... | collective-permute-start | bytes 393224 | tf_op jit(solution)/shard_map/ppermute | solution.py:425
  35.0 23.7 %collective-permute-start.9 = (f32[8,32,128]{2,1,0:T(8,128)S(1)}, f32[8,32,128]{2,1,0:T(8,128)S(1)}, u32[]{:S(2)}, u32[]{:S(2)}) collective-permute-start(f32[8,32,128]{2,1,0:T(8,128)S(1)} %get-tuple-element.81), channel_id=1, source_target_pairs={{0,2},{1,3},{2,0},{3,1},{4,6},{5,7},{6,4},{7,5},{8,10},{9,11},{10,... | collective-permute-start | bytes 393224 | tf_op jit(solution)/shard_map/ppermute | solution.py:425
  36.1 22.6 %collective-permute-start.10 = (f32[8,32,128]{2,1,0:T(8,128)S(1)}, f32[8,32,128]{2,1,0:T(8,128)S(1)}, u32[]{:S(2)}, u32[]{:S(2)}) collective-permute-start(f32[8,32,128]{2,1,0:T(8,128)S(1)} %get-tuple-element.82), channel_id=1, source_target_pairs={{0,3},{1,0},{2,1},{3,2},{4,7},{5,4},{6,5},{7,6},{8,11},{9,8},{10,9... | collective-permute-start | bytes 393224 | tf_op jit(solution)/shard_map/ppermute | solution.py:425

commit v6 on v5

--- a/solution.py
+++ b/solution.py
@@ -230,11 +230,11 @@
             ref_rows(i, HALO + CORE)[...] = ref_rows(i, HALO + CORE - 1)[...]
 
 
-def gather_state(own, r1, r2, r3, h0):
+def gather_state(own, r1, r3, r2, h0):
     _gather((own, r1, r2, r3), h0, HALO, CORE)
 
 
-def gather_seed(own, r1, r2, r3, h0, light, a_ref, to_inner, to_outer, edges):
+def gather_seed(own, r1, r3, r2, h0, light, a_ref, to_inner, to_outer, edges):
     _gather((own, r1, r2, r3), a_ref.at[0], HALO, CORE)
     for side, first, seed_first in ((0, HALO, HALO), (1, CORE, HALO + CORE - SEED_HALO)):
         edges[side, 0:32] = h0[:, BASE + first : BASE + first + HALO]
@@ -330,11 +330,12 @@
         _retreat(3 - i, tiles, a_ref.at[i], t_ref, k_ref, c_ref, r_ref, l_ref, light, put)
         return carry
 
-    lax.fori_loop(0, 3, step, 0)
+    lax.fori_loop(0, 4, step, 0)
 
 
 def sides(inner, outer, zid, *refs):
-    zpart, h0, h1, h2, t_ref, k_ref, c_ref, r_ref, l_ref, light, a_ref = refs[10:]
+    zpart, *outs = refs[10:15]
+    h0, h1, h2, t_ref, k_ref, c_ref, r_ref, l_ref, light, a_ref = refs[15:]
     fields = (t_ref, k_ref, c_ref, r_ref, l_ref)
     even = lax.rem(_group(lax.axis_index("dep")), 2) == 0
 
@@ -367,7 +368,7 @@
             _properties(n + 1, rf, tiles, new, *fields)
 
         _advance(n, tiles, source, t_ref, k_ref, l_ref, light, then)
-    for m in range(3):
+    for m in range(4):
         _ghost(lambda i, c, m=m: a_ref.at[m, i, pl.ds(BASE + c, 1)])
         tiles = _Tiles((SEED_HALO + m, HALO + CORE - SEED_HALO - m), HALO, True)
 
@@ -375,7 +376,6 @@
             tiles.store(value, a_ref, m + 1, j)
 
         _retreat(3 - m, tiles, a_ref.at[m], *fields, light, put)
-    _ghost(lambda i, c: a_ref.at[3, i, pl.ds(BASE + c, 1)])
     core = pl.ds(BASE + HALO, CORE)
     rows = []
     sums = []
@@ -391,20 +391,10 @@
         rows.append(jnp.sum((picked[0] + picked[1]) + (picked[2] + picked[3]), axis=0, keepdims=True))
     spread = jnp.concatenate(rows + [jnp.zeros((128 - NZONE, 128), F32)], axis=0)
     zpart[...] = jnp.sum(spread.T, axis=0, keepdims=True)
-
-
-def last_step(a_ref, t_ref, k_ref, c_ref, r_ref, l_ref, light, o0, o1, o2, o3):
     masks = [jnp.broadcast_to(m[0:1], (CORE, 128)) for m in _source_masks()]
-    values = [None] * 32
-
-    def put(i, value):
-        values[i] = value
-
-    tiles = _Tiles((HALO,), CORE, True)
-    _retreat(0, tiles, a_ref.at[3], t_ref, k_ref, c_ref, r_ref, l_ref, light, put)
-    for g in range(8):
-        turned = [values[g]] + [pltpu.roll(values[8 * rf + g], 32 * rf, 1) for rf in (1, 2, 3)]
-        for k, out in enumerate((o0, o1, o2, o3)):
+    for g in range(8):
+        turned = [a_ref[4, g, core]] + [pltpu.roll(a_ref[4, 8 * rf + g, core], 32 * rf, 1) for rf in (1, 2, 3)]
+        for k, out in enumerate(outs):
             out[g] = _pick(masks, k, turned)
 
 
@@ -497,27 +487,26 @@
         ),
     )
     s2, s1, s3 = _around(s2, 2), _around(s1, 1), _around(s3, 3)
-    one, four = _vmem(32, HIGH, 128), _vmem(4, 32, HIGH, 128)
+    one, four, five = _vmem(32, HIGH, 128), _vmem(4, 32, HIGH, 128), _vmem(5, 32, HIGH, 128)
     fields = (one, one, four, four, four, four, _vmem(4, 36, HIGH, 128))
-    (state,) = _call(gather_state, (h0, h1, h2, h3), (one,))
+    (state,) = _call(gather_state, (h0, h1, h3, h2), (one,))
     states = _call(forward_core, (state, light), fields)
     edge = _shape(52, HALO, 128)
     s0, light, *states = lax.optimization_barrier((s0, light, *states))
     a, to_inner, to_outer = _call(
-        gather_seed, (s0, s1, s2, s3, state, light), (four, edge, edge), (_vmem(2, 52, HALO, 128),)
+        gather_seed, (s0, s1, s3, s2, state, light), (five, edge, edge), (_vmem(2, 52, HALO, 128),)
     )
     axes = ("lat", "dep")
     line = [4 * l + (c if l % 2 == 0 else 3 - c) for l in range(32) for c in range(4)]
     outer, inner = _swap(to_outer, axes, line, 1), _swap(to_inner, axes, line, 0)
-    (a,) = _call(backward_core, (a, *states[2:], light), (four,), (), {0: 0})
-    zpart, *states = _call(
+    (a,) = _call(backward_core, (a, *states[2:], light), (five,), (), {0: 0})
+    zpart, o0, o1, o2, o3 = _call(
         sides,
         (inner, outer, zid, state, *states, light, a),
-        (_shape(1, 128), one) + fields + (surface, four),
+        (_shape(1, 128),) + (piece,) * 4 + (one,) + fields + (surface, five),
         (),
-        {3 + i: 1 + i for i in range(10)},
-    )
-    o0, o1, o2, o3 = _call(last_step, (states[9], *states[3:9]), (piece,) * 4)
+        {3 + i: 5 + i for i in range(10)},
+    )[:5]
     o2, o1, o3 = _around(o2, 2), _around(o1, 1), _around(o3, 3)
     parts = lax.all_to_all(jnp.broadcast_to(zpart[None], (128, 1, 128)), axes, 0, 0)
     out, total = _call(unpack, (o0, o1, o2, o3, parts), (_shape(32, 32, 128), _shape(NZONE)), (_vmem(8, 128, 128),))

time: 60 us -> 58.8 us (0.980)
  blocking collectives: 20.6 us -> 19.8 us
  starting transfers between devices: 18.1 us -> 17.4 us
    ppermute x9, starting transfers between devices: 11.7 us -> 10.7 us  [_around(): return lax.ppermute(x, 'dep', [(s, (s + k) % 4) for s in range(4)])]
    all_to_all x1, blocking collectives: 20.6 us -> 19.8 us  [per_device(): lax.all_to_all(jnp.broadcast_to(zpart[None], (128, 1, 128)), axes, 0, 0)]
    pallas_call x7 -> x6, Pallas kernels: 15.4 us -> 15.9 us  [_call(): pl.pallas_call(kernel, out_shape=tuple(outs), in_specs=[_full()] * len(in...]
  transfers between devices with their start and end apart: 11 -> 11, of which waited for: 3 -> 2; matrix products, arithmetic and copies ran while one was open for 0% -> 0% of each run, Pallas kernels for 14% -> 16%
where the time goes in v6:
time: 58.8 us; the launch traced here: 58.6 us
  blocking collectives  19.8 us (34%)
  Pallas kernels  18.5 us (31%)
  starting transfers between devices  17.4 us (30%)
  waiting for transfers between devices  2.08 us (4%)
  between operations  0.74 us (1%)
    all_to_all x1, blocking collectives, per_device(): lax.all_to_all(jnp.broadcast_to(zpart[None], (128, 1, 128)), axes, 0, 0)  19.8 us
    pallas_call x6, Pallas kernels, _call(): pl.pallas_call(kernel, out_shape=tuple(outs), in_specs=[_full()] * len(in...  15.9 us
    ppermute x9, starting transfers between devices, _around(): return lax.ppermute(x, 'dep', [(s, (s + k) % 4) for s in range(4)])  10.7 us
    ppermute x2, starting transfers between devices, _swap(): lax.ppermute(x, axes, [pair for a, b in list(zip(places, places[1:], stri...  6.73 us
    pallas_call x2, Pallas kernels, _call_hbm(): pl.pallas_call(kernel, out_shape=tuple(outs), in_specs=[pl.BlockSpec(memo...  2.61 us
    ppermute x9, waiting for transfers between devices, _around(): return lax.ppermute(x, 'dep', [(s, (s + k) % 4) for s in range(4)])  2.07 us
  transfers between devices with their start and end apart: 11, of which 2 were waited for; matrix products, arithmetic and copies ran while one was open for 0% of the time, Pallas kernels for 16%

profile of v6, /device:TPU:1, one launch (start us, length us, event | category | flops | bytes accessed | tf_op | source)
XLA Modules:
  0.0 58.6 jit_solution(1962612992578301960)
XLA Ops:
  0.6 1.3 %pack_state.1 = (f32[8,32,128]{2,1,0:T(8,128)S(1)}, f32[8,32,128]{2,1,0:T(8,128)S(1)}, f32[8,32,128]{2,1,0:T(8,128)S(1)}, f32[8,32,128]{2,1,0:T(8,128)S(1)}) custom-call(f32[32,32,128]{2,1,0:T(8,128)} %h_in.1), custom_call_target="tpu_custom_call" | custom-call | tf_op jit(solution)/shard_map/pack_state/pallas_call | solution.py:451
  1.9 2.1 %collective-permute-start = (f32[8,32,128]{2,1,0:T(8,128)S(1)}, f32[8,32,128]{2,1,0:T(8,128)S(1)}, u32[]{:S(2)}, u32[]{:S(2)}) collective-permute-start(f32[8,32,128]{2,1,0:T(8,128)S(1)} %get-tuple-element.39), channel_id=1, source_target_pairs={{0,1},{1,2},{2,3},{3,0},{4,5},{5,6},{6,7},{7,4},{8,9},{9,10},{10,1... | collective-permute-start | bytes 393224 | tf_op jit(solution)/shard_map/ppermute | solution.py:415
  4.0 1.3 %collective-permute-start.1 = (f32[8,32,128]{2,1,0:T(8,128)S(1)}, f32[8,32,128]{2,1,0:T(8,128)S(1)}, u32[]{:S(2)}, u32[]{:S(2)}) collective-permute-start(f32[8,32,128]{2,1,0:T(8,128)S(1)} %get-tuple-element.40), channel_id=1, source_target_pairs={{0,3},{1,0},{2,1},{3,2},{4,7},{5,4},{6,5},{7,6},{8,11},{9,8},{10,9... | collective-permute-start | bytes 393224 | tf_op jit(solution)/shard_map/ppermute | solution.py:415
  5.4 1.6 %collective-permute-start.2 = (f32[8,32,128]{2,1,0:T(8,128)S(1)}, f32[8,32,128]{2,1,0:T(8,128)S(1)}, u32[]{:S(2)}, u32[]{:S(2)}) collective-permute-start(f32[8,32,128]{2,1,0:T(8,128)S(1)} %get-tuple-element.41), channel_id=1, source_target_pairs={{0,2},{1,3},{2,0},{3,1},{4,6},{5,7},{6,4},{7,5},{8,10},{9,11},{10,... | collective-permute-start | bytes 393224 | tf_op jit(solution)/shard_map/ppermute | solution.py:415
  7.0 1.3 %pack_rest.1 = (f32[8,32,128]{2,1,0:T(8,128)S(1)}, f32[8,32,128]{2,1,0:T(8,128)S(1)}, f32[8,32,128]{2,1,0:T(8,128)S(1)}, f32[8,32,128]{2,1,0:T(8,128)S(1)}, f32[...) custom-call(f32[16]{0:T(128)} %fluence_in.1, s32[32,128]{1,0:T(8,128)} %zones_in.1, f32[32,32,128]{2,1,0:T(8,128)} %a_in.1), custom_call_target="tpu_custom_call" | custom-call | tf_op jit(solution)/shard_map/pack_rest/pallas_call | solution.py:451
  8.4 0.4 collective-permute-start.3
  8.7 2.4 %collective-permute-start.4 = (f32[8,32,128]{2,1,0:T(8,128)S(1)}, f32[8,32,128]{2,1,0:T(8,128)S(1)}, u32[]{:S(2)}, u32[]{:S(2)}) collective-permute-start(f32[8,32,128]{2,1,0:T(8,128)S(1)} %get-tuple-element.51), channel_id=1, source_target_pairs={{0,3},{1,0},{2,1},{3,2},{4,7},{5,4},{6,5},{7,6},{8,11},{9,8},{10,9... | collective-permute-start | bytes 393224 | tf_op jit(solution)/shard_map/ppermute | solution.py:415
  11.1 0.0 collective-permute-done.r1
  11.1 0.1 collective-permute-start.5
  11.2 0.0 collective-permute-done.1.r3
  11.2 1.1 %collective-permute-done.2.r2 = f32[8,32,128]{2,1,0:T(8,128)S(1)} collective-permute-done((f32[8,32,128]{2,1,0:T(8,128)S(1)}, f32[8,32,128]{2,1,0:T(8,128)S(1)}, u32[]{:S(2)}, u32[]{:S(2)}) %collective-permute-start.2) | collective-permute-done | bytes 131104 | tf_op jit(solution)/shard_map/ppermute | solution.py:415
  12.4 0.2 gather_state.1.h0.refs_0_
  12.5 3.8 %forward_core.1 = (f32[32,64,128]{2,1,0:T(8,128)S(1)}, f32[32,64,128]{2,1,0:T(8,128)S(1)}, f32[4,32,64,128]{3,2,1,0:T(8,128)S(1)}, f32[4,32,64,128]{3,2,1,0:T(8,...) custom-call(f32[32,64,128]{2,1,0:T(8,128)S(1)} %gather_state.1.h0.refs_0_, ...), custom_call_target="tpu_custom_call" | custom-call | tf_op jit(solution)/shard_map/forward_core/pallas_call | solution.py:437
  16.3 0.0 collective-permute-done.3.r1
  16.3 0.0 collective-permute-done.4.r3
  16.3 0.9 %collective-permute-done.5.r2 = f32[8,32,128]{2,1,0:T(8,128)S(1)} collective-permute-done((f32[8,32,128]{2,1,0:T(8,128)S(1)}, f32[8,32,128]{2,1,0:T(8,128)S(1)}, u32[]{:S(2)}, u32[]{:S(2)}) %collective-permute-start.5) | collective-permute-done | bytes 131104 | tf_op jit(solution)/shard_map/ppermute | solution.py:415
  17.3 0.3 gather_seed.1
  17.5 1.4 %collective-permute-start.6 = (f32[52,8,128]{2,1,0:T(8,128)S(1)}, f32[52,8,128]{2,1,0:T(8,128)S(1)}, u32[]{:S(2)}, u32[]{:S(2)}) collective-permute-start(f32[52,8,128]{2,1,0:T(8,128)S(1)} %get-tuple-element.54), channel_id=1, source_target_pairs={{0,1},{1,0},{2,3},{3,2},{7,6},{6,7},{5,4},{4,5},{8,9},{9,8},{10,11... | collective-permute-start | bytes 638984 | tf_op jit(solution)/shard_map/ppermute | solution.py:463
  19.0 5.3 %collective-permute-start.7 = (f32[52,8,128]{2,1,0:T(8,128)S(1)}, f32[52,8,128]{2,1,0:T(8,128)S(1)}, u32[]{:S(2)}, u32[]{:S(2)}) collective-permute-start(f32[52,8,128]{2,1,0:T(8,128)S(1)} %get-tuple-element.55), channel_id=1, source_target_pairs={{1,2},{2,1},{3,7},{7,3},{6,5},{5,6},{4,8},{8,4},{9,10},{10,9},{11,... | collective-permute-start | bytes 638984 | tf_op jit(solution)/shard_map/ppermute | solution.py:463
  24.3 4.2 %backward_core.1.refs_9_ = f32[5,32,64,128]{3,2,1,0:T(8,128)S(1)} custom-call(f32[5,32,64,128]{3,2,1,0:T(8,128)S(1)} %get-tuple-element.64.a_in, f32[4,32,64,128]{3,2,1,0:T(8,128)S(1)} %get-tuple-element.59.t_ref.refs_3_, f32[4,32,64,128]{3,2,1,0:T(8,128)S(1)} %get-tuple-element.60.k_ref.refs_4_, ...), custom_call_target="tpu_custom_call", output_to_operand_aliasing={{}: (0, {})} | custom-call | tf_op jit(solution)/shard_map/backward_core/pallas_call | solution.py:437
  28.5 0.0 collective-permute-done.6.inner
  28.5 0.0 collective-permute-done.7.outer
  28.5 6.4 %sides.1 = (f32[1,128]{1,0:T(1,128)S(1)}, f32[8,32,128]{2,1,0:T(8,128)S(1)}, f32[8,32,128]{2,1,0:T(8,128)S(1)}, f32[8,32,128]{2,1,0:T(8,128)S(1)}, f32[8,32,128]...) custom-call(f32[52,8,128]{2,1,0:T(8,128)S(1)} %collective-permute-do, ...), custom_call_target="tpu_custom_call", output_to_operand_aliasing={{5}: (3, {}), {6}: (4, {}), {7}: (5, {}), {8}: (6, {}), {9}... | custom-call | tf_op jit(solution)/shard_map/sides/pallas_call | solution.py:437
  35.0 0.1 collective-permute-start.8
  35.1 0.5 collective-permute-start.9
  35.6 2.2 %collective-permute-start.10 = (f32[8,32,128]{2,1,0:T(8,128)S(1)}, f32[8,32,128]{2,1,0:T(8,128)S(1)}, u32[]{:S(2)}, u32[]{:S(2)}) collective-permute-start(f32[8,32,128]{2,1,0:T(8,128)S(1)} %get-tuple-element.68), channel_id=1, source_target_pairs={{0,3},{1,0},{2,1},{3,2},{4,7},{5,4},{6,5},{7,6},{8,11},{9,8},{10,9... | collective-permute-start | bytes 393224 | tf_op jit(solution)/shard_map/ppermute | solution.py:415
  37.8 19.8 %all_to_all.5.parts = f32[128,1,128]{2,1,0:T(1,128)S(1)} all-to-all(f32[128,1,128]{2,1,0:T(1,128)S(1)} %broadcast_in_dim.9), channel_id=1, replica_groups=mesh['lat'=32,'dep'=4] {'lat','dep'}, dimensions={0} | all-to-all | bytes 131072 | tf_op jit(solution)/shard_map/all_to_all | solution.py:511
  57.5 0.0 collective-permute-done.8.r1
  57.5 0.0 collective-permute-done.9.r2
  57.5 0.0 collective-permute-done.10.r3
  57.5 1.1 %unpack.1 = (f32[32,32,128]{2,1,0:T(8,128)}, f32[16]{0:T(128)}) custom-call(f32[8,32,128]{2,1,0:T(8,128)S(1)} %get-tuple-element.65.own, f32[8,32,128]{2,1,0:T(8,128)S(1)} %collective-permute-done.8.r1, f32[8,32,128]{2,1,0:T(8,128)S(1)} %collective-permute-done.9.r2, f32[8,32,128]{2,1,0:T(8,128)S(1)} %collective-permute-done.10.r3, ...), custom_call_target="tpu_custom_call" | custom-call | tf_op jit(solution)/shard_map/unpack/pallas_call | solution.py:437
  (1 shorter events, 0.0 us)
Async XLA Ops:
  1.9 9.2 %collective-permute-start = (f32[8,32,128]{2,1,0:T(8,128)S(1)}, f32[8,32,128]{2,1,0:T(8,128)S(1)}, u32[]{:S(2)}, u32[]{:S(2)}) collective-permute-start(f32[8,32,128]{2,1,0:T(8,128)S(1)} %get-tuple-element.39), channel_id=1, source_target_pairs={{0,1},{1,2},{2,3},{3,0},{4,5},{5,6},{6,7},{7,4},{8,9},{9,10},{10,1... | collective-permute-start | bytes 393224 | tf_op jit(solution)/shard_map/ppermute | solution.py:415
  4.0 7.2 %collective-permute-start.1 = (f32[8,32,128]{2,1,0:T(8,128)S(1)}, f32[8,32,128]{2,1,0:T(8,128)S(1)}, u32[]{:S(2)}, u32[]{:S(2)}) collective-permute-start(f32[8,32,128]{2,1,0:T(8,128)S(1)} %get-tuple-element.40), channel_id=1, source_target_pairs={{0,3},{1,0},{2,1},{3,2},{4,7},{5,4},{6,5},{7,6},{8,11},{9,8},{10,9... | collective-permute-start | bytes 393224 | tf_op jit(solution)/shard_map/ppermute | solution.py:415
  5.4 7.0 %collective-permute-start.2 = (f32[8,32,128]{2,1,0:T(8,128)S(1)}, f32[8,32,128]{2,1,0:T(8,128)S(1)}, u32[]{:S(2)}, u32[]{:S(2)}) collective-permute-start(f32[8,32,128]{2,1,0:T(8,128)S(1)} %get-tuple-element.41), channel_id=1, source_target_pairs={{0,2},{1,3},{2,0},{3,1},{4,6},{5,7},{6,4},{7,5},{8,10},{9,11},{10,... | collective-permute-start | bytes 393224 | tf_op jit(solution)/shard_map/ppermute | solution.py:415
  8.4 8.0 %collective-permute-start.3 = (f32[8,32,128]{2,1,0:T(8,128)S(1)}, f32[8,32,128]{2,1,0:T(8,128)S(1)}, u32[]{:S(2)}, u32[]{:S(2)}) collective-permute-start(f32[8,32,128]{2,1,0:T(8,128)S(1)} %get-tuple-element.50), channel_id=1, source_target_pairs={{0,1},{1,2},{2,3},{3,0},{4,5},{5,6},{6,7},{7,4},{8,9},{9,10},{10,1... | collective-permute-start | bytes 393224 | tf_op jit(solution)/shard_map/ppermute | solution.py:415
  8.7 7.6 %collective-permute-start.4 = (f32[8,32,128]{2,1,0:T(8,128)S(1)}, f32[8,32,128]{2,1,0:T(8,128)S(1)}, u32[]{:S(2)}, u32[]{:S(2)}) collective-permute-start(f32[8,32,128]{2,1,0:T(8,128)S(1)} %get-tuple-element.51), channel_id=1, source_target_pairs={{0,3},{1,0},{2,1},{3,2},{4,7},{5,4},{6,5},{7,6},{8,11},{9,8},{10,9... | collective-permute-start | bytes 393224 | tf_op jit(solution)/shard_map/ppermute | solution.py:415
  11.1 6.2 %collective-permute-start.5 = (f32[8,32,128]{2,1,0:T(8,128)S(1)}, f32[8,32,128]{2,1,0:T(8,128)S(1)}, u32[]{:S(2)}, u32[]{:S(2)}) collective-permute-start(f32[8,32,128]{2,1,0:T(8,128)S(1)} %get-tuple-element.52), channel_id=1, source_target_pairs={{0,2},{1,3},{2,0},{3,1},{4,6},{5,7},{6,4},{7,5},{8,10},{9,11},{10,... | collective-permute-start | bytes 393224 | tf_op jit(solution)/shard_map/ppermute | solution.py:415
  17.5 11.0 %collective-permute-start.6 = (f32[52,8,128]{2,1,0:T(8,128)S(1)}, f32[52,8,128]{2,1,0:T(8,128)S(1)}, u32[]{:S(2)}, u32[]{:S(2)}) collective-permute-start(f32[52,8,128]{2,1,0:T(8,128)S(1)} %get-tuple-element.54), channel_id=1, source_target_pairs={{0,1},{1,0},{2,3},{3,2},{7,6},{6,7},{5,4},{4,5},{8,9},{9,8},{10,11... | collective-permute-start | bytes 638984 | tf_op jit(solution)/shard_map/ppermute | solution.py:463
  19.0 9.6 %collective-permute-start.7 = (f32[52,8,128]{2,1,0:T(8,128)S(1)}, f32[52,8,128]{2,1,0:T(8,128)S(1)}, u32[]{:S(2)}, u32[]{:S(2)}) collective-permute-start(f32[52,8,128]{2,1,0:T(8,128)S(1)} %get-tuple-element.55), channel_id=1, source_target_pairs={{1,2},{2,1},{3,7},{7,3},{6,5},{5,6},{4,8},{8,4},{9,10},{10,9},{11,... | collective-permute-start | bytes 638984 | tf_op jit(solution)/shard_map/ppermute | solution.py:463
  35.0 22.6 %collective-permute-start.8 = (f32[8,32,128]{2,1,0:T(8,128)S(1)}, f32[8,32,128]{2,1,0:T(8,128)S(1)}, u32[]{:S(2)}, u32[]{:S(2)}) collective-permute-start(f32[8,32,128]{2,1,0:T(8,128)S(1)} %get-tuple-element.66), channel_id=1, source_target_pairs={{0,1},{1,2},{2,3},{3,0},{4,5},{5,6},{6,7},{7,4},{8,9},{9,10},{10,1... | collective-permute-start | bytes 393224 | tf_op jit(solution)/shard_map/ppermute | solution.py:415
  35.1 22.5 %collective-permute-start.9 = (f32[8,32,128]{2,1,0:T(8,128)S(1)}, f32[8,32,128]{2,1,0:T(8,128)S(1)}, u32[]{:S(2)}, u32[]{:S(2)}) collective-permute-start(f32[8,32,128]{2,1,0:T(8,128)S(1)} %get-tuple-element.67), channel_id=1, source_target_pairs={{0,2},{1,3},{2,0},{3,1},{4,6},{5,7},{6,4},{7,5},{8,10},{9,11},{10,... | collective-permute-start | bytes 393224 | tf_op jit(solution)/shard_map/ppermute | solution.py:415
  35.6 22.0 %collective-permute-start.10 = (f32[8,32,128]{2,1,0:T(8,128)S(1)}, f32[8,32,128]{2,1,0:T(8,128)S(1)}, u32[]{:S(2)}, u32[]{:S(2)}) collective-permute-start(f32[8,32,128]{2,1,0:T(8,128)S(1)} %get-tuple-element.68), channel_id=1, source_target_pairs={{0,3},{1,0},{2,1},{3,2},{4,7},{5,4},{6,5},{7,6},{8,11},{9,8},{10,9... | collective-permute-start | bytes 393224 | tf_op jit(solution)/shard_map/ppermute | solution.py:415

commit v7 on v6

--- a/solution.py
+++ b/solution.py
@@ -508,7 +508,7 @@
         {3 + i: 5 + i for i in range(10)},
     )[:5]
     o2, o1, o3 = _around(o2, 2), _around(o1, 1), _around(o3, 3)
-    parts = lax.all_to_all(jnp.broadcast_to(zpart[None], (128, 1, 128)), axes, 0, 0)
+    parts = lax.all_to_all(jnp.broadcast_to(zpart[None], (128, 1, 128)), ("dep", "lat"), 0, 0)
     out, total = _call(unpack, (o0, o1, o2, o3, parts), (_shape(32, 32, 128), _shape(NZONE)), (_vmem(8, 128, 128),))
     return out, total
 

time: 58.8 us -> 58.3 us (level)
  blocking collectives: 19.8 us -> 19.2 us
where the time goes in v7:
time: 58.3 us; the launch traced here: 58.1 us
  blocking collectives  19.2 us (33%)
  Pallas kernels  18.5 us (32%)
  starting transfers between devices  17.4 us (30%)
  waiting for transfers between devices  2.08 us (4%)
  between operations  0.74 us (1%)
    all_to_all x1, blocking collectives, per_device(): lax.all_to_all(jnp.broadcast_to(zpart[None], (128, 1, 128)), ('dep', 'lat...  19.2 us
    pallas_call x6, Pallas kernels, _call(): pl.pallas_call(kernel, out_shape=tuple(outs), in_specs=[_full()] * len(in...  15.9 us
    ppermute x9, starting transfers between devices, _around(): return lax.ppermute(x, 'dep', [(s, (s + k) % 4) for s in range(4)])  10.7 us
    ppermute x2, starting transfers between devices, _swap(): lax.ppermute(x, axes, [pair for a, b in list(zip(places, places[1:], stri...  6.73 us
    pallas_call x2, Pallas kernels, _call_hbm(): pl.pallas_call(kernel, out_shape=tuple(outs), in_specs=[pl.BlockSpec(memo...  2.61 us
    ppermute x9, waiting for transfers between devices, _around(): return lax.ppermute(x, 'dep', [(s, (s + k) % 4) for s in range(4)])  2.07 us
  transfers between devices with their start and end apart: 11, of which 2 were waited for; matrix products, arithmetic and copies ran while one was open for 0% of the time, Pallas kernels for 16%

profile of v7, /device:TPU:1, one launch (start us, length us, event | category | flops | bytes accessed | tf_op | source)
XLA Modules:
  0.0 58.1 jit_solution(4090637917649299831)
XLA Ops:
  0.6 1.3 %pack_state.1 = (f32[8,32,128]{2,1,0:T(8,128)S(1)}, f32[8,32,128]{2,1,0:T(8,128)S(1)}, f32[8,32,128]{2,1,0:T(8,128)S(1)}, f32[8,32,128]{2,1,0:T(8,128)S(1)}) custom-call(f32[32,32,128]{2,1,0:T(8,128)} %h_in.1), custom_call_target="tpu_custom_call" | custom-call | tf_op jit(solution)/shard_map/pack_state/pallas_call | solution.py:451
  1.9 2.1 %collective-permute-start = (f32[8,32,128]{2,1,0:T(8,128)S(1)}, f32[8,32,128]{2,1,0:T(8,128)S(1)}, u32[]{:S(2)}, u32[]{:S(2)}) collective-permute-start(f32[8,32,128]{2,1,0:T(8,128)S(1)} %get-tuple-element.39), channel_id=1, source_target_pairs={{0,1},{1,2},{2,3},{3,0},{4,5},{5,6},{6,7},{7,4},{8,9},{9,10},{10,1... | collective-permute-start | bytes 393224 | tf_op jit(solution)/shard_map/ppermute | solution.py:415
  4.0 1.3 %collective-permute-start.1 = (f32[8,32,128]{2,1,0:T(8,128)S(1)}, f32[8,32,128]{2,1,0:T(8,128)S(1)}, u32[]{:S(2)}, u32[]{:S(2)}) collective-permute-start(f32[8,32,128]{2,1,0:T(8,128)S(1)} %get-tuple-element.40), channel_id=1, source_target_pairs={{0,3},{1,0},{2,1},{3,2},{4,7},{5,4},{6,5},{7,6},{8,11},{9,8},{10,9... | collective-permute-start | bytes 393224 | tf_op jit(solution)/shard_map/ppermute | solution.py:415
  5.4 1.6 %collective-permute-start.2 = (f32[8,32,128]{2,1,0:T(8,128)S(1)}, f32[8,32,128]{2,1,0:T(8,128)S(1)}, u32[]{:S(2)}, u32[]{:S(2)}) collective-permute-start(f32[8,32,128]{2,1,0:T(8,128)S(1)} %get-tuple-element.41), channel_id=1, source_target_pairs={{0,2},{1,3},{2,0},{3,1},{4,6},{5,7},{6,4},{7,5},{8,10},{9,11},{10,... | collective-permute-start | bytes 393224 | tf_op jit(solution)/shard_map/ppermute | solution.py:415
  7.0 1.3 %pack_rest.1 = (f32[8,32,128]{2,1,0:T(8,128)S(1)}, f32[8,32,128]{2,1,0:T(8,128)S(1)}, f32[8,32,128]{2,1,0:T(8,128)S(1)}, f32[8,32,128]{2,1,0:T(8,128)S(1)}, f32[...) custom-call(f32[16]{0:T(128)} %fluence_in.1, s32[32,128]{1,0:T(8,128)} %zones_in.1, f32[32,32,128]{2,1,0:T(8,128)} %a_in.1), custom_call_target="tpu_custom_call" | custom-call | tf_op jit(solution)/shard_map/pack_rest/pallas_call | solution.py:451
  8.4 0.4 collective-permute-start.3
  8.7 2.4 %collective-permute-start.4 = (f32[8,32,128]{2,1,0:T(8,128)S(1)}, f32[8,32,128]{2,1,0:T(8,128)S(1)}, u32[]{:S(2)}, u32[]{:S(2)}) collective-permute-start(f32[8,32,128]{2,1,0:T(8,128)S(1)} %get-tuple-element.51), channel_id=1, source_target_pairs={{0,3},{1,0},{2,1},{3,2},{4,7},{5,4},{6,5},{7,6},{8,11},{9,8},{10,9... | collective-permute-start | bytes 393224 | tf_op jit(solution)/shard_map/ppermute | solution.py:415
  11.1 0.0 collective-permute-done.r1
  11.1 0.1 collective-permute-start.5
  11.2 0.0 collective-permute-done.1.r3
  11.2 1.1 %collective-permute-done.2.r2 = f32[8,32,128]{2,1,0:T(8,128)S(1)} collective-permute-done((f32[8,32,128]{2,1,0:T(8,128)S(1)}, f32[8,32,128]{2,1,0:T(8,128)S(1)}, u32[]{:S(2)}, u32[]{:S(2)}) %collective-permute-start.2) | collective-permute-done | bytes 131104 | tf_op jit(solution)/shard_map/ppermute | solution.py:415
  12.4 0.2 gather_state.1.h0.refs_0_
  12.5 3.8 %forward_core.1 = (f32[32,64,128]{2,1,0:T(8,128)S(1)}, f32[32,64,128]{2,1,0:T(8,128)S(1)}, f32[4,32,64,128]{3,2,1,0:T(8,128)S(1)}, f32[4,32,64,128]{3,2,1,0:T(8,...) custom-call(f32[32,64,128]{2,1,0:T(8,128)S(1)} %gather_state.1.h0.refs_0_, ...), custom_call_target="tpu_custom_call" | custom-call | tf_op jit(solution)/shard_map/forward_core/pallas_call | solution.py:437
  16.3 0.0 collective-permute-done.3.r1
  16.3 0.0 collective-permute-done.4.r3
  16.3 0.9 %collective-permute-done.5.r2 = f32[8,32,128]{2,1,0:T(8,128)S(1)} collective-permute-done((f32[8,32,128]{2,1,0:T(8,128)S(1)}, f32[8,32,128]{2,1,0:T(8,128)S(1)}, u32[]{:S(2)}, u32[]{:S(2)}) %collective-permute-start.5) | collective-permute-done | bytes 131104 | tf_op jit(solution)/shard_map/ppermute | solution.py:415
  17.3 0.3 gather_seed.1
  17.5 1.4 %collective-permute-start.6 = (f32[52,8,128]{2,1,0:T(8,128)S(1)}, f32[52,8,128]{2,1,0:T(8,128)S(1)}, u32[]{:S(2)}, u32[]{:S(2)}) collective-permute-start(f32[52,8,128]{2,1,0:T(8,128)S(1)} %get-tuple-element.54), channel_id=1, source_target_pairs={{0,1},{1,0},{2,3},{3,2},{7,6},{6,7},{5,4},{4,5},{8,9},{9,8},{10,11... | collective-permute-start | bytes 638984 | tf_op jit(solution)/shard_map/ppermute | solution.py:463
  19.0 5.3 %collective-permute-start.7 = (f32[52,8,128]{2,1,0:T(8,128)S(1)}, f32[52,8,128]{2,1,0:T(8,128)S(1)}, u32[]{:S(2)}, u32[]{:S(2)}) collective-permute-start(f32[52,8,128]{2,1,0:T(8,128)S(1)} %get-tuple-element.55), channel_id=1, source_target_pairs={{1,2},{2,1},{3,7},{7,3},{6,5},{5,6},{4,8},{8,4},{9,10},{10,9},{11,... | collective-permute-start | bytes 638984 | tf_op jit(solution)/shard_map/ppermute | solution.py:463
  24.3 4.2 %backward_core.1.refs_9_ = f32[5,32,64,128]{3,2,1,0:T(8,128)S(1)} custom-call(f32[5,32,64,128]{3,2,1,0:T(8,128)S(1)} %get-tuple-element.64.a_in, f32[4,32,64,128]{3,2,1,0:T(8,128)S(1)} %get-tuple-element.59.t_ref.refs_3_, f32[4,32,64,128]{3,2,1,0:T(8,128)S(1)} %get-tuple-element.60.k_ref.refs_4_, ...), custom_call_target="tpu_custom_call", output_to_operand_aliasing={{}: (0, {})} | custom-call | tf_op jit(solution)/shard_map/backward_core/pallas_call | solution.py:437
  28.5 0.0 collective-permute-done.6.inner
  28.5 0.0 collective-permute-done.7.outer
  28.5 6.4 %sides.1 = (f32[1,128]{1,0:T(1,128)S(1)}, f32[8,32,128]{2,1,0:T(8,128)S(1)}, f32[8,32,128]{2,1,0:T(8,128)S(1)}, f32[8,32,128]{2,1,0:T(8,128)S(1)}, f32[8,32,128]...) custom-call(f32[52,8,128]{2,1,0:T(8,128)S(1)} %collective-permute-do, ...), custom_call_target="tpu_custom_call", output_to_operand_aliasing={{5}: (3, {}), {6}: (4, {}), {7}: (5, {}), {8}: (6, {}), {9}... | custom-call | tf_op jit(solution)/shard_map/sides/pallas_call | solution.py:437
  35.0 0.1 collective-permute-start.8
  35.1 0.5 collective-permute-start.9
  35.6 2.2 %collective-permute-start.10 = (f32[8,32,128]{2,1,0:T(8,128)S(1)}, f32[8,32,128]{2,1,0:T(8,128)S(1)}, u32[]{:S(2)}, u32[]{:S(2)}) collective-permute-start(f32[8,32,128]{2,1,0:T(8,128)S(1)} %get-tuple-element.68), channel_id=1, source_target_pairs={{0,3},{1,0},{2,1},{3,2},{4,7},{5,4},{6,5},{7,6},{8,11},{9,8},{10,9... | collective-permute-start | bytes 393224 | tf_op jit(solution)/shard_map/ppermute | solution.py:415
  37.8 19.2 %all_to_all.5.parts = f32[128,1,128]{2,1,0:T(1,128)S(1)} all-to-all(f32[128,1,128]{2,1,0:T(1,128)S(1)} %broadcast_in_dim.9), channel_id=1, replica_groups=mesh['lat'=32,'dep'=4] {'dep','lat'}, dimensions={0} | all-to-all | bytes 131072 | tf_op jit(solution)/shard_map/all_to_all | solution.py:511
  57.0 0.0 collective-permute-done.8.r1
  57.0 0.0 collective-permute-done.9.r2
  57.0 0.0 collective-permute-done.10.r3
  57.0 1.1 %unpack.1 = (f32[32,32,128]{2,1,0:T(8,128)}, f32[16]{0:T(128)}) custom-call(f32[8,32,128]{2,1,0:T(8,128)S(1)} %get-tuple-element.65.own, f32[8,32,128]{2,1,0:T(8,128)S(1)} %collective-permute-done.8.r1, f32[8,32,128]{2,1,0:T(8,128)S(1)} %collective-permute-done.9.r2, f32[8,32,128]{2,1,0:T(8,128)S(1)} %collective-permute-done.10.r3, ...), custom_call_target="tpu_custom_call" | custom-call | tf_op jit(solution)/shard_map/unpack/pallas_call | solution.py:437
  (1 shorter events, 0.0 us)
Async XLA Ops:
  1.9 9.2 %collective-permute-start = (f32[8,32,128]{2,1,0:T(8,128)S(1)}, f32[8,32,128]{2,1,0:T(8,128)S(1)}, u32[]{:S(2)}, u32[]{:S(2)}) collective-permute-start(f32[8,32,128]{2,1,0:T(8,128)S(1)} %get-tuple-element.39), channel_id=1, source_target_pairs={{0,1},{1,2},{2,3},{3,0},{4,5},{5,6},{6,7},{7,4},{8,9},{9,10},{10,1... | collective-permute-start | bytes 393224 | tf_op jit(solution)/shard_map/ppermute | solution.py:415
  4.0 7.2 %collective-permute-start.1 = (f32[8,32,128]{2,1,0:T(8,128)S(1)}, f32[8,32,128]{2,1,0:T(8,128)S(1)}, u32[]{:S(2)}, u32[]{:S(2)}) collective-permute-start(f32[8,32,128]{2,1,0:T(8,128)S(1)} %get-tuple-element.40), channel_id=1, source_target_pairs={{0,3},{1,0},{2,1},{3,2},{4,7},{5,4},{6,5},{7,6},{8,11},{9,8},{10,9... | collective-permute-start | bytes 393224 | tf_op jit(solution)/shard_map/ppermute | solution.py:415
  5.4 7.0 %collective-permute-start.2 = (f32[8,32,128]{2,1,0:T(8,128)S(1)}, f32[8,32,128]{2,1,0:T(8,128)S(1)}, u32[]{:S(2)}, u32[]{:S(2)}) collective-permute-start(f32[8,32,128]{2,1,0:T(8,128)S(1)} %get-tuple-element.41), channel_id=1, source_target_pairs={{0,2},{1,3},{2,0},{3,1},{4,6},{5,7},{6,4},{7,5},{8,10},{9,11},{10,... | collective-permute-start | bytes 393224 | tf_op jit(solution)/shard_map/ppermute | solution.py:415
  8.4 8.0 %collective-permute-start.3 = (f32[8,32,128]{2,1,0:T(8,128)S(1)}, f32[8,32,128]{2,1,0:T(8,128)S(1)}, u32[]{:S(2)}, u32[]{:S(2)}) collective-permute-start(f32[8,32,128]{2,1,0:T(8,128)S(1)} %get-tuple-element.50), channel_id=1, source_target_pairs={{0,1},{1,2},{2,3},{3,0},{4,5},{5,6},{6,7},{7,4},{8,9},{9,10},{10,1... | collective-permute-start | bytes 393224 | tf_op jit(solution)/shard_map/ppermute | solution.py:415
  8.7 7.6 %collective-permute-start.4 = (f32[8,32,128]{2,1,0:T(8,128)S(1)}, f32[8,32,128]{2,1,0:T(8,128)S(1)}, u32[]{:S(2)}, u32[]{:S(2)}) collective-permute-start(f32[8,32,128]{2,1,0:T(8,128)S(1)} %get-tuple-element.51), channel_id=1, source_target_pairs={{0,3},{1,0},{2,1},{3,2},{4,7},{5,4},{6,5},{7,6},{8,11},{9,8},{10,9... | collective-permute-start | bytes 393224 | tf_op jit(solution)/shard_map/ppermute | solution.py:415
  11.1 6.2 %collective-permute-start.5 = (f32[8,32,128]{2,1,0:T(8,128)S(1)}, f32[8,32,128]{2,1,0:T(8,128)S(1)}, u32[]{:S(2)}, u32[]{:S(2)}) collective-permute-start(f32[8,32,128]{2,1,0:T(8,128)S(1)} %get-tuple-element.52), channel_id=1, source_target_pairs={{0,2},{1,3},{2,0},{3,1},{4,6},{5,7},{6,4},{7,5},{8,10},{9,11},{10,... | collective-permute-start | bytes 393224 | tf_op jit(solution)/shard_map/ppermute | solution.py:415
  17.5 11.0 %collective-permute-start.6 = (f32[52,8,128]{2,1,0:T(8,128)S(1)}, f32[52,8,128]{2,1,0:T(8,128)S(1)}, u32[]{:S(2)}, u32[]{:S(2)}) collective-permute-start(f32[52,8,128]{2,1,0:T(8,128)S(1)} %get-tuple-element.54), channel_id=1, source_target_pairs={{0,1},{1,0},{2,3},{3,2},{7,6},{6,7},{5,4},{4,5},{8,9},{9,8},{10,11... | collective-permute-start | bytes 638984 | tf_op jit(solution)/shard_map/ppermute | solution.py:463
  19.0 9.6 %collective-permute-start.7 = (f32[52,8,128]{2,1,0:T(8,128)S(1)}, f32[52,8,128]{2,1,0:T(8,128)S(1)}, u32[]{:S(2)}, u32[]{:S(2)}) collective-permute-start(f32[52,8,128]{2,1,0:T(8,128)S(1)} %get-tuple-element.55), channel_id=1, source_target_pairs={{1,2},{2,1},{3,7},{7,3},{6,5},{5,6},{4,8},{8,4},{9,10},{10,9},{11,... | collective-permute-start | bytes 638984 | tf_op jit(solution)/shard_map/ppermute | solution.py:463
  35.0 22.0 %collective-permute-start.8 = (f32[8,32,128]{2,1,0:T(8,128)S(1)}, f32[8,32,128]{2,1,0:T(8,128)S(1)}, u32[]{:S(2)}, u32[]{:S(2)}) collective-permute-start(f32[8,32,128]{2,1,0:T(8,128)S(1)} %get-tuple-element.66), channel_id=1, source_target_pairs={{0,1},{1,2},{2,3},{3,0},{4,5},{5,6},{6,7},{7,4},{8,9},{9,10},{10,1... | collective-permute-start | bytes 393224 | tf_op jit(solution)/shard_map/ppermute | solution.py:415
  35.1 21.9 %collective-permute-start.9 = (f32[8,32,128]{2,1,0:T(8,128)S(1)}, f32[8,32,128]{2,1,0:T(8,128)S(1)}, u32[]{:S(2)}, u32[]{:S(2)}) collective-permute-start(f32[8,32,128]{2,1,0:T(8,128)S(1)} %get-tuple-element.67), channel_id=1, source_target_pairs={{0,2},{1,3},{2,0},{3,1},{4,6},{5,7},{6,4},{7,5},{8,10},{9,11},{10,... | collective-permute-start | bytes 393224 | tf_op jit(solution)/shard_map/ppermute | solution.py:415
  35.6 21.4 %collective-permute-start.10 = (f32[8,32,128]{2,1,0:T(8,128)S(1)}, f32[8,32,128]{2,1,0:T(8,128)S(1)}, u32[]{:S(2)}, u32[]{:S(2)}) collective-permute-start(f32[8,32,128]{2,1,0:T(8,128)S(1)} %get-tuple-element.68), channel_id=1, source_target_pairs={{0,3},{1,0},{2,1},{3,2},{4,7},{5,4},{6,5},{7,6},{8,11},{9,8},{10,9... | collective-permute-start | bytes 393224 | tf_op jit(solution)/shard_map/ppermute | solution.py:415

commit v8 on v7

--- a/solution.py
+++ b/solution.py
@@ -145,7 +145,7 @@
     tri = jnp.where(jnp.logical_and(same, a >= b if reverse else a <= b), 1.0, 0.0).astype(jnp.bfloat16)
     high = total.astype(jnp.bfloat16)
     low = (total - high.astype(F32)).astype(jnp.bfloat16)
-    return jnp.dot(high, tri, preferred_element_type=F32) + jnp.dot(low, tri, preferred_element_type=F32)
+    return jnp.dot(jnp.concatenate([high, low], axis=1), jnp.concatenate([tri, tri], axis=0), preferred_element_type=F32)
 
 
 def _properties(n, rf, tiles, states, t_ref, k_ref, c_ref, r_ref, l_ref):

time: 58.3 us -> 58.2 us (level)
  no operation moved by 1% of the time
where the time goes in v8:
time: 58.2 us; the launch traced here: 58 us
  blocking collectives  19.2 us (33%)
  Pallas kernels  18.5 us (32%)
  starting transfers between devices  17.4 us (30%)
  waiting for transfers between devices  2.08 us (4%)
  between operations  0.74 us (1%)
    all_to_all x1, blocking collectives, per_device(): lax.all_to_all(jnp.broadcast_to(zpart[None], (128, 1, 128)), ('dep', 'lat...  19.2 us
    pallas_call x6, Pallas kernels, _call(): pl.pallas_call(kernel, out_shape=tuple(outs), in_specs=[_full()] * len(in...  15.9 us
    ppermute x9, starting transfers between devices, _around(): return lax.ppermute(x, 'dep', [(s, (s + k) % 4) for s in range(4)])  10.7 us
    ppermute x2, starting transfers between devices, _swap(): lax.ppermute(x, axes, [pair for a, b in list(zip(places, places[1:], stri...  6.73 us
    pallas_call x2, Pallas kernels, _call_hbm(): pl.pallas_call(kernel, out_shape=tuple(outs), in_specs=[pl.BlockSpec(memo...  2.61 us
    ppermute x9, waiting for transfers between devices, _around(): return lax.ppermute(x, 'dep', [(s, (s + k) % 4) for s in range(4)])  2.08 us
  transfers between devices with their start and end apart: 11, of which 2 were waited for; matrix products, arithmetic and copies ran while one was open for 0% of the time, Pallas kernels for 16%

profile of v8, /device:TPU:1, one launch (start us, length us, event | category | flops | bytes accessed | tf_op | source)
XLA Modules:
  0.0 58.0 jit_solution(2584985725016726154)
XLA Ops:
  0.6 1.3 %pack_state.1 = (f32[8,32,128]{2,1,0:T(8,128)S(1)}, f32[8,32,128]{2,1,0:T(8,128)S(1)}, f32[8,32,128]{2,1,0:T(8,128)S(1)}, f32[8,32,128]{2,1,0:T(8,128)S(1)}) custom-call(f32[32,32,128]{2,1,0:T(8,128)} %h_in.1), custom_call_target="tpu_custom_call" | custom-call | tf_op jit(solution)/shard_map/pack_state/pallas_call | solution.py:451
  1.9 2.1 %collective-permute-start = (f32[8,32,128]{2,1,0:T(8,128)S(1)}, f32[8,32,128]{2,1,0:T(8,128)S(1)}, u32[]{:S(2)}, u32[]{:S(2)}) collective-permute-start(f32[8,32,128]{2,1,0:T(8,128)S(1)} %get-tuple-element.39), channel_id=1, source_target_pairs={{0,1},{1,2},{2,3},{3,0},{4,5},{5,6},{6,7},{7,4},{8,9},{9,10},{10,1... | collective-permute-start | bytes 393224 | tf_op jit(solution)/shard_map/ppermute | solution.py:415
  4.0 1.3 %collective-permute-start.1 = (f32[8,32,128]{2,1,0:T(8,128)S(1)}, f32[8,32,128]{2,1,0:T(8,128)S(1)}, u32[]{:S(2)}, u32[]{:S(2)}) collective-permute-start(f32[8,32,128]{2,1,0:T(8,128)S(1)} %get-tuple-element.40), channel_id=1, source_target_pairs={{0,3},{1,0},{2,1},{3,2},{4,7},{5,4},{6,5},{7,6},{8,11},{9,8},{10,9... | collective-permute-start | bytes 393224 | tf_op jit(solution)/shard_map/ppermute | solution.py:415
  5.4 1.6 %collective-permute-start.2 = (f32[8,32,128]{2,1,0:T(8,128)S(1)}, f32[8,32,128]{2,1,0:T(8,128)S(1)}, u32[]{:S(2)}, u32[]{:S(2)}) collective-permute-start(f32[8,32,128]{2,1,0:T(8,128)S(1)} %get-tuple-element.41), channel_id=1, source_target_pairs={{0,2},{1,3},{2,0},{3,1},{4,6},{5,7},{6,4},{7,5},{8,10},{9,11},{10,... | collective-permute-start | bytes 393224 | tf_op jit(solution)/shard_map/ppermute | solution.py:415
  7.0 1.3 %pack_rest.1 = (f32[8,32,128]{2,1,0:T(8,128)S(1)}, f32[8,32,128]{2,1,0:T(8,128)S(1)}, f32[8,32,128]{2,1,0:T(8,128)S(1)}, f32[8,32,128]{2,1,0:T(8,128)S(1)}, f32[...) custom-call(f32[16]{0:T(128)} %fluence_in.1, s32[32,128]{1,0:T(8,128)} %zones_in.1, f32[32,32,128]{2,1,0:T(8,128)} %a_in.1), custom_call_target="tpu_custom_call" | custom-call | tf_op jit(solution)/shard_map/pack_rest/pallas_call | solution.py:451
  8.4 0.4 collective-permute-start.3
  8.7 2.4 %collective-permute-start.4 = (f32[8,32,128]{2,1,0:T(8,128)S(1)}, f32[8,32,128]{2,1,0:T(8,128)S(1)}, u32[]{:S(2)}, u32[]{:S(2)}) collective-permute-start(f32[8,32,128]{2,1,0:T(8,128)S(1)} %get-tuple-element.51), channel_id=1, source_target_pairs={{0,3},{1,0},{2,1},{3,2},{4,7},{5,4},{6,5},{7,6},{8,11},{9,8},{10,9... | collective-permute-start | bytes 393224 | tf_op jit(solution)/shard_map/ppermute | solution.py:415
  11.1 0.0 collective-permute-done.r1
  11.1 0.1 collective-permute-start.5
  11.2 0.0 collective-permute-done.1.r3
  11.2 1.1 %collective-permute-done.2.r2 = f32[8,32,128]{2,1,0:T(8,128)S(1)} collective-permute-done((f32[8,32,128]{2,1,0:T(8,128)S(1)}, f32[8,32,128]{2,1,0:T(8,128)S(1)}, u32[]{:S(2)}, u32[]{:S(2)}) %collective-permute-start.2) | collective-permute-done | bytes 131104 | tf_op jit(solution)/shard_map/ppermute | solution.py:415
  12.4 0.2 gather_state.1.h0.refs_0_
  12.5 3.8 %forward_core.1 = (f32[32,64,128]{2,1,0:T(8,128)S(1)}, f32[32,64,128]{2,1,0:T(8,128)S(1)}, f32[4,32,64,128]{3,2,1,0:T(8,128)S(1)}, f32[4,32,64,128]{3,2,1,0:T(8,...) custom-call(f32[32,64,128]{2,1,0:T(8,128)S(1)} %gather_state.1.h0.refs_0_, ...), custom_call_target="tpu_custom_call" | custom-call | tf_op jit(solution)/shard_map/forward_core/pallas_call | solution.py:437
  16.3 0.0 collective-permute-done.3.r1
  16.3 0.0 collective-permute-done.4.r3
  16.3 0.9 %collective-permute-done.5.r2 = f32[8,32,128]{2,1,0:T(8,128)S(1)} collective-permute-done((f32[8,32,128]{2,1,0:T(8,128)S(1)}, f32[8,32,128]{2,1,0:T(8,128)S(1)}, u32[]{:S(2)}, u32[]{:S(2)}) %collective-permute-start.5) | collective-permute-done | bytes 131104 | tf_op jit(solution)/shard_map/ppermute | solution.py:415
  17.3 0.3 gather_seed.1
  17.5 1.4 %collective-permute-start.6 = (f32[52,8,128]{2,1,0:T(8,128)S(1)}, f32[52,8,128]{2,1,0:T(8,128)S(1)}, u32[]{:S(2)}, u32[]{:S(2)}) collective-permute-start(f32[52,8,128]{2,1,0:T(8,128)S(1)} %get-tuple-element.54), channel_id=1, source_target_pairs={{0,1},{1,0},{2,3},{3,2},{7,6},{6,7},{5,4},{4,5},{8,9},{9,8},{10,11... | collective-permute-start | bytes 638984 | tf_op jit(solution)/shard_map/ppermute | solution.py:463
  19.0 5.3 %collective-permute-start.7 = (f32[52,8,128]{2,1,0:T(8,128)S(1)}, f32[52,8,128]{2,1,0:T(8,128)S(1)}, u32[]{:S(2)}, u32[]{:S(2)}) collective-permute-start(f32[52,8,128]{2,1,0:T(8,128)S(1)} %get-tuple-element.55), channel_id=1, source_target_pairs={{1,2},{2,1},{3,7},{7,3},{6,5},{5,6},{4,8},{8,4},{9,10},{10,9},{11,... | collective-permute-start | bytes 638984 | tf_op jit(solution)/shard_map/ppermute | solution.py:463
  24.3 4.3 %backward_core.1.refs_9_ = f32[5,32,64,128]{3,2,1,0:T(8,128)S(1)} custom-call(f32[5,32,64,128]{3,2,1,0:T(8,128)S(1)} %get-tuple-element.64.a_in, f32[4,32,64,128]{3,2,1,0:T(8,128)S(1)} %get-tuple-element.59.t_ref.refs_3_, f32[4,32,64,128]{3,2,1,0:T(8,128)S(1)} %get-tuple-element.60.k_ref.refs_4_, ...), custom_call_target="tpu_custom_call", output_to_operand_aliasing={{}: (0, {})} | custom-call | tf_op jit(solution)/shard_map/backward_core/pallas_call | solution.py:437
  28.6 0.0 collective-permute-done.6.inner
  28.6 0.0 collective-permute-done.7.outer
  28.6 6.4 %sides.1 = (f32[1,128]{1,0:T(1,128)S(1)}, f32[8,32,128]{2,1,0:T(8,128)S(1)}, f32[8,32,128]{2,1,0:T(8,128)S(1)}, f32[8,32,128]{2,1,0:T(8,128)S(1)}, f32[8,32,128]...) custom-call(f32[52,8,128]{2,1,0:T(8,128)S(1)} %collective-permute-do, ...), custom_call_target="tpu_custom_call", output_to_operand_aliasing={{5}: (3, {}), {6}: (4, {}), {7}: (5, {}), {8}: (6, {}), {9}... | custom-call | tf_op jit(solution)/shard_map/sides/pallas_call | solution.py:437
  35.0 0.1 collective-permute-start.8
  35.1 0.5 collective-permute-start.9
  35.6 2.2 %collective-permute-start.10 = (f32[8,32,128]{2,1,0:T(8,128)S(1)}, f32[8,32,128]{2,1,0:T(8,128)S(1)}, u32[]{:S(2)}, u32[]{:S(2)}) collective-permute-start(f32[8,32,128]{2,1,0:T(8,128)S(1)} %get-tuple-element.68), channel_id=1, source_target_pairs={{0,3},{1,0},{2,1},{3,2},{4,7},{5,4},{6,5},{7,6},{8,11},{9,8},{10,9... | collective-permute-start | bytes 393224 | tf_op jit(solution)/shard_map/ppermute | solution.py:415
  37.8 19.2 %all_to_all.5.parts = f32[128,1,128]{2,1,0:T(1,128)S(1)} all-to-all(f32[128,1,128]{2,1,0:T(1,128)S(1)} %broadcast_in_dim.9), channel_id=1, replica_groups=mesh['lat'=32,'dep'=4] {'dep','lat'}, dimensions={0} | all-to-all | bytes 131072 | tf_op jit(solution)/shard_map/all_to_all | solution.py:511
  56.9 0.0 collective-permute-done.8.r1
  56.9 0.0 collective-permute-done.9.r2
  56.9 0.0 collective-permute-done.10.r3
  57.0 1.1 %unpack.1 = (f32[32,32,128]{2,1,0:T(8,128)}, f32[16]{0:T(128)}) custom-call(f32[8,32,128]{2,1,0:T(8,128)S(1)} %get-tuple-element.65.own, f32[8,32,128]{2,1,0:T(8,128)S(1)} %collective-permute-done.8.r1, f32[8,32,128]{2,1,0:T(8,128)S(1)} %collective-permute-done.9.r2, f32[8,32,128]{2,1,0:T(8,128)S(1)} %collective-permute-done.10.r3, ...), custom_call_target="tpu_custom_call" | custom-call | tf_op jit(solution)/shard_map/unpack/pallas_call | solution.py:437
  (1 shorter events, 0.0 us)
Async XLA Ops:
  1.9 9.2 %collective-permute-start = (f32[8,32,128]{2,1,0:T(8,128)S(1)}, f32[8,32,128]{2,1,0:T(8,128)S(1)}, u32[]{:S(2)}, u32[]{:S(2)}) collective-permute-start(f32[8,32,128]{2,1,0:T(8,128)S(1)} %get-tuple-element.39), channel_id=1, source_target_pairs={{0,1},{1,2},{2,3},{3,0},{4,5},{5,6},{6,7},{7,4},{8,9},{9,10},{10,1... | collective-permute-start | bytes 393224 | tf_op jit(solution)/shard_map/ppermute | solution.py:415
  4.0 7.2 %collective-permute-start.1 = (f32[8,32,128]{2,1,0:T(8,128)S(1)}, f32[8,32,128]{2,1,0:T(8,128)S(1)}, u32[]{:S(2)}, u32[]{:S(2)}) collective-permute-start(f32[8,32,128]{2,1,0:T(8,128)S(1)} %get-tuple-element.40), channel_id=1, source_target_pairs={{0,3},{1,0},{2,1},{3,2},{4,7},{5,4},{6,5},{7,6},{8,11},{9,8},{10,9... | collective-permute-start | bytes 393224 | tf_op jit(solution)/shard_map/ppermute | solution.py:415
  5.4 7.0 %collective-permute-start.2 = (f32[8,32,128]{2,1,0:T(8,128)S(1)}, f32[8,32,128]{2,1,0:T(8,128)S(1)}, u32[]{:S(2)}, u32[]{:S(2)}) collective-permute-start(f32[8,32,128]{2,1,0:T(8,128)S(1)} %get-tuple-element.41), channel_id=1, source_target_pairs={{0,2},{1,3},{2,0},{3,1},{4,6},{5,7},{6,4},{7,5},{8,10},{9,11},{10,... | collective-permute-start | bytes 393224 | tf_op jit(solution)/shard_map/ppermute | solution.py:415
  8.4 8.0 %collective-permute-start.3 = (f32[8,32,128]{2,1,0:T(8,128)S(1)}, f32[8,32,128]{2,1,0:T(8,128)S(1)}, u32[]{:S(2)}, u32[]{:S(2)}) collective-permute-start(f32[8,32,128]{2,1,0:T(8,128)S(1)} %get-tuple-element.50), channel_id=1, source_target_pairs={{0,1},{1,2},{2,3},{3,0},{4,5},{5,6},{6,7},{7,4},{8,9},{9,10},{10,1... | collective-permute-start | bytes 393224 | tf_op jit(solution)/shard_map/ppermute | solution.py:415
  8.7 7.6 %collective-permute-start.4 = (f32[8,32,128]{2,1,0:T(8,128)S(1)}, f32[8,32,128]{2,1,0:T(8,128)S(1)}, u32[]{:S(2)}, u32[]{:S(2)}) collective-permute-start(f32[8,32,128]{2,1,0:T(8,128)S(1)} %get-tuple-element.51), channel_id=1, source_target_pairs={{0,3},{1,0},{2,1},{3,2},{4,7},{5,4},{6,5},{7,6},{8,11},{9,8},{10,9... | collective-permute-start | bytes 393224 | tf_op jit(solution)/shard_map/ppermute | solution.py:415
  11.1 6.2 %collective-permute-start.5 = (f32[8,32,128]{2,1,0:T(8,128)S(1)}, f32[8,32,128]{2,1,0:T(8,128)S(1)}, u32[]{:S(2)}, u32[]{:S(2)}) collective-permute-start(f32[8,32,128]{2,1,0:T(8,128)S(1)} %get-tuple-element.52), channel_id=1, source_target_pairs={{0,2},{1,3},{2,0},{3,1},{4,6},{5,7},{6,4},{7,5},{8,10},{9,11},{10,... | collective-permute-start | bytes 393224 | tf_op jit(solution)/shard_map/ppermute | solution.py:415
  17.5 11.1 %collective-permute-start.6 = (f32[52,8,128]{2,1,0:T(8,128)S(1)}, f32[52,8,128]{2,1,0:T(8,128)S(1)}, u32[]{:S(2)}, u32[]{:S(2)}) collective-permute-start(f32[52,8,128]{2,1,0:T(8,128)S(1)} %get-tuple-element.54), channel_id=1, source_target_pairs={{0,1},{1,0},{2,3},{3,2},{7,6},{6,7},{5,4},{4,5},{8,9},{9,8},{10,11... | collective-permute-start | bytes 638984 | tf_op jit(solution)/shard_map/ppermute | solution.py:463
  19.0 9.6 %collective-permute-start.7 = (f32[52,8,128]{2,1,0:T(8,128)S(1)}, f32[52,8,128]{2,1,0:T(8,128)S(1)}, u32[]{:S(2)}, u32[]{:S(2)}) collective-permute-start(f32[52,8,128]{2,1,0:T(8,128)S(1)} %get-tuple-element.55), channel_id=1, source_target_pairs={{1,2},{2,1},{3,7},{7,3},{6,5},{5,6},{4,8},{8,4},{9,10},{10,9},{11,... | collective-permute-start | bytes 638984 | tf_op jit(solution)/shard_map/ppermute | solution.py:463
  35.0 22.0 %collective-permute-start.8 = (f32[8,32,128]{2,1,0:T(8,128)S(1)}, f32[8,32,128]{2,1,0:T(8,128)S(1)}, u32[]{:S(2)}, u32[]{:S(2)}) collective-permute-start(f32[8,32,128]{2,1,0:T(8,128)S(1)} %get-tuple-element.66), channel_id=1, source_target_pairs={{0,1},{1,2},{2,3},{3,0},{4,5},{5,6},{6,7},{7,4},{8,9},{9,10},{10,1... | collective-permute-start | bytes 393224 | tf_op jit(solution)/shard_map/ppermute | solution.py:415
  35.1 21.9 %collective-permute-start.9 = (f32[8,32,128]{2,1,0:T(8,128)S(1)}, f32[8,32,128]{2,1,0:T(8,128)S(1)}, u32[]{:S(2)}, u32[]{:S(2)}) collective-permute-start(f32[8,32,128]{2,1,0:T(8,128)S(1)} %get-tuple-element.67), channel_id=1, source_target_pairs={{0,2},{1,3},{2,0},{3,1},{4,6},{5,7},{6,4},{7,5},{8,10},{9,11},{10,... | collective-permute-start | bytes 393224 | tf_op jit(solution)/shard_map/ppermute | solution.py:415
  35.6 21.4 %collective-permute-start.10 = (f32[8,32,128]{2,1,0:T(8,128)S(1)}, f32[8,32,128]{2,1,0:T(8,128)S(1)}, u32[]{:S(2)}, u32[]{:S(2)}) collective-permute-start(f32[8,32,128]{2,1,0:T(8,128)S(1)} %get-tuple-element.68), channel_id=1, source_target_pairs={{0,3},{1,0},{2,1},{3,2},{4,7},{5,4},{6,5},{7,6},{8,11},{9,8},{10,9... | collective-permute-start | bytes 393224 | tf_op jit(solution)/shard_map/ppermute | solution.py:415
